TPU v7x, 128 devices: a whole 4x4x4 slice. The times are simulated.
128 devices in a mesh: dp: 16 (over x, y), tensor: 8 (over z, core).
Axes of the slice: x: 4, y: 4, z: 4, core: 2. Of those that a mesh axis runs over, the one named last changes fastest.
Arguments:
- gate_pre: bfloat16 [8192, 14336], P('dp', 'tensor'), may hold values from -6 to 6
- up_pre: bfloat16 [8192, 14336], P('dp', 'tensor'), may hold values from -6 to 6
- down_weight: bfloat16 [14336, 4096], P('tensor', 'dp'), as said below
- grad_out: bfloat16 [8192, 4096], P('dp', 'tensor'), may hold values from -6 to 6
- weight_history: float32 [16], replicated
- act_history: float32 [16], replicated
Outputs:
- mixed: bfloat16 [8192, 4096], P('dp', 'tensor')
- grad_gate: bfloat16 [8192, 14336], P('dp', 'tensor')
- grad_up: bfloat16 [8192, 14336], P('dp', 'tensor')
- weight_grad: bfloat16 [14336, 4096], P('tensor', 'dp')
- new_weight_history: float32 [16], replicated
- new_act_history: float32 [16], replicated
Inputs may be any that keep to these rules, and one draw needn't show every extreme that they name: Entries of down_weight lie within 24 / sqrt(14336) in magnitude.
All inputs are finite; a program needn't handle non-finite values.
Results may differ from a plain program's by a relative error of at most 0.019.
Values may be sent and summed in bfloat16 or wider, within the bound.
No kernel may reach another device: no remote copies, remote signals or barrier semaphores. Data moves between devices by JAX's collectives and lax.ppermute only.
A program may use at most 192 MiB of HBM per device.

v0:
```python
import jax
import jax.numpy as jnp
from jax import lax
from jax.sharding import PartitionSpec as P


def on_device(gate_pre, up_pre, down_weight, grad_out, weight_history, act_history):
    gate = gate_pre.astype(jnp.float32)
    up = up_pre.astype(jnp.float32)
    sigm = jax.nn.sigmoid(gate)
    silu_gate = gate * sigm
    act = silu_gate * up
    act_limit = jnp.max(act_history)
    act_q = jnp.clip(act, -act_limit, act_limit).astype(jnp.bfloat16)
    weight_limit = jnp.max(weight_history)
    weight_local = down_weight.astype(jnp.float32)
    weight_q = jnp.clip(weight_local, -weight_limit, weight_limit).astype(jnp.bfloat16)
    weight_local_peak = jnp.max(jnp.abs(weight_local))
    act_local_peak = jnp.max(jnp.abs(act))
    weight_peak = lax.pmax(weight_local_peak, ("dp", "tensor"))
    act_peak = lax.pmax(act_local_peak, ("dp", "tensor"))
    piece = lax.all_gather(weight_q, "dp", axis=1, tiled=True)
    partial_out = jnp.dot(act_q, piece, preferred_element_type=jnp.float32)
    mixed = lax.psum_scatter(
        partial_out.astype(jnp.bfloat16), "tensor", scatter_dimension=1, tiled=True
    )
    grad_whole = lax.all_gather(grad_out, "tensor", axis=1, tiled=True)
    grad_act = lax.dot_general(
        grad_whole, piece, (((1,), (1,)), ((), ())), preferred_element_type=jnp.float32
    )
    grad_gate = (grad_act * up * sigm * (1.0 + gate * (1.0 - sigm))).astype(jnp.bfloat16)
    grad_up = (grad_act * silu_gate).astype(jnp.bfloat16)
    terms = lax.dot_general(
        act_q, grad_whole, (((0,), (0,)), ((), ())), preferred_element_type=jnp.float32
    )
    terms = terms.astype(jnp.bfloat16)
    weight_grad = (
        lax.psum_scatter(terms, "dp", scatter_dimension=1, tiled=True)
        .astype(jnp.float32)
        .astype(jnp.bfloat16)
    )
    new_weight_history = jnp.concatenate([weight_peak[None], weight_history[:-1]])
    new_act_history = jnp.concatenate([act_peak[None], act_history[:-1]])
    return (mixed, grad_gate, grad_up, weight_grad, new_weight_history, new_act_history)


def solution(mesh):
    in_specs = (
        P("dp", "tensor"),
        P("dp", "tensor"),
        P("tensor", "dp"),
        P("dp", "tensor"),
        P(),
        P(),
    )
    out_specs = (
        P("dp", "tensor"),
        P("dp", "tensor"),
        P("dp", "tensor"),
        P("tensor", "dp"),
        P(),
        P(),
    )
    return jax.shard_map(
        on_device, mesh=mesh, in_specs=in_specs, out_specs=out_specs, check_vma=False
    )
```

profile of v0, /device:TPU:15, one launch (start us, length us, event | category | flops | bytes accessed | tf_op | source)
XLA Modules:
  0.0 308.4 jit_solution(12584594269641483449)
XLA Ops:
  7.2 0.0 all-gather.3.cloned.1.call-start
  7.2 1.4 reduce_max.37
  9.3 3.0 fusion.9
  12.3 0.0 all-gather.3.cloned.1.call-update
  12.3 0.0 all-gather.5.cloned.1.call-start
  12.3 0.7 all-gather.5.cloned.1.call-update
  13.0 0.0 reduce-scatter.3.cloned.1.call-start
  13.1 2.3 copy.13
  15.4 0.6 reduce_max.36
  16.7 3.8 %copy.12 = bf16[512,1792]{0,1:T(8,128)(2,1)} copy(bf16[512,1792]{1,0:T(8,128)(2,1)} %param.6) | data formatting | bytes 3670016 | tf_op args[0]
  20.5 102.0 %all-gather.3.cloned.1.call-done = bf16[1792,4096]{1,0:T(8,128)(2,1)} async-done(((bf16[1792,256]{1,0:T(8,128)(2,1)}), bf16[1792,4096]{1,0:T(8,128)(2,1)}) %all-gather.3.cloned.1.call-update) | async-done | bytes 14680080 | tf_op jit(solution)/shard_map/all_gather | solution.py:22
  122.5 15.1 %convolution_convert_fusion.1 = bf16[512,4096]{1,0:T(8,128)(2,1)} fusion(bf16[1792,4096]{1,0:T(8,128)(2,1)} %all-gather.3.cloned.1.call-done, bf16[512,1792]{0,1:T(8,128)(2,1)S(1)} %copy-done.2, bf16[]{:T(256)S(6)} %neg.9, f32[]{:T(128)} %reduce_max.36, bf16[512,1792]{0,1:T(8,128)(2,1)} %copy.12), kind=kOutput, calls=%fused_computation.1 | convolution fusion | flops 7529299968 | bytes 22544390 | tf_op jit(solution)/shard_map/dot_general | solution.py:23
  137.6 0.2 reduce-scatter.5.cloned.1.call-start
  137.8 20.9 %all-gather.5.cloned.1.call-done = bf16[512,4096]{1,0:T(8,128)(2,1)} async-done(((bf16[512,512]{1,0:T(8,128)(2,1)}), bf16[512,4096]{1,0:T(8,128)(2,1)}) %all-gather.5.cloned.1.call-update) | async-done | bytes 4194320 | tf_op jit(solution)/shard_map/all_gather | solution.py:27
  158.8 14.7 %convolution_convert_fusion = bf16[1792,4096]{1,0:T(8,128)(2,1)} fusion(bf16[512,4096]{1,0:T(8,128)(2,1)} %all-gather.5.cloned.1.call-done, bf16[512,1792]{0,1:T(8,128)(2,1)S(1)} %copy-done.2, bf16[]{:T(256)S(6)} %neg.9, f32[]{:T(128)} %reduce_max.36, bf16[512,1792]{0,1:T(8,128)(2,1)} %copy.12), kind=kOutput, calls=%fused_computation | convolution fusion | flops 7534542848 | bytes 22544390 | tf_op jit(solution)/shard_map/dot_general | solution.py:33
  173.5 0.0 reduce-scatter.5.cloned.1.call-update
  173.5 1.2 copy-done
  174.7 0.7 fusion.10
  175.4 16.2 %fusion.7 = (bf16[512,1792]{0,1:T(8,128)(2,1)}, bf16[512,1792]{0,1:T(8,128)(2,1)}, f32[]{:T(128)}) fusion(bf16[512,1792]{0,1:T(8,128)(2,1)} %copy.12, bf16[512,1792]{0,1:T(8,128)(2,1)S(1)} %copy-done.2, bf16[1792,4096]{1,0:T(8,128)(2,1)} %all-gather.3.cloned.1.call-done, bf16[512,4096]{1,0:T(8,128)(2,1)} %all-gather.5.cloned.1.call-done), kind=kOutput, calls=%fused_computation.15 | convolution fusion | flops 7532707840 | bytes 26214404 | tf_op jit(solution)/shard_map/dot_general | solution.py:28
  191.6 64.4 %all-reduce = (f32[1]{0:T(128)}, f32[1]{0:T(128)}) all-reduce(f32[1]{0:T(128)} %bitcast.1, f32[1]{0:T(128)} %bitcast.2), channel_id=1, replica_groups=mesh['dp'=16,'tensor'=8] {'dp','tensor'}, use_global_device_ids=true, to_apply=%region_5.6 | all-reduce | flops 2 | bytes 16 | tf_op jit(solution)/shard_map/pmax | solution.py:20
  256.0 3.9 %copy.14 = bf16[512,1792]{1,0:T(8,128)(2,1)} copy(bf16[512,1792]{0,1:T(8,128)(2,1)} %get-tuple-element.15) | data formatting | bytes 3670016
  259.9 2.4 copy.15
  262.3 1.9 pad_maximum_fusion
  264.2 37.7 %reduce-scatter.5.cloned.1.call-done = bf16[1792,256]{1,0:T(8,128)(2,1)} async-done(((bf16[1792,4096]{1,0:T(8,128)(2,1)}), bf16[1792,256]{1,0:T(8,128)(2,1)}) %reduce-scatter.5.cloned.1.call-update) | async-done | bytes 917520 | tf_op jit(solution)/shard_map/reduce_scatter | solution.py:38
  (13 shorter events, 0.0 us)
Async XLA Ops:
  7.2 5.9 %copy-start.1 = (bf16[512,1792]{1,0:T(8,128)(2,1)S(1)}, bf16[512,1792]{1,0:T(8,128)(2,1)}, u32[]{:S(2)}) copy-start(bf16[512,1792]{1,0:T(8,128)(2,1)} %param.7) | copy-start | bytes 5505028
  7.2 8.2 %copy-start.5 = (f32[16]{0:T(128)S(1)}, f32[16]{0:T(128)}, u32[]{:S(2)}) copy-start(f32[16]{0:T(128)} %param.11) | copy-start | bytes 196
  7.2 115.3 %all-gather.3.cloned.1.call-start = ((), (), s32[]{:S(2)}) async-start(), calls=%async_computation.2 | async-start | bytes 15597568 | tf_op jit(solution)/shard_map/all_gather | solution.py:22
  12.3 146.5 %all-gather.5.cloned.1.call-start = ((), (), s32[]{:S(2)}) async-start(), calls=%async_computation.4 | async-start | bytes 4718592 | tf_op jit(solution)/shard_map/all_gather | solution.py:27
  13.0 251.2 %reduce-scatter.3.cloned.1.call-start = ((), (), s32[]{:S(2)}) async-start(), calls=%async_computation.3 | async-start | bytes 4718592 | tf_op jit(solution)/shard_map/reduce_scatter | solution.py:24
  15.4 107.1 %copy-start.2 = (bf16[512,1792]{0,1:T(8,128)(2,1)S(1)}, bf16[512,1792]{0,1:T(8,128)(2,1)}, u32[]{:S(2)}) copy-start(bf16[512,1792]{0,1:T(8,128)(2,1)} %copy.13) | copy-start | bytes 5505028
  137.6 164.3 %reduce-scatter.5.cloned.1.call-start = ((), (), s32[]{:S(2)}) async-start(), calls=%async_computation.5 | async-start | bytes 15597568 | tf_op jit(solution)/shard_map/reduce_scatter | solution.py:38
  173.5 1.2 copy-start
  191.6 68.3 %copy-start.3 = (bf16[512,1792]{0,1:T(8,128)(2,1)S(1)}, bf16[512,1792]{0,1:T(8,128)(2,1)}, u32[]{:S(2)}) copy-start(bf16[512,1792]{0,1:T(8,128)(2,1)} %get-tuple-element.14) | copy-start | bytes 5505028
  256.0 6.3 %copy-start.4 = (f32[16]{0:T(128)S(1)}, f32[16]{0:T(128)}, u32[]{:S(2)}) copy-start(f32[16]{0:T(128)} %param.10) | copy-start | bytes 196
Sparse Core Ops, SparseCore 0:
  12.4 110.0 all-gather.2
  124.2 34.5 all-gather.4
  161.7 34.4 reduce-scatter.2
  200.1 101.7 reduce-scatter.4
where the time goes:
time: 312 us; the launch traced here: 308 us
  waiting for transfers between devices  161 us (52%)
  blocking collectives  64.4 us (21%)
  matrix products  46 us (15%)
  between operations  15.1 us (5%)
  local copies, waits for them, and re-layouts  13.6 us (4%)
  other arithmetic  7.56 us (2%)
    all_gather x1, waiting for transfers between devices, on_device(): piece = lax.all_gather(weight_q, 'dp', axis=1, tiled=True)  102 us
    pmax x1, blocking collectives, on_device(): weight_peak = lax.pmax(weight_local_peak, ('dp', 'tensor'))  64.4 us
    reduce_scatter x1, waiting for transfers between devices, on_device(): lax.psum_scatter(terms, 'dp', scatter_dimension=1, tiled=True)  37.7 us
    all_gather x1, waiting for transfers between devices, on_device(): grad_whole = lax.all_gather(grad_out, 'tensor', axis=1, tiled=True)  20.9 us
    dot_general x1, matrix products, on_device(): lax.dot_general(grad_whole, piece, (((1,), (1,)), ((), ())), preferred_el...  16.2 us
    dot_general x1, matrix products, on_device(): partial_out = jnp.dot(act_q, piece, preferred_element_type=jnp.float32)  15.1 us
    dot_general x1, matrix products, on_device(): lax.dot_general(act_q, grad_whole, (((0,), (0,)), ((), ())), preferred_el...  14.7 us
    unnamed x16, local copies, waits for them, and re-layouts  13.6 us
  transfers between devices with their start and end apart: 4, of which 3 were waited for; matrix products, arithmetic and copies ran while one was open for 20% of the time, Pallas kernels for 0%

commit v1 on v0

v1 whole, which is shorter than its diff:
```python
import functools

import jax
import jax.numpy as jnp
import numpy as np
from jax import lax
from jax.experimental import pallas as pl
from jax.experimental.pallas import tpu as pltpu
from jax.sharding import Mesh, PartitionSpec as P

AXES = ("x", "y", "z", "c")
N = 4
BF16 = jnp.bfloat16
F32 = jnp.float32
VMEM_BYTES = 24 * 1024 * 1024
ANYWHERE = pl.BlockSpec(memory_space=pl.ANY)
SCALARS = pl.BlockSpec(memory_space=pltpu.SMEM)
IN_VMEM = pl.BlockSpec(memory_space=pltpu.VMEM)
IN_HBM = pl.BlockSpec(memory_space=pltpu.HBM)
NOTE = 16


def flat(x, y, z, c):
    return ((x % N * N + y % N) * N + z % N) * 2 + c


def places():
    return [(x, y, z, c) for x in range(N) for y in range(N) for z in range(N) for c in range(2)]


def token_ring(step):
    return [
        (flat(x, y, z, c), flat(x, y + step, z, c) if c == 0 else flat(x + step, y, z, c))
        for x, y, z, c in places()
    ]


def feature_ring(step):
    return [
        (flat(x, y, z, c), flat(x + step, y, z, c) if c == 0 else flat(x, y + step, z, c))
        for x, y, z, c in places()
    ]


def hidden_ring(step):
    return [(flat(x, y, z, c), flat(x, y, z + step, c)) for x, y, z, c in places()]


def token_groups():
    first = [[flat(x, y, z, 0) for y in range(N)] for x in range(N) for z in range(N)]
    second = [[flat(x, y, z, 1) for x in range(N)] for y in range(N) for z in range(N)]
    return first + second


def tile_edges():
    edges = []
    for x, y, z, c in places():
        for half in range(2):
            block = 2 * c + half
            edges.append((flat(x, y, z, c), flat(x, block, z, 0), half, y))
            edges.append((flat(x, y, z, c), flat(z, y, block, 1), half, x))
    return edges


def rounds():
    rest = tile_edges()
    out = []
    for _ in range(4):
        outgoing = {}
        for edge in rest:
            outgoing.setdefault(edge[0], []).append(edge)
        chosen = {}

        def augment(owner, seen):
            for edge in outgoing[owner]:
                if edge[1] in seen:
                    continue
                seen.add(edge[1])
                if edge[1] not in chosen or augment(chosen[edge[1]][0], seen):
                    chosen[edge[1]] = edge
                    return True
            return False

        for owner in range(128):
            augment(owner, set())
        picked = sorted(chosen.values())
        out.append(picked)
        rest = [edge for edge in rest if edge not in picked]
    return out


ROUNDS = rounds()
TABLE = np.zeros((8, 128), np.int32)
for number, picked in enumerate(ROUNDS):
    for owner, user, half, slot in picked:
        TABLE[number, owner] = half
        TABLE[4 + number, user] = slot


def send(value, pairs):
    return lax.ppermute(value, AXES, pairs)


def here():
    x, y, z, c = (lax.axis_index(name) for name in AXES)
    return flat(x, y, z, c), jnp.where(c == 0, x, y), z


def call(kernel, out_shape, cost, in_specs, operands, after=(), stored=(), vmem=VMEM_BYTES, **options):
    flops, moved = cost
    count = len(operands)
    extra = len(after) + len(stored)

    def body(*refs):
        kernel(*refs[:count], *refs[count + extra :])

    return pl.pallas_call(
        body,
        out_shape=out_shape,
        in_specs=list(in_specs) + [ANYWHERE] * len(after) + [IN_HBM] * len(stored),
        compiler_params=pltpu.CompilerParams(vmem_limit_bytes=vmem),
        cost_estimate=pl.CostEstimate(flops=flops, bytes_accessed=moved, transcendentals=0),
        **options,
    )(*operands, *after, *stored)


def shape(*dims, dtype=BF16):
    return jax.ShapeDtypeStruct(dims, dtype)


def ring_gather(own, ring):
    far = send(own, ring(2))
    return own, send(own, ring(-1)), far, send(own, ring(1))


def ring_exchange(parts, ring):
    far = send(parts[2], ring(2))
    return parts[0], send(parts[1], ring(1)), far, send(parts[3], ring(-1))


def peak_of(values):
    return jnp.max(jnp.abs(values), axis=0, keepdims=True)


def keep_peak(step, top, peak):
    @pl.when(step == 0)
    def _():
        top[...] = peak

    @pl.when(step > 0)
    def _():
        top[...] = jnp.maximum(top[...], peak)


def row_blocks(array, steps):
    return pl.BlockSpec((array.shape[0] // steps, array.shape[1]), lambda i: (i, 0))


def fixed(*dims):
    return pl.BlockSpec(dims, lambda i: (0, 0))


def note_of(peaks, width):
    row = lax.broadcasted_iota(jnp.int32, (NOTE, width), 0)
    note = jnp.zeros((NOTE, width), F32)
    for number in range(2):
        rest = jnp.broadcast_to(peaks[number : number + 1, :1], (NOTE, width))
        for piece in range(3):
            value = rest.astype(BF16).astype(F32)
            note = jnp.where(row == 3 * number + piece, value, note)
            rest = rest - value
    return note.astype(BF16)


def peaks_in(notes):
    best = []
    for number in range(2):
        values = []
        for note in notes:
            note = note[...].astype(F32)
            pieces = [note[3 * number + piece : 3 * number + piece + 1, :128] for piece in range(3)]
            values.append(pieces[0] + pieces[1] + pieces[2])
        best.append(functools.reduce(jnp.maximum, values))
    row = lax.broadcasted_iota(jnp.int32, (8, 128), 0)
    return jnp.where(row == 0, jnp.broadcast_to(best[0], (8, 128)), jnp.broadcast_to(best[1], (8, 128)))


def note_block(array):
    last = array.shape[0] // NOTE - 1
    return pl.BlockSpec((NOTE, array.shape[1]), lambda *i: (last, 0))


def share_kernel(table, grad, peaks, others, out0, out1, out2, out3):
    me, _, _ = here()
    tokens, width = grad.shape[0], grad.shape[1] // 2
    note = note_of(jnp.maximum(peaks[...], others[...]), width)
    for number, out in enumerate((out0, out1, out2, out3)):
        half = table[number, me]

        @pl.when(half == 0)
        def _():
            out[:tokens, :] = grad[:, :width]

        @pl.when(half == 1)
        def _():
            out[:tokens, :] = grad[:, width:]

        out[tokens:, :] = note


def share(grad, peaks, others):
    block = shape(grad.shape[0] + NOTE, grad.shape[1] // 2)
    return call(
        share_kernel,
        (block, block, block, block),
        (0, 0),
        [SCALARS] + [IN_VMEM] * 3,
        (jnp.asarray(TABLE), grad, peaks, others),
        out_specs=[IN_VMEM] * 4,
    )


def activate_kernel(gate, up, weight, act_history, weight_history,
                    act_q, weight_q, peaks, act_top, weight_top):
    step = pl.program_id(0)
    gate_v = gate[...].astype(F32)
    act = gate_v * jax.nn.sigmoid(gate_v) * up[...].astype(F32)
    limit = jnp.max(act_history[...], axis=1, keepdims=True)
    act_q[...] = jnp.clip(act, -limit, limit).astype(BF16)
    weight_v = weight[...].astype(F32)
    limit = jnp.max(weight_history[...], axis=1, keepdims=True)
    weight_q[...] = jnp.clip(weight_v, -limit, limit).astype(BF16)
    keep_peak(step, act_top, peak_of(act))
    keep_peak(step, weight_top, peak_of(weight_v))

    @pl.when(step == pl.num_programs(0) - 1)
    def _():
        row = lax.broadcasted_iota(jnp.int32, peaks.shape, 0)
        top = jnp.max(act_top[...], axis=1, keepdims=True)
        other = jnp.max(weight_top[...], axis=1, keepdims=True)
        peaks[...] = jnp.where(
            row == 0, jnp.broadcast_to(top, peaks.shape), jnp.broadcast_to(other, peaks.shape)
        )


def activate(gate, up, weight, act_history, weight_history):
    steps = 8
    rows, weight_rows = row_blocks(gate, steps), row_blocks(weight, steps)
    return call(
        activate_kernel,
        (shape(*gate.shape), shape(*weight.shape), shape(8, 128, dtype=F32)),
        (0, 0),
        [rows, rows, weight_rows, fixed(1, act_history.shape[1]), fixed(1, act_history.shape[1])],
        (gate, up, weight, act_history, weight_history),
        grid=(steps,),
        out_specs=[rows, weight_rows, fixed(8, 128)],
        scratch_shapes=[pltpu.VMEM((1, gate.shape[1]), F32), pltpu.VMEM((1, weight.shape[1]), F32)],
    )


def slopes_kernel(gate, up, slope, silu, token):
    gate_v = gate[...].astype(F32)
    sigm = jax.nn.sigmoid(gate_v)
    slope[...] = (up[...].astype(F32) * sigm * (1.0 + gate_v * (1.0 - sigm))).astype(BF16)
    silu[...] = (gate_v * sigm).astype(BF16)
    token[...] = jnp.zeros(token.shape, F32)


def slopes(gate, up, after):
    steps = 8
    rows = row_blocks(gate, steps)
    return call(
        slopes_kernel,
        (shape(*gate.shape), shape(*gate.shape), shape(8, 128, dtype=F32)),
        (0, 0),
        [rows, rows],
        (gate, up),
        after,
        grid=(steps,),
        out_specs=[rows, rows, fixed(8, 128)],
    )


def place_kernel(table, in0, in1, in2, in3, out):
    me, _, _ = here()
    rows = in0.shape[0] - NOTE
    for number, block in enumerate((in0, in1, in2, in3)):
        start = pl.multiple_of(table[4 + number, me] * rows, rows)
        out[pl.ds(start, rows), :] = block[:rows, :]
    peaks = peaks_in([block[rows:, :] for block in (in0, in1, in2, in3)])
    out[4 * rows :, :] = note_of(peaks, out.shape[1])


def place(blocks):
    rows, features = blocks[0].shape
    return call(
        place_kernel,
        shape(4 * (rows - NOTE) + NOTE, features),
        (0, 0),
        [SCALARS] + [IN_VMEM] * 4,
        (jnp.asarray(TABLE), *blocks),
        out_specs=IN_VMEM,
    )


def gate_kernel(*refs):
    pass


def gate(values, after=(), stored=()):
    count = len(values)
    return call(
        gate_kernel,
        tuple(shape(*value.shape) for value in values),
        (0, 0),
        [ANYWHERE] * count,
        values,
        after,
        stored,
        vmem=1024 * 1024,
        out_specs=[ANYWHERE] * count,
        input_output_aliases={number: number for number in range(count)},
    )


def columns_kernel(place, own, after, far, before, out):
    width = own.shape[1]
    for step, block in enumerate((own, after, far, before)):
        column = pl.multiple_of(lax.rem(place + step, N) * width, width)
        out[:, pl.ds(column, width)] = block[...]


def weight_tile_kernel(*refs):
    columns_kernel(here()[1], *refs)


def weight_tile(parts, after):
    steps = 4
    out = shape(parts[0].shape[0], N * parts[0].shape[1])
    return call(
        weight_tile_kernel,
        out,
        (0, 0),
        [row_blocks(parts[0], steps)] * N,
        parts,
        after,
        grid=(steps,),
        out_specs=row_blocks(out, steps),
    )


def grad_tile_kernel(own, after, far, before, note0, note1, note2, note3, out, peaks):
    columns_kernel(here()[2], own, after, far, before, out)
    peaks[...] = peaks_in((note0, note1, note2, note3))


def grad_tile(parts):
    steps = 4
    rows, features = parts[0].shape[0] - NOTE, parts[0].shape[1]
    out = shape(rows, N * features)
    block = pl.BlockSpec((rows // steps, features), lambda i: (i, 0))
    return call(
        grad_tile_kernel,
        (out, shape(8, 128, dtype=F32)),
        (0, 0),
        [block] * N + [note_block(part) for part in parts],
        (*parts, *parts),
        grid=(steps,),
        out_specs=[row_blocks(out, steps), fixed(8, 128)],
    )


def later_kernel(value, out):
    out[...] = value[...]


def later(value, after):
    return call(
        later_kernel,
        shape(*value.shape, dtype=value.dtype),
        (0, 0),
        [IN_VMEM],
        (value,),
        after,
        out_specs=IN_VMEM,
    )


def histories_kernel(peaks, others, old_weight, old_act, new_weight, new_act):
    for row, old, new in ((1, old_weight, new_weight), (0, old_act, new_act)):
        new[:, 1:] = old[:, :-1]
        new[:, :1] = jnp.maximum(peaks[row : row + 1, :1], others[row : row + 1, :1])


def histories(peaks, others, old_weight, old_act):
    new = shape(*old_weight.shape, dtype=F32)
    return call(
        histories_kernel,
        (new, new),
        (0, 0),
        [IN_VMEM] * 4,
        (peaks, others, old_weight, old_act),
        out_specs=[IN_VMEM] * 2,
    )


def return_kernel(table, part0, part1, part2, part3, out0, out1, out2, out3):
    me, _, _ = here()
    tokens = out0.shape[0]
    for number, out in enumerate((out0, out1, out2, out3)):
        rows = pl.ds(pl.multiple_of(table[4 + number, me] * tokens, tokens), tokens)
        total = part0[rows, :].astype(F32) + part1[rows, :].astype(F32)
        total = total + (part2[rows, :].astype(F32) + part3[rows, :].astype(F32))
        out[...] = total.astype(BF16)


def return_blocks(parts, after):
    rows, features = parts[0].shape
    return call(
        return_kernel,
        (shape(rows // N, features),) * 4,
        (0, 0),
        [SCALARS] + [IN_VMEM] * 4,
        (jnp.asarray(TABLE), *parts),
        after,
        out_specs=[IN_VMEM] * 4,
    )


def add_kernel(part0, part1, part2, part3, out, token):
    total = part0[...].astype(F32) + part1[...].astype(F32)
    out[...] = (total + (part2[...].astype(F32) + part3[...].astype(F32))).astype(BF16)
    token[...] = jnp.zeros(token.shape, F32)


def add(parts):
    steps = 4
    rows = row_blocks(parts[0], steps)
    return call(
        add_kernel,
        (shape(*parts[0].shape), shape(8, 128, dtype=F32)),
        (0, 0),
        [rows] * 4,
        parts,
        grid=(steps,),
        out_specs=[rows, fixed(8, 128)],
    )


def merge_kernel(table, in0, in1, in2, in3, out):
    me, _, _ = here()
    width = in0.shape[1]
    for half in range(2):
        total = jnp.zeros(in0.shape, F32)
        for number, block in enumerate((in0, in1, in2, in3)):
            keep = (table[number, me] == half).astype(F32)
            total = total + block[...].astype(F32) * keep
        out[:, half * width : (half + 1) * width] = total.astype(BF16)


def merge(blocks):
    steps = 2
    out = shape(blocks[0].shape[0], 2 * blocks[0].shape[1])
    return call(
        merge_kernel,
        out,
        (0, 0),
        [SCALARS] + [row_blocks(blocks[0], steps)] * 4,
        (jnp.asarray(TABLE), *blocks),
        grid=(steps,),
        out_specs=row_blocks(out, steps),
    )


def finish_kernel(slope, silu, grad_act, grad_gate, grad_up):
    value = grad_act[...].astype(F32)
    grad_gate[...] = (value * slope[...].astype(F32)).astype(BF16)
    grad_up[...] = (value * silu[...].astype(F32)).astype(BF16)


def finish(slope, silu, grad_act):
    steps = 4
    rows = row_blocks(slope, steps)
    return call(
        finish_kernel,
        (shape(*slope.shape),) * 2,
        (0, 0),
        [rows] * 3,
        (slope, silu, grad_act),
        grid=(steps,),
        out_specs=[rows] * 2,
    )


def raise_peaks(peaks, bits):
    for bit in bits:
        peaks = jnp.maximum(peaks, send(peaks, [(n, n ^ (1 << bit)) for n in range(128)]))
    return peaks


def dot(left, right, dims):
    product = lax.dot_general(left, right, (dims, ((), ())), preferred_element_type=F32)
    return product.astype(BF16)


def on_device(gate_pre, up_pre, down_weight, grad_out, weight_history, act_history):
    features = down_weight.shape[1]
    _, feature_place, z = here()
    groups = token_groups()
    swap = [(n, n ^ 1) for n in range(128)]
    act_q, weight_q, peaks = activate(
        gate_pre, up_pre, down_weight, act_history[None], weight_history[None]
    )
    blocks = share(grad_out, peaks, send(peaks, swap))
    blocks = [
        send(block, [(edge[0], edge[1]) for edge in ROUNDS[number]])
        for number, block in enumerate(blocks)
    ]
    grad = place(blocks)
    act_q, weight_q = gate((act_q, weight_q), (grad,))
    act = lax.all_gather(act_q, AXES, axis=0, tiled=True, axis_index_groups=groups)
    weight_parts = ring_gather(weight_q, feature_ring)
    slope, silu, token = slopes(gate_pre, up_pre, (grad,))
    tile, peaks = grad_tile(ring_gather(grad, hidden_ring))
    weight = weight_tile(weight_parts, (token,))

    def block_of(array, number):
        return lax.dynamic_slice_in_dim(array, number % N * features, features, axis=1)

    grad_act = dot(tile, weight, ((1,), (1,)))
    grad_act = lax.psum_scatter(
        grad_act, AXES, scatter_dimension=0, tiled=True, axis_index_groups=groups
    )
    mixed = [dot(act, block_of(weight, z + step), ((1,), (0,))) for step in range(N)]
    act = gate((act,), mixed)[0]
    mixed = ring_exchange(mixed, hidden_ring)
    weight_grad = [
        dot(act, block_of(tile, feature_place + step), ((0,), (0,))) for step in range(N)
    ]
    weight_grad, token = add(ring_exchange(weight_grad, feature_ring))
    blocks = return_blocks(mixed, (token,))
    blocks = [
        send(block, [(edge[1], edge[0]) for edge in ROUNDS[number]])
        for number, block in enumerate(blocks)
    ]
    grad_gate, grad_up = finish(slope, silu, grad_act)
    peaks = raise_peaks(later(peaks, (token,)), (5, 6))
    new_weight, new_act = histories(
        peaks, send(peaks, swap), weight_history[None], act_history[None]
    )
    return (merge(blocks), grad_gate, grad_up, weight_grad, new_weight[0], new_act[0])


def solution(mesh):
    cube = Mesh(mesh.devices.reshape(N, N, N, 2), AXES)
    whole = P(("x", "y"), ("z", "c"))
    flipped = P(("z", "c"), ("x", "y"))
    return jax.shard_map(
        on_device,
        mesh=cube,
        in_specs=(whole, whole, flipped, whole, P(), P()),
        out_specs=(whole, whole, whole, flipped, P(), P()),
        check_vma=False,
    )
```

time: 312 us -> 227 us (0.73)
  waiting for transfers between devices: 161 us -> 83.4 us
  blocking collectives: 64.4 us -> 0 us
  starting transfers between devices: 0.34 us -> 50.8 us
  Pallas kernels: 0 us -> 17.4 us
  other arithmetic: 7.56 us -> 0.01 us
  matrix products: 46 us -> 38.6 us
  local copies, waits for them, and re-layouts: 13.6 us -> 19.8 us
    all_gather x2 -> x1, waiting for transfers between devices: 123 us -> 0.02 us  [on_device(): lax.all_gather(act_q, AXES, axis=0, tiled=True, axis_index_groups=groups)]
    ppermute x0 -> x24, waiting for transfers between devices: none -> 83.3 us  [send(): return lax.ppermute(value, AXES, pairs)]
    pmax x1 -> x0, blocking collectives: 64.4 us -> none  [on_device(): weight_peak = lax.pmax(weight_local_peak, ('dp', 'tensor'))]
    ppermute x0 -> x24, starting transfers between devices: none -> 50.8 us  [send(): return lax.ppermute(value, AXES, pairs)]
    reduce_scatter x2 -> x1, waiting for transfers between devices: 37.7 us -> 0.01 us  [on_device(): lax.psum_scatter(grad_act, AXES, scatter_dimension=0, tiled=True, axis_in...]
    pallas_call x0 -> x14, Pallas kernels: none -> 17.4 us  [call(): pl.pallas_call(body, out_shape=out_shape, in_specs=list(in_specs) + [ANYW...]
    dot_general x3 -> x9, matrix products: 46 us -> 38.6 us  [dot(): lax.dot_general(left, right, (dims, ((), ())), preferred_element_type=F32)]
    unnamed x16 -> x54, local copies, waits for them, and re-layouts: 13.6 us -> 19.8 us
  transfers between devices with their start and end apart: 4 -> 26, of which waited for: 3 -> 11; matrix products, arithmetic and copies ran while one was open for 20% -> 17% of each run, Pallas kernels for 0% -> 5%
where the time goes in v1:
time: 227 us; the launch traced here: 225 us
  waiting for transfers between devices  83.4 us (37%)
  starting transfers between devices  50.8 us (22%)
  matrix products  38.6 us (17%)
  local copies, waits for them, and re-layouts  19.8 us (9%)
  Pallas kernels  17.4 us (8%)
  between operations  14.5 us (6%)
    ppermute x24, waiting for transfers between devices, send(): return lax.ppermute(value, AXES, pairs)  83.3 us
    ppermute x24, starting transfers between devices, send(): return lax.ppermute(value, AXES, pairs)  50.8 us
    dot_general x9, matrix products, dot(): lax.dot_general(left, right, (dims, ((), ())), preferred_element_type=F32)  38.6 us
    unnamed x54, local copies, waits for them, and re-layouts  19.8 us
    pallas_call x14, Pallas kernels, call(): pl.pallas_call(body, out_shape=out_shape, in_specs=list(in_specs) + [ANYW...  17.4 us
  transfers between devices with their start and end apart: 26, of which 11 were waited for; matrix products, arithmetic and copies ran while one was open for 17% of the time, Pallas kernels for 5%

profile of v1, /device:TPU:15, one launch (start us, length us, event | category | flops | bytes accessed | tf_op | source)
XLA Modules:
  0.0 224.5 jit_solution(3057866817827852883)
XLA Ops:
  17.2 4.1 %collective-permute-start.1 = (bf16[528,256]{1,0:T(8,128)(2,1)S(1)}, bf16[528,256]{1,0:T(8,128)(2,1)S(1)}, u32[]{:S(2)}, u32[]{:S(2)}) collective-permute-start(bf16[528,256]{1,0:T(8,128)(2,1)S(1)} %get-tuple-element.33), channel_id=1, source_target_pairs={{0,8},{1,24},{2,10},{3,26},{4,12},{5,28},{6,14},{7,30},{8,11},{9,1... | collective-permute-start | bytes 811016 | tf_op jit(solution)/shard_map/ppermute | solution.py:101
  23.3 7.0 %collective-permute-start.3 = (bf16[528,256]{1,0:T(8,128)(2,1)S(1)}, bf16[528,256]{1,0:T(8,128)(2,1)S(1)}, u32[]{:S(2)}, u32[]{:S(2)}) collective-permute-start(bf16[528,256]{1,0:T(8,128)(2,1)S(1)} %get-tuple-element.35), channel_id=1, source_target_pairs={{0,0},{1,16},{2,2},{3,18},{4,4},{5,20},{6,6},{7,22},{8,8},{9,24},{... | collective-permute-start | bytes 811016 | tf_op jit(solution)/shard_map/ppermute | solution.py:101
  33.1 16.7 %collective-permute-done.2.refs_2_ = bf16[528,256]{1,0:T(8,128)(2,1)S(1)} collective-permute-done((bf16[528,256]{1,0:T(8,128)(2,1)S(1)}, bf16[528,256]{1,0:T(8,128)(2,1)S(1)}, u32[]{:S(2)}, u32[]{:S(2)}) %collective-permute-start.2) | collective-permute-done | bytes 270368 | tf_op jit(solution)/shard_map/ppermute | solution.py:101
  55.5 4.6 %collective-permute-start.6 = (bf16[1792,256]{1,0:T(8,128)(2,1)}, bf16[1792,256]{1,0:T(8,128)(2,1)S(1)}, u32[]{:S(2)}, u32[]{:S(2)}) collective-permute-start(bf16[1792,256]{1,0:T(8,128)(2,1)} %copy-done.9), channel_id=1, source_target_pairs={{0,64},{1,17},{2,66},{3,19},{4,68},{5,21},{6,70},{7,23},{8,72},{9,... | collective-permute-start | bytes 2752520 | tf_op jit(solution)/shard_map/ppermute | solution.py:101
  60.2 8.7 %collective-permute-done.5.refs_1_ = bf16[1792,256]{1,0:T(8,128)(2,1)S(1)} collective-permute-done((bf16[1792,256]{1,0:T(8,128)(2,1)}, bf16[1792,256]{1,0:T(8,128)(2,1)S(1)}, u32[]{:S(2)}, u32[]{:S(2)}) %collective-permute-start.5) | collective-permute-done | bytes 917536 | tf_op jit(solution)/shard_map/ppermute | solution.py:101
  76.0 13.1 %collective-permute-done.6.refs_2_ = bf16[1792,256]{1,0:T(8,128)(2,1)S(1)} collective-permute-done((bf16[1792,256]{1,0:T(8,128)(2,1)}, bf16[1792,256]{1,0:T(8,128)(2,1)S(1)}, u32[]{:S(2)}, u32[]{:S(2)}) %collective-permute-start.6) | collective-permute-done | bytes 917536 | tf_op jit(solution)/shard_map/ppermute | solution.py:101
  89.1 7.1 %collective-permute-done.7.refs_3_ = bf16[1792,256]{1,0:T(8,128)(2,1)S(1)} collective-permute-done((bf16[1792,256]{1,0:T(8,128)(2,1)}, bf16[1792,256]{1,0:T(8,128)(2,1)S(1)}, u32[]{:S(2)}, u32[]{:S(2)}) %collective-permute-start.7) | collective-permute-done | bytes 917536 | tf_op jit(solution)/shard_map/ppermute | solution.py:101
  96.8 4.9 %collective-permute-done.13.refs_3_.refs_7_ = bf16[2064,256]{1,0:T(8,128)(2,1)S(1)} collective-permute-done((bf16[2064,256]{1,0:T(8,128)(2,1)S(1)}, bf16[2064,256]{1,0:T(8,128)(2,1)S(1)}, u32[]{:S(2)}, u32[]{:S(2)}) %collective-permute-start.13) | collective-permute-done | bytes 1056800 | tf_op jit(solution)/shard_map/ppermute | solution.py:101
  104.3 9.7 %convolution_convert_fusion = bf16[2048,1792]{1,0:T(8,128)(2,1)} fusion(bf16[2048,1024]{1,0:T(8,128)(2,1)S(1)} %get-tuple-element.40, bf16[1792,1024]{1,0:T(8,128)(2,1)S(1)} %shard_map.123), kind=kOutput, calls=%fused_computation | convolution fusion | flops 7519862784 | bytes 15204352 | tf_op jit(solution)/shard_map/dot_general | solution.py:502
  114.1 6.5 %convolution_convert_fusion.5.refs_4_ = bf16[2048,256]{1,0:T(8,128)(2,1)} fusion(bf16[2048,1792]{1,0:T(8,128)(2,1)} %all-gather.2.cloned.1.call-done.refs_0_, bf16[1792,1024]{1,0:T(8,128)(2,1)} %copy-done.7, s32[]{:T(128)S(6)} %select_n.69), kind=kOutput, calls=%fused_computation.5 | convolution fusion | flops 1879572480 | bytes 9306116 | tf_op jit(solution)/shard_map/dot_general | solution.py:502
  121.1 3.1 %convolution_convert_fusion.6.refs_3_ = bf16[2048,256]{1,0:T(8,128)(2,1)} fusion(bf16[2048,1792]{1,0:T(8,128)(2,1)S(1)} %copy-done, bf16[1792,1024]{1,0:T(8,128)(2,1)S(1)} %copy-done.8, s32[]{:T(128)S(6)} %select_n.67), kind=kOutput, calls=%fused_computation.6 | convolution fusion | flops 1879572480 | bytes 9306116 | tf_op jit(solution)/shard_map/dot_general | solution.py:502
  126.6 3.1 %convolution_convert_fusion.7.refs_2_ = bf16[2048,256]{1,0:T(8,128)(2,1)} fusion(bf16[2048,1792]{1,0:T(8,128)(2,1)S(1)} %copy-done, bf16[1792,1024]{1,0:T(8,128)(2,1)S(1)} %copy-done.8, s32[]{:T(128)S(6)} %select_n.65), kind=kOutput, calls=%fused_computation.7 | convolution fusion | flops 1879572480 | bytes 9306116 | tf_op jit(solution)/shard_map/dot_general | solution.py:502
  137.6 3.1 %convolution_convert_fusion.2 = bf16[1792,256]{1,0:T(8,128)(2,1)} fusion(bf16[2048,1792]{1,0:T(8,128)(2,1)S(1)} %shard_map.124, bf16[2048,1024]{1,0:T(8,128)(2,1)S(1)} %copy-done.26, s32[]{:T(128)S(6)} %select_n.76), kind=kOutput, calls=%fused_computation.2 | convolution fusion | flops 1879506944 | bytes 9306116 | tf_op jit(solution)/shard_map/dot_general | solution.py:502
  142.7 3.1 %convolution_convert_fusion.3 = bf16[1792,256]{1,0:T(8,128)(2,1)} fusion(bf16[2048,1792]{1,0:T(8,128)(2,1)S(1)} %shard_map.124, bf16[2048,1024]{1,0:T(8,128)(2,1)S(1)} %copy-done.26, s32[]{:T(128)S(6)} %select_n.74), kind=kOutput, calls=%fused_computation.3 | convolution fusion | flops 1879506944 | bytes 9306116 | tf_op jit(solution)/shard_map/dot_general | solution.py:502
  145.9 13.2 %collective-permute-done.16.refs_3_ = bf16[1792,256]{1,0:T(8,128)(2,1)S(1)} collective-permute-done((bf16[1792,256]{1,0:T(8,128)(2,1)S(1)}, bf16[1792,256]{1,0:T(8,128)(2,1)S(1)}, u32[]{:S(2)}, u32[]{:S(2)}) %collective-permute-start.16) | collective-permute-done | bytes 917536 | tf_op jit(solution)/shard_map/ppermute | solution.py:101
  161.9 5.5 %convolution_convert_fusion.4.refs_0_ = bf16[1792,256]{1,0:T(8,128)(2,1)S(1)} fusion(bf16[2048,1792]{1,0:T(8,128)(2,1)} %copy-done.1, bf16[2048,1024]{1,0:T(8,128)(2,1)} %copy-done.25, s32[]{:T(128)S(6)} %select_n.72), kind=kOutput, calls=%fused_computation.4 | convolution fusion | flops 1879506944 | bytes 9306116 | tf_op jit(solution)/shard_map/dot_general | solution.py:502
  167.4 10.0 %collective-permute-done.15.refs_2_ = bf16[1792,256]{1,0:T(8,128)(2,1)} collective-permute-done((bf16[1792,256]{1,0:T(8,128)(2,1)}, bf16[1792,256]{1,0:T(8,128)(2,1)}, u32[]{:S(2)}, u32[]{:S(2)}) %collective-permute-start.15) | collective-permute-done | bytes 917536 | tf_op jit(solution)/shard_map/ppermute | solution.py:101
  177.4 3.8 %shard_map.126 = (bf16[1792,256]{1,0:T(8,128)(2,1)}, f32[8,128]{1,0:T(8,128)S(1)}) custom-call(bf16[1792,256]{1,0:T(8,128)(2,1)S(1)} %convolution_convert_fusion.4.refs_0_, bf16[1792,256]{1,0:T(8,128)(2,1)} %collective-permute-done.14.refs_1_, bf16[1792,256]{1,0:T(8,128)(2,1)} %collective-permute-done.15.refs_2_, bf16[1792,256]{1,0:T(8,128)(2,1)S(1)} %copy-done.18), custom_call_target="tpu_custom_call" | custom-call | tf_op jit(solution)/shard_map/pallas_call | solution.py:117
  183.6 5.6 %collective-permute-start.17 = (bf16[512,256]{1,0:T(8,128)(2,1)S(1)}, bf16[512,256]{1,0:T(8,128)(2,1)S(1)}, u32[]{:S(2)}, u32[]{:S(2)}) collective-permute-start(bf16[512,256]{1,0:T(8,128)(2,1)S(1)} %get-tuple-element.42), channel_id=1, source_target_pairs={{8,0},{24,1},{10,2},{26,3},{12,4},{28,5},{14,6},{30,7},{11,8},{15,... | collective-permute-start | bytes 786440 | tf_op jit(solution)/shard_map/ppermute | solution.py:101
  189.2 4.1 %collective-permute-start.18 = (bf16[512,256]{1,0:T(8,128)(2,1)S(1)}, bf16[512,256]{1,0:T(8,128)(2,1)S(1)}, u32[]{:S(2)}, u32[]{:S(2)}) collective-permute-start(bf16[512,256]{1,0:T(8,128)(2,1)S(1)} %get-tuple-element.43), channel_id=1, source_target_pairs={{3,0},{7,1},{35,2},{39,3},{67,4},{71,5},{99,6},{103,7},{9,8},{13,9... | collective-permute-start | bytes 786440 | tf_op jit(solution)/shard_map/ppermute | solution.py:101
  193.3 3.1 %collective-permute-start.19 = (bf16[512,256]{1,0:T(8,128)(2,1)S(1)}, bf16[512,256]{1,0:T(8,128)(2,1)S(1)}, u32[]{:S(2)}, u32[]{:S(2)}) collective-permute-start(bf16[512,256]{1,0:T(8,128)(2,1)S(1)} %get-tuple-element.44), channel_id=1, source_target_pairs={{0,0},{16,1},{2,2},{18,3},{4,4},{20,5},{6,6},{22,7},{8,8},{24,9},{... | collective-permute-start | bytes 786440 | tf_op jit(solution)/shard_map/ppermute | solution.py:101
  196.3 3.6 %collective-permute-start.20 = (bf16[512,256]{1,0:T(8,128)(2,1)S(1)}, bf16[512,256]{1,0:T(8,128)(2,1)S(1)}, u32[]{:S(2)}, u32[]{:S(2)}) collective-permute-start(bf16[512,256]{1,0:T(8,128)(2,1)S(1)} %get-tuple-element.45), channel_id=1, source_target_pairs={{1,0},{5,1},{33,2},{37,3},{65,4},{69,5},{97,6},{101,7},{0,8},{16,9... | collective-permute-start | bytes 786440 | tf_op jit(solution)/shard_map/ppermute | solution.py:101
  201.2 3.6 %collective-permute-done.21 = f32[8,128]{1,0:T(8,128)S(1)} collective-permute-done((f32[8,128]{1,0:T(8,128)S(1)}, f32[8,128]{1,0:T(8,128)S(1)}, u32[]{:S(2)}, u32[]{:S(2)}) %collective-permute-start.21) | collective-permute-done | bytes 4128 | tf_op jit(solution)/shard_map/ppermute | solution.py:101
  204.8 4.0 %collective-permute-done.22 = f32[8,128]{1,0:T(8,128)S(1)} collective-permute-done((f32[8,128]{1,0:T(8,128)S(1)}, f32[8,128]{1,0:T(8,128)S(1)}, u32[]{:S(2)}, u32[]{:S(2)}) %collective-permute-start.22) | collective-permute-done | bytes 4128 | tf_op jit(solution)/shard_map/ppermute | solution.py:101
  (109 shorter events, 58.6 us)
Async XLA Ops:
  7.2 106.9 %all-gather.2.cloned.1.call-start = ((), (), s32[]{:S(2)}) async-start(), calls=%async_computation.1 | async-start | bytes 9175040 | tf_op jit(solution)/shard_map/all_gather | solution.py:521
  17.2 15.9 %collective-permute-start.1 = (bf16[528,256]{1,0:T(8,128)(2,1)S(1)}, bf16[528,256]{1,0:T(8,128)(2,1)S(1)}, u32[]{:S(2)}, u32[]{:S(2)}) collective-permute-start(bf16[528,256]{1,0:T(8,128)(2,1)S(1)} %get-tuple-element.33), channel_id=1, source_target_pairs={{0,8},{1,24},{2,10},{3,26},{4,12},{5,28},{6,14},{7,30},{8,11},{9,1... | collective-permute-start | bytes 811016 | tf_op jit(solution)/shard_map/ppermute | solution.py:101
  21.3 28.5 %collective-permute-start.2 = (bf16[528,256]{1,0:T(8,128)(2,1)S(1)}, bf16[528,256]{1,0:T(8,128)(2,1)S(1)}, u32[]{:S(2)}, u32[]{:S(2)}) collective-permute-start(bf16[528,256]{1,0:T(8,128)(2,1)S(1)} %get-tuple-element.34), channel_id=1, source_target_pairs={{0,3},{1,7},{2,35},{3,39},{4,67},{5,71},{6,99},{7,103},{8,9},{9,13... | collective-permute-start | bytes 811016 | tf_op jit(solution)/shard_map/ppermute | solution.py:101
  23.3 26.6 %collective-permute-start.3 = (bf16[528,256]{1,0:T(8,128)(2,1)S(1)}, bf16[528,256]{1,0:T(8,128)(2,1)S(1)}, u32[]{:S(2)}, u32[]{:S(2)}) collective-permute-start(bf16[528,256]{1,0:T(8,128)(2,1)S(1)} %get-tuple-element.35), channel_id=1, source_target_pairs={{0,0},{1,16},{2,2},{3,18},{4,4},{5,20},{6,6},{7,22},{8,8},{9,24},{... | collective-permute-start | bytes 811016 | tf_op jit(solution)/shard_map/ppermute | solution.py:101
  30.3 19.6 %collective-permute-start.4 = (bf16[528,256]{1,0:T(8,128)(2,1)S(1)}, bf16[528,256]{1,0:T(8,128)(2,1)S(1)}, u32[]{:S(2)}, u32[]{:S(2)}) collective-permute-start(bf16[528,256]{1,0:T(8,128)(2,1)S(1)} %get-tuple-element.36), channel_id=1, source_target_pairs={{0,1},{1,5},{2,33},{3,37},{4,65},{5,69},{6,97},{7,101},{8,0},{9,16... | collective-permute-start | bytes 811016 | tf_op jit(solution)/shard_map/ppermute | solution.py:101
  52.8 159.5 %reduce-scatter.2.cloned.1.call-start = ((), (), s32[]{:S(2)}) async-start(), calls=%async_computation.2 | async-start | bytes 9175040 | tf_op jit(solution)/shard_map/reduce_scatter | solution.py:531
  52.8 16.1 %collective-permute-start.5 = (bf16[1792,256]{1,0:T(8,128)(2,1)}, bf16[1792,256]{1,0:T(8,128)(2,1)S(1)}, u32[]{:S(2)}, u32[]{:S(2)}) collective-permute-start(bf16[1792,256]{1,0:T(8,128)(2,1)} %copy-done.9), channel_id=1, source_target_pairs={{0,96},{1,25},{2,98},{3,27},{4,100},{5,29},{6,102},{7,31},{8,104},... | collective-permute-start | bytes 2752520 | tf_op jit(solution)/shard_map/ppermute | solution.py:101
  52.9 43.8 %collective-permute-start.11 = (bf16[2064,256]{1,0:T(8,128)(2,1)S(1)}, bf16[2064,256]{1,0:T(8,128)(2,1)S(1)}, u32[]{:S(2)}, u32[]{:S(2)}) collective-permute-start(bf16[2064,256]{1,0:T(8,128)(2,1)S(1)} %shard_map.120.refs_2_.refs_0_.refs_4_), channel_id=1, source_target_pairs={{0,6},{1,7},{2,0},{3,1},{4,2},{5,3},{6,4},{7,5},{8,14},{9,15},{10,... | collective-permute-start | bytes 3170312 | tf_op jit(solution)/shard_map/ppermute | solution.py:101
  53.0 43.8 %collective-permute-start.12 = (bf16[2064,256]{1,0:T(8,128)(2,1)S(1)}, bf16[2064,256]{1,0:T(8,128)(2,1)S(1)}, u32[]{:S(2)}, u32[]{:S(2)}) collective-permute-start(bf16[2064,256]{1,0:T(8,128)(2,1)S(1)} %shard_map.120.refs_2_.refs_0_.refs_4_), channel_id=1, source_target_pairs={{0,4},{1,5},{2,6},{3,7},{4,0},{5,1},{6,2},{7,3},{8,12},{9,13},{10,... | collective-permute-start | bytes 3170312 | tf_op jit(solution)/shard_map/ppermute | solution.py:101
  55.5 46.2 %collective-permute-start.13 = (bf16[2064,256]{1,0:T(8,128)(2,1)S(1)}, bf16[2064,256]{1,0:T(8,128)(2,1)S(1)}, u32[]{:S(2)}, u32[]{:S(2)}) collective-permute-start(bf16[2064,256]{1,0:T(8,128)(2,1)S(1)} %shard_map.120.refs_2_.refs_0_.refs_4_), channel_id=1, source_target_pairs={{0,2},{1,3},{2,4},{3,5},{4,6},{5,7},{6,0},{7,1},{8,10},{9,11},{10,... | collective-permute-start | bytes 3170312 | tf_op jit(solution)/shard_map/ppermute | solution.py:101
  55.5 33.6 %collective-permute-start.6 = (bf16[1792,256]{1,0:T(8,128)(2,1)}, bf16[1792,256]{1,0:T(8,128)(2,1)S(1)}, u32[]{:S(2)}, u32[]{:S(2)}) collective-permute-start(bf16[1792,256]{1,0:T(8,128)(2,1)} %copy-done.9), channel_id=1, source_target_pairs={{0,64},{1,17},{2,66},{3,19},{4,68},{5,21},{6,70},{7,23},{8,72},{9,... | collective-permute-start | bytes 2752520 | tf_op jit(solution)/shard_map/ppermute | solution.py:101
  68.9 27.3 %collective-permute-start.7 = (bf16[1792,256]{1,0:T(8,128)(2,1)}, bf16[1792,256]{1,0:T(8,128)(2,1)S(1)}, u32[]{:S(2)}, u32[]{:S(2)}) collective-permute-start(bf16[1792,256]{1,0:T(8,128)(2,1)} %copy-done.9), channel_id=1, source_target_pairs={{0,32},{1,9},{2,34},{3,11},{4,36},{5,13},{6,38},{7,15},{8,40},{9,1... | collective-permute-start | bytes 2752520 | tf_op jit(solution)/shard_map/ppermute | solution.py:101
  120.6 60.5 %collective-permute-start.10 = (bf16[2048,256]{1,0:T(8,128)(2,1)}, bf16[2048,256]{1,0:T(8,128)(2,1)}, u32[]{:S(2)}, u32[]{:S(2)}) collective-permute-start(bf16[2048,256]{1,0:T(8,128)(2,1)} %convolution_convert_fusion.5.refs_4_), channel_id=1, source_target_pairs={{0,6},{1,7},{2,0},{3,1},{4,2},{5,3},{6,4},{7,5},{8,14},{9,15},{10,... | collective-permute-start | bytes 3145736 | tf_op jit(solution)/shard_map/ppermute | solution.py:101
  124.3 56.9 %collective-permute-start.9 = (bf16[2048,256]{1,0:T(8,128)(2,1)}, bf16[2048,256]{1,0:T(8,128)(2,1)}, u32[]{:S(2)}, u32[]{:S(2)}) collective-permute-start(bf16[2048,256]{1,0:T(8,128)(2,1)} %convolution_convert_fusion.6.refs_3_), channel_id=1, source_target_pairs={{0,4},{1,5},{2,6},{3,7},{4,0},{5,1},{6,2},{7,3},{8,12},{9,13},{10,... | collective-permute-start | bytes 3145736 | tf_op jit(solution)/shard_map/ppermute | solution.py:101
  129.7 51.5 %collective-permute-start.8 = (bf16[2048,256]{1,0:T(8,128)(2,1)}, bf16[2048,256]{1,0:T(8,128)(2,1)}, u32[]{:S(2)}, u32[]{:S(2)}) collective-permute-start(bf16[2048,256]{1,0:T(8,128)(2,1)} %convolution_convert_fusion.7.refs_2_), channel_id=1, source_target_pairs={{0,2},{1,3},{2,4},{3,5},{4,6},{5,7},{6,0},{7,1},{8,10},{9,11},{10,... | collective-permute-start | bytes 3145736 | tf_op jit(solution)/shard_map/ppermute | solution.py:101
  136.4 22.6 %collective-permute-start.16 = (bf16[1792,256]{1,0:T(8,128)(2,1)S(1)}, bf16[1792,256]{1,0:T(8,128)(2,1)S(1)}, u32[]{:S(2)}, u32[]{:S(2)}) collective-permute-start(bf16[1792,256]{1,0:T(8,128)(2,1)S(1)} %convolution_convert_fusion.1), channel_id=1, source_target_pairs={{0,96},{1,25},{2,98},{3,27},{4,100},{5,29},{6,102},{7,31},{8,104},... | collective-permute-start | bytes 2752520 | tf_op jit(solution)/shard_map/ppermute | solution.py:101
  140.8 36.6 %collective-permute-start.15 = (bf16[1792,256]{1,0:T(8,128)(2,1)}, bf16[1792,256]{1,0:T(8,128)(2,1)}, u32[]{:S(2)}, u32[]{:S(2)}) collective-permute-start(bf16[1792,256]{1,0:T(8,128)(2,1)} %convolution_convert_fusion.2), channel_id=1, source_target_pairs={{0,64},{1,17},{2,66},{3,19},{4,68},{5,21},{6,70},{7,23},{8,72},{9,... | collective-permute-start | bytes 2752520 | tf_op jit(solution)/shard_map/ppermute | solution.py:101
  160.0 17.4 %collective-permute-start.14 = (bf16[1792,256]{1,0:T(8,128)(2,1)}, bf16[1792,256]{1,0:T(8,128)(2,1)}, u32[]{:S(2)}, u32[]{:S(2)}) collective-permute-start(bf16[1792,256]{1,0:T(8,128)(2,1)} %convolution_convert_fusion.3), channel_id=1, source_target_pairs={{0,32},{1,9},{2,34},{3,11},{4,36},{5,13},{6,38},{7,15},{8,40},{9,1... | collective-permute-start | bytes 2752520 | tf_op jit(solution)/shard_map/ppermute | solution.py:101
  183.6 26.9 %collective-permute-start.17 = (bf16[512,256]{1,0:T(8,128)(2,1)S(1)}, bf16[512,256]{1,0:T(8,128)(2,1)S(1)}, u32[]{:S(2)}, u32[]{:S(2)}) collective-permute-start(bf16[512,256]{1,0:T(8,128)(2,1)S(1)} %get-tuple-element.42), channel_id=1, source_target_pairs={{8,0},{24,1},{10,2},{26,3},{12,4},{28,5},{14,6},{30,7},{11,8},{15,... | collective-permute-start | bytes 786440 | tf_op jit(solution)/shard_map/ppermute | solution.py:101
  189.2 21.3 %collective-permute-start.18 = (bf16[512,256]{1,0:T(8,128)(2,1)S(1)}, bf16[512,256]{1,0:T(8,128)(2,1)S(1)}, u32[]{:S(2)}, u32[]{:S(2)}) collective-permute-start(bf16[512,256]{1,0:T(8,128)(2,1)S(1)} %get-tuple-element.43), channel_id=1, source_target_pairs={{3,0},{7,1},{35,2},{39,3},{67,4},{71,5},{99,6},{103,7},{9,8},{13,9... | collective-permute-start | bytes 786440 | tf_op jit(solution)/shard_map/ppermute | solution.py:101
  193.3 17.3 %collective-permute-start.19 = (bf16[512,256]{1,0:T(8,128)(2,1)S(1)}, bf16[512,256]{1,0:T(8,128)(2,1)S(1)}, u32[]{:S(2)}, u32[]{:S(2)}) collective-permute-start(bf16[512,256]{1,0:T(8,128)(2,1)S(1)} %get-tuple-element.44), channel_id=1, source_target_pairs={{0,0},{16,1},{2,2},{18,3},{4,4},{20,5},{6,6},{22,7},{8,8},{24,9},{... | collective-permute-start | bytes 786440 | tf_op jit(solution)/shard_map/ppermute | solution.py:101
  196.3 14.2 %collective-permute-start.20 = (bf16[512,256]{1,0:T(8,128)(2,1)S(1)}, bf16[512,256]{1,0:T(8,128)(2,1)S(1)}, u32[]{:S(2)}, u32[]{:S(2)}) collective-permute-start(bf16[512,256]{1,0:T(8,128)(2,1)S(1)} %get-tuple-element.45), channel_id=1, source_target_pairs={{1,0},{5,1},{33,2},{37,3},{65,4},{69,5},{97,6},{101,7},{0,8},{16,9... | collective-permute-start | bytes 786440 | tf_op jit(solution)/shard_map/ppermute | solution.py:101
  200.0 4.8 %collective-permute-start.21 = (f32[8,128]{1,0:T(8,128)S(1)}, f32[8,128]{1,0:T(8,128)S(1)}, u32[]{:S(2)}, u32[]{:S(2)}) collective-permute-start(f32[8,128]{1,0:T(8,128)S(1)} %shard_map.130), channel_id=1, source_target_pairs={{0,32},{1,33},{2,34},{3,35},{4,36},{5,37},{6,38},{7,39},{8,40},{9,... | collective-permute-start | bytes 12296 | tf_op jit(solution)/shard_map/ppermute | solution.py:101
  204.8 4.0 %collective-permute-start.22 = (f32[8,128]{1,0:T(8,128)S(1)}, f32[8,128]{1,0:T(8,128)S(1)}, u32[]{:S(2)}, u32[]{:S(2)}) collective-permute-start(f32[8,128]{1,0:T(8,128)S(1)} %max.6), channel_id=1, source_target_pairs={{0,64},{1,65},{2,66},{3,67},{4,68},{5,69},{6,70},{7,71},{8,72},{9,... | collective-permute-start | bytes 12296 | tf_op jit(solution)/shard_map/ppermute | solution.py:101
  (29 other events, 288.9 us)
Sparse Core Ops, SparseCore 0:
  52.9 57.9 all-gather.1
  114.1 56.2 reduce-scatter.1

commit v2 on v1

--- a/solution.py
+++ b/solution.py
@@ -220,41 +220,60 @@
     )
 
 
-def activate_kernel(gate, up, weight, act_history, weight_history,
-                    act_q, weight_q, peaks, act_top, weight_top):
+def clip_kernel(weight, history, weight_q, peak, top):
+    step = pl.program_id(0)
+    weight_v = weight[...].astype(F32)
+    limit = jnp.max(history[...], axis=1, keepdims=True)
+    weight_q[...] = jnp.clip(weight_v, -limit, limit).astype(BF16)
+    keep_peak(step, top, peak_of(weight_v))
+
+    @pl.when(step == pl.num_programs(0) - 1)
+    def _():
+        peak[...] = jnp.broadcast_to(jnp.max(top[...], axis=1, keepdims=True), peak.shape)
+
+
+def clip_weight(weight, history):
+    steps = 2
+    rows = row_blocks(weight, steps)
+    return call(
+        clip_kernel,
+        (shape(*weight.shape), shape(8, 128, dtype=F32)),
+        (0, 0),
+        [rows, fixed(1, history.shape[1])],
+        (weight, history),
+        grid=(steps,),
+        out_specs=[rows, fixed(8, 128)],
+        scratch_shapes=[pltpu.VMEM((1, weight.shape[1]), F32)],
+    )
+
+
+def activate_kernel(gate, up, weight_peak, history, act_q, peaks, top):
     step = pl.program_id(0)
     gate_v = gate[...].astype(F32)
     act = gate_v * jax.nn.sigmoid(gate_v) * up[...].astype(F32)
-    limit = jnp.max(act_history[...], axis=1, keepdims=True)
+    limit = jnp.max(history[...], axis=1, keepdims=True)
     act_q[...] = jnp.clip(act, -limit, limit).astype(BF16)
-    weight_v = weight[...].astype(F32)
-    limit = jnp.max(weight_history[...], axis=1, keepdims=True)
-    weight_q[...] = jnp.clip(weight_v, -limit, limit).astype(BF16)
-    keep_peak(step, act_top, peak_of(act))
-    keep_peak(step, weight_top, peak_of(weight_v))
+    keep_peak(step, top, peak_of(act))
 
     @pl.when(step == pl.num_programs(0) - 1)
     def _():
         row = lax.broadcasted_iota(jnp.int32, peaks.shape, 0)
-        top = jnp.max(act_top[...], axis=1, keepdims=True)
-        other = jnp.max(weight_top[...], axis=1, keepdims=True)
-        peaks[...] = jnp.where(
-            row == 0, jnp.broadcast_to(top, peaks.shape), jnp.broadcast_to(other, peaks.shape)
-        )
-
-
-def activate(gate, up, weight, act_history, weight_history):
+        act_peak = jnp.broadcast_to(jnp.max(top[...], axis=1, keepdims=True), peaks.shape)
+        peaks[...] = jnp.where(row == 0, act_peak, weight_peak[...])
+
+
+def activate(gate, up, weight_peak, history):
     steps = 8
-    rows, weight_rows = row_blocks(gate, steps), row_blocks(weight, steps)
+    rows = row_blocks(gate, steps)
     return call(
         activate_kernel,
-        (shape(*gate.shape), shape(*weight.shape), shape(8, 128, dtype=F32)),
-        (0, 0),
-        [rows, rows, weight_rows, fixed(1, act_history.shape[1]), fixed(1, act_history.shape[1])],
-        (gate, up, weight, act_history, weight_history),
-        grid=(steps,),
-        out_specs=[rows, weight_rows, fixed(8, 128)],
-        scratch_shapes=[pltpu.VMEM((1, gate.shape[1]), F32), pltpu.VMEM((1, weight.shape[1]), F32)],
+        (shape(*gate.shape), shape(8, 128, dtype=F32)),
+        (0, 0),
+        [rows, rows, fixed(8, 128), fixed(1, history.shape[1])],
+        (gate, up, weight_peak, history),
+        grid=(steps,),
+        out_specs=[rows, fixed(8, 128)],
+        scratch_shapes=[pltpu.VMEM((1, gate.shape[1]), F32)],
     )
 
 
@@ -326,45 +345,97 @@
 def columns_kernel(place, own, after, far, before, out):
     width = own.shape[1]
     for step, block in enumerate((own, after, far, before)):
-        column = pl.multiple_of(lax.rem(place + step, N) * width, width)
+        column = (place + step) % N * width
+        if not isinstance(column, int):
+            column = pl.multiple_of(column, width)
         out[:, pl.ds(column, width)] = block[...]
 
 
-def weight_tile_kernel(*refs):
-    columns_kernel(here()[1], *refs)
-
-
-def weight_tile(parts, after):
+def half_blocks(steps, dims):
+    first = pl.BlockSpec(dims, lambda i: (jnp.minimum(i, steps // 2 - 1), 0))
+    second = pl.BlockSpec(dims, lambda i: (jnp.maximum(i - steps // 2, 0), 0))
+    return [first, second]
+
+
+def weight_tile_kernel(own, after, top, bottom, before, out):
+    place = here()[1]
+    step = pl.program_id(0)
+
+    @pl.when(step < pl.num_programs(0) // 2)
+    def _():
+        columns_kernel(place, own, after, top, before, out)
+
+    @pl.when(step >= pl.num_programs(0) // 2)
+    def _():
+        columns_kernel(place, own, after, bottom, before, out)
+
+
+def weight_tile(*parts):
     steps = 4
-    out = shape(parts[0].shape[0], N * parts[0].shape[1])
+    hidden, features = parts[0].shape
+    dims = (hidden // steps, features)
+    block = pl.BlockSpec(dims, lambda i: (i, 0))
+    out = shape(hidden, N * features)
     return call(
         weight_tile_kernel,
         out,
         (0, 0),
-        [row_blocks(parts[0], steps)] * N,
+        [block, block, *half_blocks(steps, dims), block],
         parts,
-        after,
         grid=(steps,),
         out_specs=row_blocks(out, steps),
     )
 
 
-def grad_tile_kernel(own, after, far, before, note0, note1, note2, note3, out, peaks):
-    columns_kernel(here()[2], own, after, far, before, out)
+def raise_kernel(after, before, top, bottom, out_after, out_before):
+    rows = top.shape[0]
+    out_after[:rows, :] = (after[:rows, :].astype(F32) + top[...].astype(F32)).astype(BF16)
+    out_after[rows:, :] = after[rows:, :]
+    out_before[:rows, :] = before[:rows, :]
+    out_before[rows:, :] = (before[rows:, :].astype(F32) + bottom[...].astype(F32)).astype(BF16)
+
+
+def add_halves(after, before, top, bottom):
+    whole = shape(*after.shape)
+    return call(
+        raise_kernel,
+        (whole, whole),
+        (0, 0),
+        [IN_VMEM] * 4,
+        (after, before, top, bottom),
+        out_specs=[IN_VMEM] * 2,
+    )
+
+
+def grad_tile_kernel(own, after, top, bottom, before, note0, note1, note2, note3, out, peaks):
+    place = here()[2]
+    step = pl.program_id(0)
+
+    @pl.when(step < pl.num_programs(0) // 2)
+    def _():
+        columns_kernel(place, own, after, top, before, out)
+
+    @pl.when(step >= pl.num_programs(0) // 2)
+    def _():
+        columns_kernel(place, own, after, bottom, before, out)
+
     peaks[...] = peaks_in((note0, note1, note2, note3))
 
 
-def grad_tile(parts):
+def grad_tile(own, after, top, bottom, before, order):
     steps = 4
-    rows, features = parts[0].shape[0] - NOTE, parts[0].shape[1]
+    rows, features = own.shape[0] - NOTE, own.shape[1]
     out = shape(rows, N * features)
-    block = pl.BlockSpec((rows // steps, features), lambda i: (i, 0))
+    dims = (rows // steps, features)
+    block = pl.BlockSpec(dims, lambda i: (i, 0))
+    noted = (own, after, bottom, before)
     return call(
         grad_tile_kernel,
         (out, shape(8, 128, dtype=F32)),
         (0, 0),
-        [block] * N + [note_block(part) for part in parts],
-        (*parts, *parts),
+        [block, block, *half_blocks(steps, dims), block] + [note_block(part) for part in noted],
+        (own, after, top, bottom, before, *noted),
+        order,
         grid=(steps,),
         out_specs=[row_blocks(out, steps), fixed(8, 128)],
     )
@@ -404,13 +475,12 @@
     )
 
 
-def return_kernel(table, part0, part1, part2, part3, out0, out1, out2, out3):
+def return_kernel(table, own, before, after, out0, out1, out2, out3):
     me, _, _ = here()
     tokens = out0.shape[0]
     for number, out in enumerate((out0, out1, out2, out3)):
         rows = pl.ds(pl.multiple_of(table[4 + number, me] * tokens, tokens), tokens)
-        total = part0[rows, :].astype(F32) + part1[rows, :].astype(F32)
-        total = total + (part2[rows, :].astype(F32) + part3[rows, :].astype(F32))
+        total = own[rows, :].astype(F32) + before[rows, :].astype(F32) + after[rows, :].astype(F32)
         out[...] = total.astype(BF16)
 
 
@@ -420,7 +490,7 @@
         return_kernel,
         (shape(rows // N, features),) * 4,
         (0, 0),
-        [SCALARS] + [IN_VMEM] * 4,
+        [SCALARS] + [IN_VMEM] * 3,
         (jnp.asarray(TABLE), *parts),
         after,
         out_specs=[IN_VMEM] * 4,
@@ -504,47 +574,61 @@
 
 
 def on_device(gate_pre, up_pre, down_weight, grad_out, weight_history, act_history):
-    features = down_weight.shape[1]
     _, feature_place, z = here()
     groups = token_groups()
     swap = [(n, n ^ 1) for n in range(128)]
-    act_q, weight_q, peaks = activate(
-        gate_pre, up_pre, down_weight, act_history[None], weight_history[None]
-    )
+    weight_q, weight_peak = clip_weight(down_weight, weight_history[None])
+    weight_before, weight_after = send(weight_q, feature_ring(1)), send(weight_q, feature_ring(-1))
+    half = weight_q.shape[0] // 2
+    weight = weight_tile(
+        weight_q,
+        weight_after,
+        send(weight_before[:half], feature_ring(1)),
+        send(weight_after[half:], feature_ring(-1)),
+        weight_before,
+    )
+    act_q, peaks = activate(gate_pre, up_pre, weight_peak, act_history[None])
     blocks = share(grad_out, peaks, send(peaks, swap))
     blocks = [
         send(block, [(edge[0], edge[1]) for edge in ROUNDS[number]])
         for number, block in enumerate(blocks)
     ]
     grad = place(blocks)
-    act_q, weight_q = gate((act_q, weight_q), (grad,))
+    (act_q,) = gate((act_q,), (grad,))
     act = lax.all_gather(act_q, AXES, axis=0, tiled=True, axis_index_groups=groups)
-    weight_parts = ring_gather(weight_q, feature_ring)
     slope, silu, token = slopes(gate_pre, up_pre, (grad,))
-    tile, peaks = grad_tile(ring_gather(grad, hidden_ring))
-    weight = weight_tile(weight_parts, (token,))
+    before, after = send(grad, hidden_ring(1)), send(grad, hidden_ring(-1))
+    half = (grad.shape[0] - NOTE) // 2
+    top, bottom = send(before[:half], hidden_ring(1)), send(after[half:], hidden_ring(-1))
 
     def block_of(array, number):
-        return lax.dynamic_slice_in_dim(array, number % N * features, features, axis=1)
-
+        size = array.shape[1] // N
+        return lax.dynamic_slice_in_dim(array, number % N * size, size, axis=1)
+
+    tile, peaks = grad_tile(grad, after, top, bottom, before, (token,))
     grad_act = dot(tile, weight, ((1,), (1,)))
     grad_act = lax.psum_scatter(
         grad_act, AXES, scatter_dimension=0, tiled=True, axis_index_groups=groups
     )
-    mixed = [dot(act, block_of(weight, z + step), ((1,), (0,))) for step in range(N)]
-    act = gate((act,), mixed)[0]
-    mixed = ring_exchange(mixed, hidden_ring)
+    half = act.shape[0] // 2
+    mixed = [dot(act, block_of(weight, z + step), ((1,), (0,))) for step in (0, 1, 3)]
+    far = block_of(weight, z + 2)
+    mixed_top = send(dot(act[:half], far, ((1,), (0,))), hidden_ring(1))
+    mixed_bottom = send(dot(act[half:], far, ((1,), (0,))), hidden_ring(-1))
+    mixed_after, mixed_before = add_halves(mixed[1], mixed[2], mixed_top, mixed_bottom)
+    (act,) = gate((act,), (mixed[0], mixed_after))
     weight_grad = [
         dot(act, block_of(tile, feature_place + step), ((0,), (0,))) for step in range(N)
     ]
-    weight_grad, token = add(ring_exchange(weight_grad, feature_ring))
-    blocks = return_blocks(mixed, (token,))
+    weight_grad, _ = add(ring_exchange(weight_grad, feature_ring))
+    mixed = (mixed[0], send(mixed_after, hidden_ring(1)), send(mixed_before, hidden_ring(-1)))
+    blocks = return_blocks(mixed, ())
     blocks = [
         send(block, [(edge[1], edge[0]) for edge in ROUNDS[number]])
         for number, block in enumerate(blocks)
     ]
+    peaks = raise_peaks(later(peaks, blocks[:1]), (5, 6))
     grad_gate, grad_up = finish(slope, silu, grad_act)
-    peaks = raise_peaks(later(peaks, (token,)), (5, 6))
     new_weight, new_act = histories(
         peaks, send(peaks, swap), weight_history[None], act_history[None]
     )

time: 227 us -> 219 us (0.965)
  waiting for transfers between devices: 83.4 us -> 70 us
  starting transfers between devices: 50.8 us -> 61.8 us
    ppermute x24 -> x27, waiting for transfers between devices: 83.3 us -> 69.9 us  [send(): return lax.ppermute(value, AXES, pairs)]
    ppermute x24 -> x27, starting transfers between devices: 50.8 us -> 61.7 us  [send(): return lax.ppermute(value, AXES, pairs)]
    dot_general x9 -> x10, matrix products: 38.6 us -> 36.9 us  [dot(): lax.dot_general(left, right, (dims, ((), ())), preferred_element_type=F32)]
    pallas_call x14 -> x16, Pallas kernels: 17.4 us -> 17.1 us  [call(): pl.pallas_call(body, out_shape=out_shape, in_specs=list(in_specs) + [ANYW...]
  transfers between devices with their start and end apart: 26 -> 29, of which waited for: 11 -> 12; matrix products, arithmetic and copies ran while one was open for 17% -> 17% of each run, Pallas kernels for 5% -> 5%
where the time goes in v2:
time: 219 us
  waiting for transfers between devices  70 us (32%)
  starting transfers between devices  61.8 us (28%)
  matrix products  36.9 us (17%)
  local copies, waits for them, and re-layouts  18.2 us (8%)
  Pallas kernels  17.1 us (8%)
  between operations  14.6 us (7%)
    ppermute x27, waiting for transfers between devices, send(): return lax.ppermute(value, AXES, pairs)  69.9 us
    ppermute x27, starting transfers between devices, send(): return lax.ppermute(value, AXES, pairs)  61.7 us
    dot_general x10, matrix products, dot(): lax.dot_general(left, right, (dims, ((), ())), preferred_element_type=F32)  36.9 us
    unnamed x54, local copies, waits for them, and re-layouts  18 us
    pallas_call x16, Pallas kernels, call(): pl.pallas_call(body, out_shape=out_shape, in_specs=list(in_specs) + [ANYW...  17.1 us
  transfers between devices with their start and end apart: 29, of which 12 were waited for; matrix products, arithmetic and copies ran while one was open for 17% of the time, Pallas kernels for 5%

profile of v2, /device:TPU:15, one launch (start us, length us, event | category | flops | bytes accessed | tf_op | source)
XLA Modules:
  0.0 218.5 jit_solution(13662520647976425300)
XLA Ops:
  18.3 4.1 %collective-permute-start.1 = (bf16[528,256]{1,0:T(8,128)(2,1)S(1)}, bf16[528,256]{1,0:T(8,128)(2,1)S(1)}, u32[]{:S(2)}, u32[]{:S(2)}) collective-permute-start(bf16[528,256]{1,0:T(8,128)(2,1)S(1)} %get-tuple-element.33), channel_id=1, source_target_pairs={{0,8},{1,24},{2,10},{3,26},{4,12},{5,28},{6,14},{7,30},{8,11},{9,1... | collective-permute-start | bytes 811016 | tf_op jit(solution)/shard_map/ppermute | solution.py:101
  24.4 7.0 %collective-permute-start.3 = (bf16[528,256]{1,0:T(8,128)(2,1)S(1)}, bf16[528,256]{1,0:T(8,128)(2,1)S(1)}, u32[]{:S(2)}, u32[]{:S(2)}) collective-permute-start(bf16[528,256]{1,0:T(8,128)(2,1)S(1)} %get-tuple-element.35), channel_id=1, source_target_pairs={{0,0},{1,16},{2,2},{3,18},{4,4},{5,20},{6,6},{7,22},{8,8},{9,24},{... | collective-permute-start | bytes 811016 | tf_op jit(solution)/shard_map/ppermute | solution.py:101
  31.4 2.8 %collective-permute-start.4 = (bf16[528,256]{1,0:T(8,128)(2,1)S(1)}, bf16[528,256]{1,0:T(8,128)(2,1)S(1)}, u32[]{:S(2)}, u32[]{:S(2)}) collective-permute-start(bf16[528,256]{1,0:T(8,128)(2,1)S(1)} %get-tuple-element.36), channel_id=1, source_target_pairs={{0,1},{1,5},{2,33},{3,37},{4,65},{5,69},{6,97},{7,101},{8,0},{9,16... | collective-permute-start | bytes 811016 | tf_op jit(solution)/shard_map/ppermute | solution.py:101
  34.2 16.7 %collective-permute-done.2.refs_2_ = bf16[528,256]{1,0:T(8,128)(2,1)S(1)} collective-permute-done((bf16[528,256]{1,0:T(8,128)(2,1)S(1)}, bf16[528,256]{1,0:T(8,128)(2,1)S(1)}, u32[]{:S(2)}, u32[]{:S(2)}) %collective-permute-start.2) | collective-permute-done | bytes 270368 | tf_op jit(solution)/shard_map/ppermute | solution.py:101
  54.6 4.7 %collective-permute-start.6 = (bf16[1792,256]{1,0:T(8,128)(2,1)}, bf16[1792,256]{1,0:T(8,128)(2,1)S(1)}, u32[]{:S(2)}, u32[]{:S(2)}) collective-permute-start(bf16[1792,256]{1,0:T(8,128)(2,1)} %copy-done.14), channel_id=1, source_target_pairs={{0,32},{1,9},{2,34},{3,11},{4,36},{5,13},{6,38},{7,15},{8,40},{9,1... | collective-permute-start | bytes 2752520 | tf_op jit(solution)/shard_map/ppermute | solution.py:101
  59.3 18.4 %collective-permute-done.17.refs_1_.refs_6_ = bf16[2064,256]{1,0:T(8,128)(2,1)S(1)} collective-permute-done((bf16[2064,256]{1,0:T(8,128)(2,1)S(1)}, bf16[2064,256]{1,0:T(8,128)(2,1)S(1)}, u32[]{:S(2)}, u32[]{:S(2)}) %collective-permute-start.17) | collective-permute-done | bytes 1056800 | tf_op jit(solution)/shard_map/ppermute | solution.py:101
  84.4 7.8 %collective-permute-done.7.refs_2_ = bf16[896,256]{1,0:T(8,128)(2,1)S(1)} collective-permute-done((bf16[896,256]{1,0:T(8,128)(2,1)S(1)}, bf16[896,256]{1,0:T(8,128)(2,1)S(1)}, u32[]{:S(2)}, u32[]{:S(2)}) %collective-permute-start.7) | collective-permute-done | bytes 458784 | tf_op jit(solution)/shard_map/ppermute | solution.py:101
  97.7 9.7 %convolution_convert_fusion = bf16[2048,1792]{1,0:T(8,128)(2,1)} fusion(bf16[2048,1024]{1,0:T(8,128)(2,1)S(1)} %get-tuple-element.47, bf16[1792,1024]{1,0:T(8,128)(2,1)S(1)} %shard_map.123), kind=kOutput, calls=%fused_computation | convolution fusion | flops 7519862784 | bytes 15204352 | tf_op jit(solution)/shard_map/dot_general | solution.py:572
  107.6 3.6 %fusion.4 = bf16[1024,256]{1,0:T(8,128)(2,1)S(1)} fusion(bf16[2048,1792]{1,0:T(8,128)(2,1)} %all-gather.2.cloned.1.call-done.refs_0_, bf16[1792,1024]{1,0:T(8,128)(2,1)} %copy-done.7, s32[]{:T(128)S(6)} %select_n.69), kind=kOutput, calls=%fused_computation.12 | convolution fusion | flops 939786240 | bytes 5111812 | tf_op jit(solution)/shard_map/dot_general | solution.py:572
  112.1 2.4 %fusion.7 = bf16[1024,256]{1,0:T(8,128)(2,1)S(1)} fusion(bf16[2048,1792]{1,0:T(8,128)(2,1)S(1)} %copy-done.5, bf16[1792,1024]{1,0:T(8,128)(2,1)} %copy-done.7, s32[]{:T(128)S(6)} %select_n.69), kind=kOutput, calls=%fused_computation.13 | convolution fusion | flops 939786240 | bytes 5111812 | tf_op jit(solution)/shard_map/dot_general | solution.py:572
  122.8 2.9 %collective-permute-done.9.refs_2_ = bf16[1024,256]{1,0:T(8,128)(2,1)S(1)} collective-permute-done((bf16[1024,256]{1,0:T(8,128)(2,1)S(1)}, bf16[1024,256]{1,0:T(8,128)(2,1)S(1)}, u32[]{:S(2)}, u32[]{:S(2)}) %collective-permute-start.9) | collective-permute-done | bytes 524320 | tf_op jit(solution)/shard_map/ppermute | solution.py:101
  125.8 2.4 %collective-permute-done.10.refs_3_ = bf16[1024,256]{1,0:T(8,128)(2,1)S(1)} collective-permute-done((bf16[1024,256]{1,0:T(8,128)(2,1)S(1)}, bf16[1024,256]{1,0:T(8,128)(2,1)S(1)}, u32[]{:S(2)}, u32[]{:S(2)}) %collective-permute-start.10) | collective-permute-done | bytes 524320 | tf_op jit(solution)/shard_map/ppermute | solution.py:101
  133.0 3.3 %convolution_convert_fusion.3 = bf16[1792,256]{1,0:T(8,128)(2,1)} fusion(bf16[2048,1792]{1,0:T(8,128)(2,1)S(1)} %shard_map.130, bf16[2048,1024]{1,0:T(8,128)(2,1)S(1)} %copy-done.26, s32[]{:T(128)S(6)} %select_n.74), kind=kOutput, calls=%fused_computation.7 | convolution fusion | flops 1879506944 | bytes 9306116 | tf_op jit(solution)/shard_map/dot_general | solution.py:572
  136.3 3.0 %convolution_convert_fusion.2 = bf16[1792,256]{1,0:T(8,128)(2,1)} fusion(bf16[2048,1792]{1,0:T(8,128)(2,1)S(1)} %shard_map.130, bf16[2048,1024]{1,0:T(8,128)(2,1)S(1)} %copy-done.26, s32[]{:T(128)S(6)} %select_n.76), kind=kOutput, calls=%fused_computation.6 | convolution fusion | flops 1879506944 | bytes 9306116 | tf_op jit(solution)/shard_map/dot_general | solution.py:572
  140.6 11.7 %collective-permute-done.12.refs_3_ = bf16[2048,256]{1,0:T(8,128)(2,1)S(1)} collective-permute-done((bf16[2048,256]{1,0:T(8,128)(2,1)S(1)}, bf16[2048,256]{1,0:T(8,128)(2,1)S(1)}, u32[]{:S(2)}, u32[]{:S(2)}) %collective-permute-start.12) | collective-permute-done | bytes 1048608 | tf_op jit(solution)/shard_map/ppermute | solution.py:101
  152.3 2.5 %collective-permute-done.11.refs_2_ = bf16[2048,256]{1,0:T(8,128)(2,1)S(1)} collective-permute-done((bf16[2048,256]{1,0:T(8,128)(2,1)S(1)}, bf16[2048,256]{1,0:T(8,128)(2,1)S(1)}, u32[]{:S(2)}, u32[]{:S(2)}) %collective-permute-start.11) | collective-permute-done | bytes 1048608 | tf_op jit(solution)/shard_map/ppermute | solution.py:101
  158.3 3.1 %convolution_convert_fusion.1 = bf16[1792,256]{1,0:T(8,128)(2,1)} fusion(bf16[2048,1792]{1,0:T(8,128)(2,1)S(1)} %shard_map.130, bf16[2048,1024]{1,0:T(8,128)(2,1)S(1)} %copy-done.26, s32[]{:T(128)S(6)} %select_n.78), kind=kOutput, calls=%fused_computation.5 | convolution fusion | flops 1879506944 | bytes 9306116 | tf_op jit(solution)/shard_map/dot_general | solution.py:572
  163.2 3.2 %collective-permute-done.13.refs_1_ = bf16[512,256]{1,0:T(8,128)(2,1)S(1)} collective-permute-done((bf16[512,256]{1,0:T(8,128)(2,1)S(1)}, bf16[512,256]{1,0:T(8,128)(2,1)S(1)}, u32[]{:S(2)}, u32[]{:S(2)}) %collective-permute-start.13) | collective-permute-done | bytes 262176 | tf_op jit(solution)/shard_map/ppermute | solution.py:101
  166.4 2.8 %collective-permute-start.24 = (f32[8,128]{1,0:T(8,128)S(1)}, f32[8,128]{1,0:T(8,128)S(1)}, u32[]{:S(2)}, u32[]{:S(2)}) collective-permute-start(f32[8,128]{1,0:T(8,128)S(1)} %shard_map.132), channel_id=1, source_target_pairs={{0,32},{1,33},{2,34},{3,35},{4,36},{5,37},{6,38},{7,39},{8,40},{9,... | collective-permute-start | bytes 12296 | tf_op jit(solution)/shard_map/ppermute | solution.py:101
  170.5 8.0 %collective-permute-start.25 = (f32[8,128]{1,0:T(8,128)S(1)}, f32[8,128]{1,0:T(8,128)S(1)}, u32[]{:S(2)}, u32[]{:S(2)}) collective-permute-start(f32[8,128]{1,0:T(8,128)S(1)} %max.6), channel_id=1, source_target_pairs={{0,64},{1,65},{2,66},{3,67},{4,68},{5,69},{6,70},{7,71},{8,72},{9,... | collective-permute-start | bytes 12296 | tf_op jit(solution)/shard_map/ppermute | solution.py:101
  178.6 8.6 %collective-permute-start.14 = (bf16[512,256]{1,0:T(8,128)(2,1)}, bf16[512,256]{1,0:T(8,128)(2,1)S(1)}, u32[]{:S(2)}, u32[]{:S(2)}) collective-permute-start(bf16[512,256]{1,0:T(8,128)(2,1)} %get-tuple-element.41), channel_id=1, source_target_pairs={{3,0},{7,1},{35,2},{39,3},{67,4},{71,5},{99,6},{103,7},{9,8},{13,9... | collective-permute-start | bytes 786440 | tf_op jit(solution)/shard_map/ppermute | solution.py:101
  189.1 4.6 %collective-permute-start.16 = (bf16[512,256]{1,0:T(8,128)(2,1)S(1)}, bf16[512,256]{1,0:T(8,128)(2,1)S(1)}, u32[]{:S(2)}, u32[]{:S(2)}) collective-permute-start(bf16[512,256]{1,0:T(8,128)(2,1)S(1)} %get-tuple-element.43), channel_id=1, source_target_pairs={{1,0},{5,1},{33,2},{37,3},{65,4},{69,5},{97,6},{101,7},{0,8},{16,9... | collective-permute-start | bytes 786440 | tf_op jit(solution)/shard_map/ppermute | solution.py:101
  194.7 5.5 %convolution_convert_fusion.4.refs_0_ = bf16[1792,256]{1,0:T(8,128)(2,1)S(1)} fusion(bf16[2048,1792]{1,0:T(8,128)(2,1)} %copy-done.6, bf16[2048,1024]{1,0:T(8,128)(2,1)} %copy-done.25, s32[]{:T(128)S(6)} %select_n.72), kind=kOutput, calls=%fused_computation.8 | convolution fusion | flops 1879506944 | bytes 9306116 | tf_op jit(solution)/shard_map/dot_general | solution.py:572
  200.3 3.6 %shard_map.131 = (bf16[1792,256]{1,0:T(8,128)(2,1)}, f32[8,128]{1,0:T(8,128)}) custom-call(bf16[1792,256]{1,0:T(8,128)(2,1)S(1)} %convolution_convert_fusion.4.refs_0_, bf16[1792,256]{1,0:T(8,128)(2,1)S(1)} %collective-permute-done.21.refs_1_, bf16[1792,256]{1,0:T(8,128)(2,1)S(1)} %copy-done.17, bf16[1792,256]{1,0:T(8,128)(2,1)} %collective-permute-done.23.refs_3_), custom_call_target="tpu_custom_call" | custom-call | tf_op jit(solution)/shard_map/pallas_call | solution.py:117
  (122 shorter events, 61.4 us)
Async XLA Ops:
  7.2 100.4 %all-gather.2.cloned.1.call-start = ((), (), s32[]{:S(2)}) async-start(), calls=%async_computation.1 | async-start | bytes 9175040 | tf_op jit(solution)/shard_map/all_gather | solution.py:598
  18.3 15.9 %collective-permute-start.1 = (bf16[528,256]{1,0:T(8,128)(2,1)S(1)}, bf16[528,256]{1,0:T(8,128)(2,1)S(1)}, u32[]{:S(2)}, u32[]{:S(2)}) collective-permute-start(bf16[528,256]{1,0:T(8,128)(2,1)S(1)} %get-tuple-element.33), channel_id=1, source_target_pairs={{0,8},{1,24},{2,10},{3,26},{4,12},{5,28},{6,14},{7,30},{8,11},{9,1... | collective-permute-start | bytes 811016 | tf_op jit(solution)/shard_map/ppermute | solution.py:101
  22.4 28.5 %collective-permute-start.2 = (bf16[528,256]{1,0:T(8,128)(2,1)S(1)}, bf16[528,256]{1,0:T(8,128)(2,1)S(1)}, u32[]{:S(2)}, u32[]{:S(2)}) collective-permute-start(bf16[528,256]{1,0:T(8,128)(2,1)S(1)} %get-tuple-element.34), channel_id=1, source_target_pairs={{0,3},{1,7},{2,35},{3,39},{4,67},{5,71},{6,99},{7,103},{8,9},{9,13... | collective-permute-start | bytes 811016 | tf_op jit(solution)/shard_map/ppermute | solution.py:101
  24.4 26.6 %collective-permute-start.3 = (bf16[528,256]{1,0:T(8,128)(2,1)S(1)}, bf16[528,256]{1,0:T(8,128)(2,1)S(1)}, u32[]{:S(2)}, u32[]{:S(2)}) collective-permute-start(bf16[528,256]{1,0:T(8,128)(2,1)S(1)} %get-tuple-element.35), channel_id=1, source_target_pairs={{0,0},{1,16},{2,2},{3,18},{4,4},{5,20},{6,6},{7,22},{8,8},{9,24},{... | collective-permute-start | bytes 811016 | tf_op jit(solution)/shard_map/ppermute | solution.py:101
  31.4 19.6 %collective-permute-start.4 = (bf16[528,256]{1,0:T(8,128)(2,1)S(1)}, bf16[528,256]{1,0:T(8,128)(2,1)S(1)}, u32[]{:S(2)}, u32[]{:S(2)}) collective-permute-start(bf16[528,256]{1,0:T(8,128)(2,1)S(1)} %get-tuple-element.36), channel_id=1, source_target_pairs={{0,1},{1,5},{2,33},{3,37},{4,65},{5,69},{6,97},{7,101},{8,0},{9,16... | collective-permute-start | bytes 811016 | tf_op jit(solution)/shard_map/ppermute | solution.py:101
  53.0 153.3 %reduce-scatter.2.cloned.1.call-start = ((), (), s32[]{:S(2)}) async-start(), calls=%async_computation.2 | async-start | bytes 9175040 | tf_op jit(solution)/shard_map/reduce_scatter | solution.py:610
  53.0 24.6 %collective-permute-start.17 = (bf16[2064,256]{1,0:T(8,128)(2,1)S(1)}, bf16[2064,256]{1,0:T(8,128)(2,1)S(1)}, u32[]{:S(2)}, u32[]{:S(2)}) collective-permute-start(bf16[2064,256]{1,0:T(8,128)(2,1)S(1)} %shard_map.121.refs_1_.refs_2_.refs_0_.refs_5_), channel_id=1, source_target_pairs={{0,6},{1,7},{2,0},{3,1},{4,2},{5,3},{6,4},{7,5},{8,14},{9,15},{10,... | collective-permute-start | bytes 3170312 | tf_op jit(solution)/shard_map/ppermute | solution.py:101
  53.1 25.5 %collective-permute-start.18 = (bf16[2064,256]{1,0:T(8,128)(2,1)S(1)}, bf16[2064,256]{1,0:T(8,128)(2,1)S(1)}, u32[]{:S(2)}, u32[]{:S(2)}) collective-permute-start(bf16[2064,256]{1,0:T(8,128)(2,1)S(1)} %shard_map.121.refs_1_.refs_2_.refs_0_.refs_5_), channel_id=1, source_target_pairs={{0,2},{1,3},{2,4},{3,5},{4,6},{5,7},{6,0},{7,1},{8,10},{9,11},{10,... | collective-permute-start | bytes 3170312 | tf_op jit(solution)/shard_map/ppermute | solution.py:101
  54.6 24.9 %collective-permute-start.6 = (bf16[1792,256]{1,0:T(8,128)(2,1)}, bf16[1792,256]{1,0:T(8,128)(2,1)S(1)}, u32[]{:S(2)}, u32[]{:S(2)}) collective-permute-start(bf16[1792,256]{1,0:T(8,128)(2,1)} %copy-done.14), channel_id=1, source_target_pairs={{0,32},{1,9},{2,34},{3,11},{4,36},{5,13},{6,38},{7,15},{8,40},{9,1... | collective-permute-start | bytes 2752520 | tf_op jit(solution)/shard_map/ppermute | solution.py:101
  59.2 22.1 %collective-permute-start.5 = (bf16[1792,256]{1,0:T(8,128)(2,1)}, bf16[1792,256]{1,0:T(8,128)(2,1)S(1)}, u32[]{:S(2)}, u32[]{:S(2)}) collective-permute-start(bf16[1792,256]{1,0:T(8,128)(2,1)} %copy-done.14), channel_id=1, source_target_pairs={{0,96},{1,25},{2,98},{3,27},{4,100},{5,29},{6,102},{7,31},{8,104},... | collective-permute-start | bytes 2752520 | tf_op jit(solution)/shard_map/ppermute | solution.py:101
  77.7 17.0 %collective-permute-start.20 = (bf16[1040,256]{1,0:T(8,128)(2,1)S(1)}, bf16[1040,256]{1,0:T(8,128)(2,1)S(1)}, u32[]{:S(2)}, u32[]{:S(2)}) collective-permute-start(bf16[1040,256]{1,0:T(8,128)(2,1)S(1)} %slice.29), channel_id=1, source_target_pairs={{0,6},{1,7},{2,0},{3,1},{4,2},{5,3},{6,4},{7,5},{8,14},{9,15},{10,... | collective-permute-start | bytes 1597448 | tf_op jit(solution)/shard_map/ppermute | solution.py:101
  78.7 16.0 %collective-permute-start.19 = (bf16[1024,256]{1,0:T(8,128)(2,1)S(1)}, bf16[1024,256]{1,0:T(8,128)(2,1)S(1)}, u32[]{:S(2)}, u32[]{:S(2)}) collective-permute-start(bf16[1024,256]{1,0:T(8,128)(2,1)S(1)} %slice.28), channel_id=1, source_target_pairs={{0,2},{1,3},{2,4},{3,5},{4,6},{5,7},{6,0},{7,1},{8,10},{9,11},{10,... | collective-permute-start | bytes 1572872 | tf_op jit(solution)/shard_map/ppermute | solution.py:101
  79.5 12.7 %collective-permute-start.7 = (bf16[896,256]{1,0:T(8,128)(2,1)S(1)}, bf16[896,256]{1,0:T(8,128)(2,1)S(1)}, u32[]{:S(2)}, u32[]{:S(2)}) collective-permute-start(bf16[896,256]{1,0:T(8,128)(2,1)S(1)} %slice.24), channel_id=1, source_target_pairs={{0,32},{1,9},{2,34},{3,11},{4,36},{5,13},{6,38},{7,15},{8,40},{9,1... | collective-permute-start | bytes 1376264 | tf_op jit(solution)/shard_map/ppermute | solution.py:101
  111.2 14.6 %collective-permute-start.9 = (bf16[1024,256]{1,0:T(8,128)(2,1)S(1)}, bf16[1024,256]{1,0:T(8,128)(2,1)S(1)}, u32[]{:S(2)}, u32[]{:S(2)}) collective-permute-start(bf16[1024,256]{1,0:T(8,128)(2,1)S(1)} %fusion.4), channel_id=1, source_target_pairs={{0,2},{1,3},{2,4},{3,5},{4,6},{5,7},{6,0},{7,1},{8,10},{9,11},{10,... | collective-permute-start | bytes 1572872 | tf_op jit(solution)/shard_map/ppermute | solution.py:101
  114.5 13.6 %collective-permute-start.10 = (bf16[1024,256]{1,0:T(8,128)(2,1)S(1)}, bf16[1024,256]{1,0:T(8,128)(2,1)S(1)}, u32[]{:S(2)}, u32[]{:S(2)}) collective-permute-start(bf16[1024,256]{1,0:T(8,128)(2,1)S(1)} %fusion.7), channel_id=1, source_target_pairs={{0,6},{1,7},{2,0},{3,1},{4,2},{5,3},{6,4},{7,5},{8,14},{9,15},{10,... | collective-permute-start | bytes 1572872 | tf_op jit(solution)/shard_map/ppermute | solution.py:101
  128.4 23.9 %collective-permute-start.12 = (bf16[2048,256]{1,0:T(8,128)(2,1)S(1)}, bf16[2048,256]{1,0:T(8,128)(2,1)S(1)}, u32[]{:S(2)}, u32[]{:S(2)}) collective-permute-start(bf16[2048,256]{1,0:T(8,128)(2,1)S(1)} %get-tuple-element.39), channel_id=1, source_target_pairs={{0,6},{1,7},{2,0},{3,1},{4,2},{5,3},{6,4},{7,5},{8,14},{9,15},{10,... | collective-permute-start | bytes 3145736 | tf_op jit(solution)/shard_map/ppermute | solution.py:101
  130.8 24.0 %collective-permute-start.11 = (bf16[2048,256]{1,0:T(8,128)(2,1)S(1)}, bf16[2048,256]{1,0:T(8,128)(2,1)S(1)}, u32[]{:S(2)}, u32[]{:S(2)}) collective-permute-start(bf16[2048,256]{1,0:T(8,128)(2,1)S(1)} %get-tuple-element.38.refs_2_), channel_id=1, source_target_pairs={{0,2},{1,3},{2,4},{3,5},{4,6},{5,7},{6,0},{7,1},{8,10},{9,11},{10,... | collective-permute-start | bytes 3145736 | tf_op jit(solution)/shard_map/ppermute | solution.py:101
  136.3 52.8 %collective-permute-start.21 = (bf16[1792,256]{1,0:T(8,128)(2,1)}, bf16[1792,256]{1,0:T(8,128)(2,1)S(1)}, u32[]{:S(2)}, u32[]{:S(2)}) collective-permute-start(bf16[1792,256]{1,0:T(8,128)(2,1)} %convolution_convert_fusion.3), channel_id=1, source_target_pairs={{0,32},{1,9},{2,34},{3,11},{4,36},{5,13},{6,38},{7,15},{8,40},{9,1... | collective-permute-start | bytes 2752520 | tf_op jit(solution)/shard_map/ppermute | solution.py:101
  139.4 54.4 %collective-permute-start.22 = (bf16[1792,256]{1,0:T(8,128)(2,1)}, bf16[1792,256]{1,0:T(8,128)(2,1)S(1)}, u32[]{:S(2)}, u32[]{:S(2)}) collective-permute-start(bf16[1792,256]{1,0:T(8,128)(2,1)} %convolution_convert_fusion.2), channel_id=1, source_target_pairs={{0,64},{1,17},{2,66},{3,19},{4,68},{5,21},{6,70},{7,23},{8,72},{9,... | collective-permute-start | bytes 2752520 | tf_op jit(solution)/shard_map/ppermute | solution.py:101
  161.4 38.9 %collective-permute-start.23 = (bf16[1792,256]{1,0:T(8,128)(2,1)}, bf16[1792,256]{1,0:T(8,128)(2,1)}, u32[]{:S(2)}, u32[]{:S(2)}) collective-permute-start(bf16[1792,256]{1,0:T(8,128)(2,1)} %convolution_convert_fusion.1), channel_id=1, source_target_pairs={{0,96},{1,25},{2,98},{3,27},{4,100},{5,29},{6,102},{7,31},{8,104},... | collective-permute-start | bytes 2752520 | tf_op jit(solution)/shard_map/ppermute | solution.py:101
  170.5 16.6 %collective-permute-start.25 = (f32[8,128]{1,0:T(8,128)S(1)}, f32[8,128]{1,0:T(8,128)S(1)}, u32[]{:S(2)}, u32[]{:S(2)}) collective-permute-start(f32[8,128]{1,0:T(8,128)S(1)} %max.6), channel_id=1, source_target_pairs={{0,64},{1,65},{2,66},{3,67},{4,68},{5,69},{6,70},{7,71},{8,72},{9,... | collective-permute-start | bytes 12296 | tf_op jit(solution)/shard_map/ppermute | solution.py:101
  178.6 25.3 %collective-permute-start.14 = (bf16[512,256]{1,0:T(8,128)(2,1)}, bf16[512,256]{1,0:T(8,128)(2,1)S(1)}, u32[]{:S(2)}, u32[]{:S(2)}) collective-permute-start(bf16[512,256]{1,0:T(8,128)(2,1)} %get-tuple-element.41), channel_id=1, source_target_pairs={{3,0},{7,1},{35,2},{39,3},{67,4},{71,5},{99,6},{103,7},{9,8},{13,9... | collective-permute-start | bytes 786440 | tf_op jit(solution)/shard_map/ppermute | solution.py:101
  187.2 16.8 %collective-permute-start.15 = (bf16[512,256]{1,0:T(8,128)(2,1)S(1)}, bf16[512,256]{1,0:T(8,128)(2,1)S(1)}, u32[]{:S(2)}, u32[]{:S(2)}) collective-permute-start(bf16[512,256]{1,0:T(8,128)(2,1)S(1)} %get-tuple-element.42), channel_id=1, source_target_pairs={{0,0},{16,1},{2,2},{18,3},{4,4},{20,5},{6,6},{22,7},{8,8},{24,9},{... | collective-permute-start | bytes 786440 | tf_op jit(solution)/shard_map/ppermute | solution.py:101
  189.1 14.8 %collective-permute-start.16 = (bf16[512,256]{1,0:T(8,128)(2,1)S(1)}, bf16[512,256]{1,0:T(8,128)(2,1)S(1)}, u32[]{:S(2)}, u32[]{:S(2)}) collective-permute-start(bf16[512,256]{1,0:T(8,128)(2,1)S(1)} %get-tuple-element.43), channel_id=1, source_target_pairs={{1,0},{5,1},{33,2},{37,3},{65,4},{69,5},{97,6},{101,7},{0,8},{16,9... | collective-permute-start | bytes 786440 | tf_op jit(solution)/shard_map/ppermute | solution.py:101
  (32 other events, 243.3 us)
Sparse Core Ops, SparseCore 0:
  53.1 49.9 all-gather.1
  107.6 53.4 reduce-scatter.1

commit v3 on v2

--- a/solution.py
+++ b/solution.py
@@ -300,24 +300,40 @@
     )
 
 
-def place_kernel(table, in0, in1, in2, in3, out):
+def place_kernel(table, in0, in1, in2, in3, out, peaks):
     me, _, _ = here()
     rows = in0.shape[0] - NOTE
     for number, block in enumerate((in0, in1, in2, in3)):
         start = pl.multiple_of(table[4 + number, me] * rows, rows)
         out[pl.ds(start, rows), :] = block[:rows, :]
-    peaks = peaks_in([block[rows:, :] for block in (in0, in1, in2, in3)])
-    out[4 * rows :, :] = note_of(peaks, out.shape[1])
+    peaks[...] = peaks_in([block[rows:, :] for block in (in0, in1, in2, in3)])
 
 
 def place(blocks):
     rows, features = blocks[0].shape
     return call(
         place_kernel,
-        shape(4 * (rows - NOTE) + NOTE, features),
+        (shape(4 * (rows - NOTE), features), shape(8, 128, dtype=F32)),
         (0, 0),
         [SCALARS] + [IN_VMEM] * 4,
         (jnp.asarray(TABLE), *blocks),
+        out_specs=[IN_VMEM] * 2,
+    )
+
+
+def stamp_kernel(weight, peaks, out):
+    rows = weight.shape[0]
+    out[:rows, :] = weight[...]
+    out[rows:, :] = note_of(peaks[...], weight.shape[1])
+
+
+def stamp(weight, peaks):
+    return call(
+        stamp_kernel,
+        shape(weight.shape[0] + NOTE, weight.shape[1]),
+        (0, 0),
+        [IN_VMEM] * 2,
+        (weight, peaks),
         out_specs=IN_VMEM,
     )
 
@@ -357,7 +373,7 @@
     return [first, second]
 
 
-def weight_tile_kernel(own, after, top, bottom, before, out):
+def weight_tile_kernel(own, after, top, bottom, before, note0, note1, note2, note3, out, peaks):
     place = here()[1]
     step = pl.program_id(0)
 
@@ -369,21 +385,24 @@
     def _():
         columns_kernel(place, own, after, bottom, before, out)
 
-
-def weight_tile(*parts):
+    peaks[...] = peaks_in((note0, note1, note2, note3))
+
+
+def weight_tile(own, after, top, bottom, before):
     steps = 4
-    hidden, features = parts[0].shape
+    hidden, features = own.shape[0] - NOTE, own.shape[1]
     dims = (hidden // steps, features)
     block = pl.BlockSpec(dims, lambda i: (i, 0))
     out = shape(hidden, N * features)
+    noted = (own, after, bottom, before)
     return call(
         weight_tile_kernel,
-        out,
-        (0, 0),
-        [block, block, *half_blocks(steps, dims), block],
-        parts,
-        grid=(steps,),
-        out_specs=row_blocks(out, steps),
+        (out, shape(8, 128, dtype=F32)),
+        (0, 0),
+        [block, block, *half_blocks(steps, dims), block] + [note_block(part) for part in noted],
+        (own, after, top, bottom, before, *noted),
+        grid=(steps,),
+        out_specs=[row_blocks(out, steps), fixed(8, 128)],
     )
 
 
@@ -395,7 +414,7 @@
     out_before[rows:, :] = (before[rows:, :].astype(F32) + bottom[...].astype(F32)).astype(BF16)
 
 
-def add_halves(after, before, top, bottom):
+def add_halves(after, before, top, bottom, order):
     whole = shape(*after.shape)
     return call(
         raise_kernel,
@@ -403,11 +422,12 @@
         (0, 0),
         [IN_VMEM] * 4,
         (after, before, top, bottom),
+        order,
         out_specs=[IN_VMEM] * 2,
     )
 
 
-def grad_tile_kernel(own, after, top, bottom, before, note0, note1, note2, note3, out, peaks):
+def grad_tile_kernel(own, after, top, bottom, before, out):
     place = here()[2]
     step = pl.program_id(0)
 
@@ -419,41 +439,22 @@
     def _():
         columns_kernel(place, own, after, bottom, before, out)
 
-    peaks[...] = peaks_in((note0, note1, note2, note3))
-
 
 def grad_tile(own, after, top, bottom, before, order):
     steps = 4
-    rows, features = own.shape[0] - NOTE, own.shape[1]
-    out = shape(rows, N * features)
+    rows, features = own.shape
     dims = (rows // steps, features)
     block = pl.BlockSpec(dims, lambda i: (i, 0))
-    noted = (own, after, bottom, before)
+    out = shape(rows, N * features)
     return call(
         grad_tile_kernel,
-        (out, shape(8, 128, dtype=F32)),
-        (0, 0),
-        [block, block, *half_blocks(steps, dims), block] + [note_block(part) for part in noted],
-        (own, after, top, bottom, before, *noted),
+        out,
+        (0, 0),
+        [block, block, *half_blocks(steps, dims), block],
+        (own, after, top, bottom, before),
         order,
         grid=(steps,),
-        out_specs=[row_blocks(out, steps), fixed(8, 128)],
-    )
-
-
-def later_kernel(value, out):
-    out[...] = value[...]
-
-
-def later(value, after):
-    return call(
-        later_kernel,
-        shape(*value.shape, dtype=value.dtype),
-        (0, 0),
-        [IN_VMEM],
-        (value,),
-        after,
-        out_specs=IN_VMEM,
+        out_specs=row_blocks(out, steps),
     )
 
 
@@ -475,25 +476,42 @@
     )
 
 
-def return_kernel(table, own, before, after, out0, out1, out2, out3):
+def return_kernel(table, own, before, after, peaks, out0, out1, out2, out3):
     me, _, _ = here()
-    tokens = out0.shape[0]
+    tokens = out0.shape[0] - NOTE
+    note = note_of(peaks[...], out0.shape[1])
     for number, out in enumerate((out0, out1, out2, out3)):
         rows = pl.ds(pl.multiple_of(table[4 + number, me] * tokens, tokens), tokens)
         total = own[rows, :].astype(F32) + before[rows, :].astype(F32) + after[rows, :].astype(F32)
-        out[...] = total.astype(BF16)
-
-
-def return_blocks(parts, after):
+        out[:tokens, :] = total.astype(BF16)
+        out[tokens:, :] = note
+
+
+def return_blocks(parts, peaks):
     rows, features = parts[0].shape
     return call(
         return_kernel,
-        (shape(rows // N, features),) * 4,
-        (0, 0),
-        [SCALARS] + [IN_VMEM] * 3,
-        (jnp.asarray(TABLE), *parts),
-        after,
+        (shape(rows // N + NOTE, features),) * 4,
+        (0, 0),
+        [SCALARS] + [IN_VMEM] * 4,
+        (jnp.asarray(TABLE), *parts, peaks),
         out_specs=[IN_VMEM] * 4,
+    )
+
+
+def read_kernel(note0, note1, note2, note3, peaks):
+    peaks[...] = peaks_in((note0, note1, note2, note3))
+
+
+def read_notes(blocks):
+    return call(
+        read_kernel,
+        shape(8, 128, dtype=F32),
+        (0, 0),
+        [note_block(block) for block in blocks],
+        blocks,
+        grid=(1,),
+        out_specs=fixed(8, 128),
     )
 
 
@@ -528,24 +546,28 @@
         out[:, half * width : (half + 1) * width] = total.astype(BF16)
 
 
-def merge(blocks):
+def merge(blocks, after):
     steps = 2
-    out = shape(blocks[0].shape[0], 2 * blocks[0].shape[1])
+    tokens, features = blocks[0].shape[0] - NOTE, blocks[0].shape[1]
+    block = pl.BlockSpec((tokens // steps, features), lambda i: (i, 0))
+    out = shape(tokens, 2 * features)
     return call(
         merge_kernel,
         out,
         (0, 0),
-        [SCALARS] + [row_blocks(blocks[0], steps)] * 4,
+        [SCALARS] + [block] * 4,
         (jnp.asarray(TABLE), *blocks),
+        after,
         grid=(steps,),
         out_specs=row_blocks(out, steps),
     )
 
 
-def finish_kernel(slope, silu, grad_act, grad_gate, grad_up):
+def finish_kernel(slope, silu, grad_act, grad_gate, grad_up, token):
     value = grad_act[...].astype(F32)
     grad_gate[...] = (value * slope[...].astype(F32)).astype(BF16)
     grad_up[...] = (value * silu[...].astype(F32)).astype(BF16)
+    token[...] = jnp.zeros(token.shape, F32)
 
 
 def finish(slope, silu, grad_act):
@@ -553,19 +575,13 @@
     rows = row_blocks(slope, steps)
     return call(
         finish_kernel,
-        (shape(*slope.shape),) * 2,
+        (shape(*slope.shape), shape(*slope.shape), shape(8, 128, dtype=F32)),
         (0, 0),
         [rows] * 3,
         (slope, silu, grad_act),
         grid=(steps,),
-        out_specs=[rows] * 2,
-    )
-
-
-def raise_peaks(peaks, bits):
-    for bit in bits:
-        peaks = jnp.maximum(peaks, send(peaks, [(n, n ^ (1 << bit)) for n in range(128)]))
-    return peaks
+        out_specs=[rows, rows, fixed(8, 128)],
+    )
 
 
 def dot(left, right, dims):
@@ -578,61 +594,70 @@
     groups = token_groups()
     swap = [(n, n ^ 1) for n in range(128)]
     weight_q, weight_peak = clip_weight(down_weight, weight_history[None])
-    weight_before, weight_after = send(weight_q, feature_ring(1)), send(weight_q, feature_ring(-1))
-    half = weight_q.shape[0] // 2
-    weight = weight_tile(
-        weight_q,
-        weight_after,
-        send(weight_before[:half], feature_ring(1)),
-        send(weight_after[half:], feature_ring(-1)),
-        weight_before,
-    )
     act_q, peaks = activate(gate_pre, up_pre, weight_peak, act_history[None])
     blocks = share(grad_out, peaks, send(peaks, swap))
     blocks = [
         send(block, [(edge[0], edge[1]) for edge in ROUNDS[number]])
         for number, block in enumerate(blocks)
     ]
-    grad = place(blocks)
+    grad, peaks = place(blocks)
+    weight = stamp(weight_q, peaks)
+    before, after = send(weight, feature_ring(1)), send(weight, feature_ring(-1))
+    half = weight_q.shape[0] // 2
+    weight, peaks = weight_tile(
+        weight,
+        after,
+        send(before[:half], feature_ring(1)),
+        send(after[half:], feature_ring(-1)),
+        before,
+    )
+    peaks = jnp.maximum(peaks, send(peaks, swap))
     (act_q,) = gate((act_q,), (grad,))
     act = lax.all_gather(act_q, AXES, axis=0, tiled=True, axis_index_groups=groups)
     slope, silu, token = slopes(gate_pre, up_pre, (grad,))
     before, after = send(grad, hidden_ring(1)), send(grad, hidden_ring(-1))
-    half = (grad.shape[0] - NOTE) // 2
-    top, bottom = send(before[:half], hidden_ring(1)), send(after[half:], hidden_ring(-1))
+    half = grad.shape[0] // 2
+    tile = grad_tile(
+        grad,
+        after,
+        send(before[:half], hidden_ring(1)),
+        send(after[half:], hidden_ring(-1)),
+        before,
+        (token,),
+    )
 
     def block_of(array, number):
         size = array.shape[1] // N
         return lax.dynamic_slice_in_dim(array, number % N * size, size, axis=1)
 
-    tile, peaks = grad_tile(grad, after, top, bottom, before, (token,))
     grad_act = dot(tile, weight, ((1,), (1,)))
     grad_act = lax.psum_scatter(
         grad_act, AXES, scatter_dimension=0, tiled=True, axis_index_groups=groups
     )
-    half = act.shape[0] // 2
+    far = block_of(weight, z + 2)
+    top = send(dot(act[:half], far, ((1,), (0,))), hidden_ring(1))
+    bottom = send(dot(act[half:], far, ((1,), (0,))), hidden_ring(-1))
     mixed = [dot(act, block_of(weight, z + step), ((1,), (0,))) for step in (0, 1, 3)]
-    far = block_of(weight, z + 2)
-    mixed_top = send(dot(act[:half], far, ((1,), (0,))), hidden_ring(1))
-    mixed_bottom = send(dot(act[half:], far, ((1,), (0,))), hidden_ring(-1))
-    mixed_after, mixed_before = add_halves(mixed[1], mixed[2], mixed_top, mixed_bottom)
-    (act,) = gate((act,), (mixed[0], mixed_after))
+    (act,) = gate((act,), mixed)
     weight_grad = [
         dot(act, block_of(tile, feature_place + step), ((0,), (0,))) for step in range(N)
     ]
-    weight_grad, _ = add(ring_exchange(weight_grad, feature_ring))
-    mixed = (mixed[0], send(mixed_after, hidden_ring(1)), send(mixed_before, hidden_ring(-1)))
-    blocks = return_blocks(mixed, ())
+    after, before = add_halves(mixed[1], mixed[2], top, bottom, weight_grad)
+    mixed = (mixed[0], send(after, hidden_ring(1)), send(before, hidden_ring(-1)))
+    blocks = list(return_blocks(mixed, peaks))
+    weight_grad, added = add(ring_exchange(weight_grad, feature_ring))
+    grad_gate, grad_up, finished = finish(slope, silu, grad_act)
+    blocks[2:] = gate(blocks[2:], (added, finished))
     blocks = [
         send(block, [(edge[1], edge[0]) for edge in ROUNDS[number]])
         for number, block in enumerate(blocks)
     ]
-    peaks = raise_peaks(later(peaks, blocks[:1]), (5, 6))
-    grad_gate, grad_up = finish(slope, silu, grad_act)
+    mixed = merge(blocks, ())
+    peaks = read_notes(blocks)
     new_weight, new_act = histories(
         peaks, send(peaks, swap), weight_history[None], act_history[None]
     )
-    return (merge(blocks), grad_gate, grad_up, weight_grad, new_weight[0], new_act[0])
+    return (mixed, grad_gate, grad_up, weight_grad, new_weight[0], new_act[0])
 
 
 def solution(mesh):

time: 219 us -> 213 us (0.973)
  starting transfers between devices: 61.8 us -> 55.2 us
  matrix products: 36.9 us -> 31.6 us
  waiting for transfers between devices: 70 us -> 74.9 us
  Pallas kernels: 17.1 us -> 14.9 us
    ppermute x27 -> x26, starting transfers between devices: 61.7 us -> 55.2 us  [send(): return lax.ppermute(value, AXES, pairs)]
    dot_general x10, matrix products: 36.9 us -> 31.6 us  [dot(): lax.dot_general(left, right, (dims, ((), ())), preferred_element_type=F32)]
    ppermute x27 -> x26, waiting for transfers between devices: 69.9 us -> 74.9 us  [send(): return lax.ppermute(value, AXES, pairs)]
    pallas_call x16 -> x18, Pallas kernels: 17.1 us -> 14.9 us  [call(): pl.pallas_call(body, out_shape=out_shape, in_specs=list(in_specs) + [ANYW...]
    unnamed x54 -> x48, local copies, waits for them, and re-layouts: 18 us -> 19.6 us
  transfers between devices with their start and end apart: 29 -> 28, of which waited for: 12 -> 8; matrix products, arithmetic and copies ran while one was open for 17% -> 15% of each run, Pallas kernels for 5% -> 5%
where the time goes in v3:
time: 213 us; the launch traced here: 211 us
  waiting for transfers between devices  74.9 us (35%)
  starting transfers between devices  55.2 us (26%)
  matrix products  31.6 us (15%)
  local copies, waits for them, and re-layouts  19.8 us (9%)
  Pallas kernels  14.9 us (7%)
  between operations  14.6 us (7%)
    ppermute x26, waiting for transfers between devices, send(): return lax.ppermute(value, AXES, pairs)  74.9 us
    ppermute x26, starting transfers between devices, send(): return lax.ppermute(value, AXES, pairs)  55.2 us
    dot_general x10, matrix products, dot(): lax.dot_general(left, right, (dims, ((), ())), preferred_element_type=F32)  31.6 us
    unnamed x48, local copies, waits for them, and re-layouts  19.6 us
    pallas_call x18, Pallas kernels, call(): pl.pallas_call(body, out_shape=out_shape, in_specs=list(in_specs) + [ANYW...  14.9 us
  transfers between devices with their start and end apart: 28, of which 8 were waited for; matrix products, arithmetic and copies ran while one was open for 15% of the time, Pallas kernels for 5%

profile of v3, /device:TPU:15, one launch (start us, length us, event | category | flops | bytes accessed | tf_op | source)
XLA Modules:
  0.0 211.1 jit_solution(570917967020504780)
XLA Ops:
  18.3 4.1 %collective-permute-start.1 = (bf16[528,256]{1,0:T(8,128)(2,1)S(1)}, bf16[528,256]{1,0:T(8,128)(2,1)S(1)}, u32[]{:S(2)}, u32[]{:S(2)}) collective-permute-start(bf16[528,256]{1,0:T(8,128)(2,1)S(1)} %get-tuple-element.39), channel_id=1, source_target_pairs={{0,8},{1,24},{2,10},{3,26},{4,12},{5,28},{6,14},{7,30},{8,11},{9,1... | collective-permute-start | bytes 811016 | tf_op jit(solution)/shard_map/ppermute | solution.py:101
  24.4 7.0 %collective-permute-start.3 = (bf16[528,256]{1,0:T(8,128)(2,1)S(1)}, bf16[528,256]{1,0:T(8,128)(2,1)S(1)}, u32[]{:S(2)}, u32[]{:S(2)}) collective-permute-start(bf16[528,256]{1,0:T(8,128)(2,1)S(1)} %get-tuple-element.41), channel_id=1, source_target_pairs={{0,0},{1,16},{2,2},{3,18},{4,4},{5,20},{6,6},{7,22},{8,8},{9,24},{... | collective-permute-start | bytes 811016 | tf_op jit(solution)/shard_map/ppermute | solution.py:101
  31.4 2.8 %collective-permute-start.4 = (bf16[528,256]{1,0:T(8,128)(2,1)S(1)}, bf16[528,256]{1,0:T(8,128)(2,1)S(1)}, u32[]{:S(2)}, u32[]{:S(2)}) collective-permute-start(bf16[528,256]{1,0:T(8,128)(2,1)S(1)} %get-tuple-element.42), channel_id=1, source_target_pairs={{0,1},{1,5},{2,33},{3,37},{4,65},{5,69},{6,97},{7,101},{8,0},{9,16... | collective-permute-start | bytes 811016 | tf_op jit(solution)/shard_map/ppermute | solution.py:101
  34.2 16.7 %collective-permute-done.2.refs_2_ = bf16[528,256]{1,0:T(8,128)(2,1)S(1)} collective-permute-done((bf16[528,256]{1,0:T(8,128)(2,1)S(1)}, bf16[528,256]{1,0:T(8,128)(2,1)S(1)}, u32[]{:S(2)}, u32[]{:S(2)}) %collective-permute-start.2) | collective-permute-done | bytes 270368 | tf_op jit(solution)/shard_map/ppermute | solution.py:101
  53.1 2.7 %collective-permute-start.11 = (bf16[2048,256]{1,0:T(8,128)(2,1)S(1)}, bf16[2048,256]{1,0:T(8,128)(2,1)S(1)}, u32[]{:S(2)}, u32[]{:S(2)}) collective-permute-start(bf16[2048,256]{1,0:T(8,128)(2,1)S(1)} %get-tuple-element.43.refs_1_.refs_2_.refs_0_), channel_id=1, source_target_pairs={{0,6},{1,7},{2,0},{3,1},{4,2},{5,3},{6,4},{7,5},{8,14},{9,15},{10,... | collective-permute-start | bytes 3145736 | tf_op jit(solution)/shard_map/ppermute | solution.py:101
  57.1 4.7 %collective-permute-start.6 = (bf16[1808,256]{1,0:T(8,128)(2,1)S(1)}, bf16[1808,256]{1,0:T(8,128)(2,1)S(1)}, u32[]{:S(2)}, u32[]{:S(2)}) collective-permute-start(bf16[1808,256]{1,0:T(8,128)(2,1)S(1)} %shard_map.123.refs_0_.refs_5_), channel_id=1, source_target_pairs={{0,32},{1,9},{2,34},{3,11},{4,36},{5,13},{6,38},{7,15},{8,40},{9,1... | collective-permute-start | bytes 2777096 | tf_op jit(solution)/shard_map/ppermute | solution.py:101
  61.8 16.4 %collective-permute-done.12.refs_4_ = bf16[2048,256]{1,0:T(8,128)(2,1)S(1)} collective-permute-done((bf16[2048,256]{1,0:T(8,128)(2,1)S(1)}, bf16[2048,256]{1,0:T(8,128)(2,1)S(1)}, u32[]{:S(2)}, u32[]{:S(2)}) %collective-permute-start.12) | collective-permute-done | bytes 1048608 | tf_op jit(solution)/shard_map/ppermute | solution.py:101
  78.4 2.9 %collective-permute-start.14 = (bf16[1024,256]{1,0:T(8,128)(2,1)S(1)}, bf16[1024,256]{1,0:T(8,128)(2,1)S(1)}, u32[]{:S(2)}, u32[]{:S(2)}) collective-permute-start(bf16[1024,256]{1,0:T(8,128)(2,1)S(1)} %slice.29), channel_id=1, source_target_pairs={{0,6},{1,7},{2,0},{3,1},{4,2},{5,3},{6,4},{7,5},{8,14},{9,15},{10,... | collective-permute-start | bytes 1572872 | tf_op jit(solution)/shard_map/ppermute | solution.py:101
  87.1 8.8 %collective-permute-done.7.refs_2_ = bf16[896,256]{1,0:T(8,128)(2,1)S(1)} collective-permute-done((bf16[896,256]{1,0:T(8,128)(2,1)S(1)}, bf16[896,256]{1,0:T(8,128)(2,1)S(1)}, u32[]{:S(2)}, u32[]{:S(2)}) %collective-permute-start.7) | collective-permute-done | bytes 458784 | tf_op jit(solution)/shard_map/ppermute | solution.py:101
  99.6 9.7 %convolution_convert_fusion = bf16[2048,1792]{1,0:T(8,128)(2,1)} fusion(bf16[2048,1024]{1,0:T(8,128)(2,1)S(1)} %shard_map.127, bf16[1792,1024]{1,0:T(8,128)(2,1)S(1)} %get-tuple-element.46), kind=kOutput, calls=%fused_computation | convolution fusion | flops 7519862784 | bytes 15204352 | tf_op jit(solution)/shard_map/dot_general | solution.py:588
  109.5 3.6 %fusion.7 = bf16[1024,256]{1,0:T(8,128)(2,1)S(1)} fusion(bf16[2048,1792]{1,0:T(8,128)(2,1)} %all-gather.2.cloned.1.call-done.refs_0_, bf16[1792,1024]{1,0:T(8,128)(2,1)} %copy-done.22, s32[]{:T(128)S(6)} %select_n.69), kind=kOutput, calls=%fused_computation.13 | convolution fusion | flops 939786240 | bytes 5111812 | tf_op jit(solution)/shard_map/dot_general | solution.py:588
  114.0 2.4 %fusion.4 = bf16[1024,256]{1,0:T(8,128)(2,1)S(1)} fusion(bf16[2048,1792]{1,0:T(8,128)(2,1)S(1)} %copy-done.5, bf16[1792,1024]{1,0:T(8,128)(2,1)} %copy-done.22, s32[]{:T(128)S(6)} %select_n.69), kind=kOutput, calls=%fused_computation.12 | convolution fusion | flops 939786240 | bytes 5111812 | tf_op jit(solution)/shard_map/dot_general | solution.py:588
  130.6 2.5 %convolution_convert_fusion.3.refs_5_ = bf16[1792,256]{1,0:T(8,128)(2,1)S(1)} fusion(bf16[2048,1792]{1,0:T(8,128)(2,1)S(1)} %shard_map.125, bf16[2048,1024]{1,0:T(8,128)(2,1)S(1)} %copy-done.7, s32[]{:T(128)S(6)} %select_n.74), kind=kOutput, calls=%fused_computation.7 | convolution fusion | flops 1879506944 | bytes 9306116 | tf_op jit(solution)/shard_map/dot_general | solution.py:588
  133.1 2.3 %convolution_convert_fusion.4.refs_4_.refs_0_ = bf16[1792,256]{1,0:T(8,128)(2,1)S(1)} fusion(bf16[2048,1792]{1,0:T(8,128)(2,1)S(1)} %shard_map.125, bf16[2048,1024]{1,0:T(8,128)(2,1)S(1)} %copy-done.7, s32[]{:T(128)S(6)} %select_n.72), kind=kOutput, calls=%fused_computation.8 | convolution fusion | flops 1879506944 | bytes 9306116 | tf_op jit(solution)/shard_map/dot_general | solution.py:588
  135.8 2.6 %collective-permute-start.16 = (bf16[2048,256]{1,0:T(8,128)(2,1)S(1)}, bf16[2048,256]{1,0:T(8,128)(2,1)S(1)}, u32[]{:S(2)}, u32[]{:S(2)}) collective-permute-start(bf16[2048,256]{1,0:T(8,128)(2,1)S(1)} %get-tuple-element.49), channel_id=1, source_target_pairs={{0,6},{1,7},{2,0},{3,1},{4,2},{5,3},{6,4},{7,5},{8,14},{9,15},{10,... | collective-permute-start | bytes 3145736 | tf_op jit(solution)/shard_map/ppermute | solution.py:101
  145.3 14.4 %collective-permute-done.22.refs_3_ = bf16[1792,256]{1,0:T(8,128)(2,1)S(1)} collective-permute-done((bf16[1792,256]{1,0:T(8,128)(2,1)S(1)}, bf16[1792,256]{1,0:T(8,128)(2,1)S(1)}, u32[]{:S(2)}, u32[]{:S(2)}) %collective-permute-start.22) | collective-permute-done | bytes 917536 | tf_op jit(solution)/shard_map/ppermute | solution.py:101
  159.6 10.2 %collective-permute-done.21.refs_2_ = bf16[1792,256]{1,0:T(8,128)(2,1)S(1)} collective-permute-done((bf16[1792,256]{1,0:T(8,128)(2,1)S(1)}, bf16[1792,256]{1,0:T(8,128)(2,1)S(1)}, u32[]{:S(2)}, u32[]{:S(2)}) %collective-permute-start.21) | collective-permute-done | bytes 917536 | tf_op jit(solution)/shard_map/ppermute | solution.py:101
  172.8 3.5 %collective-permute-start.18 = (bf16[528,256]{1,0:T(8,128)(2,1)S(1)}, bf16[528,256]{1,0:T(8,128)(2,1)S(1)}, u32[]{:S(2)}, u32[]{:S(2)}) collective-permute-start(bf16[528,256]{1,0:T(8,128)(2,1)S(1)} %get-tuple-element.51), channel_id=1, source_target_pairs={{8,0},{24,1},{10,2},{26,3},{12,4},{28,5},{14,6},{30,7},{11,8},{15,... | collective-permute-start | bytes 811016 | tf_op jit(solution)/shard_map/ppermute | solution.py:101
  176.3 4.3 %collective-permute-start.19 = (bf16[528,256]{1,0:T(8,128)(2,1)S(1)}, bf16[528,256]{1,0:T(8,128)(2,1)S(1)}, u32[]{:S(2)}, u32[]{:S(2)}) collective-permute-start(bf16[528,256]{1,0:T(8,128)(2,1)S(1)} %get-tuple-element.52), channel_id=1, source_target_pairs={{3,0},{7,1},{35,2},{39,3},{67,4},{71,5},{99,6},{103,7},{9,8},{13,9... | collective-permute-start | bytes 811016 | tf_op jit(solution)/shard_map/ppermute | solution.py:101
  183.6 2.4 %shard_map.131 = (bf16[512,1792]{1,0:T(8,128)(2,1)}, bf16[512,1792]{1,0:T(8,128)(2,1)}, f32[8,128]{1,0:T(8,128)S(1)}) custom-call(bf16[512,1792]{1,0:T(8,128)(2,1)S(1)} %copy-done.9, bf16[512,1792]{1,0:T(8,128)(2,1)S(1)} %copy-done.11, bf16[512,1792]{1,0:T(8,128)(2,1)S(1)} %copy-done.12), custom_call_target="tpu_custom_call" | custom-call | tf_op jit(solution)/shard_map/pallas_call | solution.py:117
  186.0 3.4 %collective-permute-start.23 = (bf16[528,256]{1,0:T(8,128)(2,1)S(1)}, bf16[528,256]{1,0:T(8,128)(2,1)S(1)}, u32[]{:S(2)}, u32[]{:S(2)}) collective-permute-start(bf16[528,256]{1,0:T(8,128)(2,1)S(1)} %get-tuple-element.59), channel_id=1, source_target_pairs={{0,0},{16,1},{2,2},{18,3},{4,4},{20,5},{6,6},{22,7},{8,8},{24,9},{... | collective-permute-start | bytes 811016 | tf_op jit(solution)/shard_map/ppermute | solution.py:101
  189.4 4.7 %collective-permute-start.24 = (bf16[528,256]{1,0:T(8,128)(2,1)S(1)}, bf16[528,256]{1,0:T(8,128)(2,1)S(1)}, u32[]{:S(2)}, u32[]{:S(2)}) collective-permute-start(bf16[528,256]{1,0:T(8,128)(2,1)S(1)} %get-tuple-element.60), channel_id=1, source_target_pairs={{1,0},{5,1},{33,2},{37,3},{65,4},{69,5},{97,6},{101,7},{0,8},{16,9... | collective-permute-start | bytes 811016 | tf_op jit(solution)/shard_map/ppermute | solution.py:101
  194.2 5.2 %collective-permute-done.23.refs_3_.refs_2_ = bf16[528,256]{1,0:T(8,128)(2,1)S(1)} collective-permute-done((bf16[528,256]{1,0:T(8,128)(2,1)S(1)}, bf16[528,256]{1,0:T(8,128)(2,1)S(1)}, u32[]{:S(2)}, u32[]{:S(2)}) %collective-permute-start.23) | collective-permute-done | bytes 270368 | tf_op jit(solution)/shard_map/ppermute | solution.py:101
  199.4 2.4 %collective-permute-done.24.refs_4_.refs_3_ = bf16[528,256]{1,0:T(8,128)(2,1)S(1)} collective-permute-done((bf16[528,256]{1,0:T(8,128)(2,1)S(1)}, bf16[528,256]{1,0:T(8,128)(2,1)S(1)}, u32[]{:S(2)}, u32[]{:S(2)}) %collective-permute-start.24) | collective-permute-done | bytes 270368 | tf_op jit(solution)/shard_map/ppermute | solution.py:101
  (115 shorter events, 57.0 us)
Async XLA Ops:
  7.2 102.3 %all-gather.2.cloned.1.call-start = ((), (), s32[]{:S(2)}) async-start(), calls=%async_computation.1 | async-start | bytes 9175040 | tf_op jit(solution)/shard_map/all_gather | solution.py:616
  18.3 15.9 %collective-permute-start.1 = (bf16[528,256]{1,0:T(8,128)(2,1)S(1)}, bf16[528,256]{1,0:T(8,128)(2,1)S(1)}, u32[]{:S(2)}, u32[]{:S(2)}) collective-permute-start(bf16[528,256]{1,0:T(8,128)(2,1)S(1)} %get-tuple-element.39), channel_id=1, source_target_pairs={{0,8},{1,24},{2,10},{3,26},{4,12},{5,28},{6,14},{7,30},{8,11},{9,1... | collective-permute-start | bytes 811016 | tf_op jit(solution)/shard_map/ppermute | solution.py:101
  22.4 28.5 %collective-permute-start.2 = (bf16[528,256]{1,0:T(8,128)(2,1)S(1)}, bf16[528,256]{1,0:T(8,128)(2,1)S(1)}, u32[]{:S(2)}, u32[]{:S(2)}) collective-permute-start(bf16[528,256]{1,0:T(8,128)(2,1)S(1)} %get-tuple-element.40), channel_id=1, source_target_pairs={{0,3},{1,7},{2,35},{3,39},{4,67},{5,71},{6,99},{7,103},{8,9},{9,13... | collective-permute-start | bytes 811016 | tf_op jit(solution)/shard_map/ppermute | solution.py:101
  24.4 26.6 %collective-permute-start.3 = (bf16[528,256]{1,0:T(8,128)(2,1)S(1)}, bf16[528,256]{1,0:T(8,128)(2,1)S(1)}, u32[]{:S(2)}, u32[]{:S(2)}) collective-permute-start(bf16[528,256]{1,0:T(8,128)(2,1)S(1)} %get-tuple-element.41), channel_id=1, source_target_pairs={{0,0},{1,16},{2,2},{3,18},{4,4},{5,20},{6,6},{7,22},{8,8},{9,24},{... | collective-permute-start | bytes 811016 | tf_op jit(solution)/shard_map/ppermute | solution.py:101
  31.4 19.6 %collective-permute-start.4 = (bf16[528,256]{1,0:T(8,128)(2,1)S(1)}, bf16[528,256]{1,0:T(8,128)(2,1)S(1)}, u32[]{:S(2)}, u32[]{:S(2)}) collective-permute-start(bf16[528,256]{1,0:T(8,128)(2,1)S(1)} %get-tuple-element.42), channel_id=1, source_target_pairs={{0,1},{1,5},{2,33},{3,37},{4,65},{5,69},{6,97},{7,101},{8,0},{9,16... | collective-permute-start | bytes 811016 | tf_op jit(solution)/shard_map/ppermute | solution.py:101
  52.9 127.7 %reduce-scatter.2.cloned.1.call-start = ((), (), s32[]{:S(2)}) async-start(), calls=%async_computation.2 | async-start | bytes 9175040 | tf_op jit(solution)/shard_map/reduce_scatter | solution.py:634
  53.0 25.2 %collective-permute-start.12 = (bf16[2048,256]{1,0:T(8,128)(2,1)S(1)}, bf16[2048,256]{1,0:T(8,128)(2,1)S(1)}, u32[]{:S(2)}, u32[]{:S(2)}) collective-permute-start(bf16[2048,256]{1,0:T(8,128)(2,1)S(1)} %get-tuple-element.43.refs_1_.refs_2_.refs_0_), channel_id=1, source_target_pairs={{0,2},{1,3},{2,4},{3,5},{4,6},{5,7},{6,0},{7,1},{8,10},{9,11},{10,... | collective-permute-start | bytes 3145736 | tf_op jit(solution)/shard_map/ppermute | solution.py:101
  53.1 25.2 %collective-permute-start.11 = (bf16[2048,256]{1,0:T(8,128)(2,1)S(1)}, bf16[2048,256]{1,0:T(8,128)(2,1)S(1)}, u32[]{:S(2)}, u32[]{:S(2)}) collective-permute-start(bf16[2048,256]{1,0:T(8,128)(2,1)S(1)} %get-tuple-element.43.refs_1_.refs_2_.refs_0_), channel_id=1, source_target_pairs={{0,6},{1,7},{2,0},{3,1},{4,2},{5,3},{6,4},{7,5},{8,14},{9,15},{10,... | collective-permute-start | bytes 3145736 | tf_op jit(solution)/shard_map/ppermute | solution.py:101
  57.0 24.2 %collective-permute-start.5 = (bf16[1808,256]{1,0:T(8,128)(2,1)S(1)}, bf16[1808,256]{1,0:T(8,128)(2,1)S(1)}, u32[]{:S(2)}, u32[]{:S(2)}) collective-permute-start(bf16[1808,256]{1,0:T(8,128)(2,1)S(1)} %shard_map.123.refs_0_.refs_5_), channel_id=1, source_target_pairs={{0,96},{1,25},{2,98},{3,27},{4,100},{5,29},{6,102},{7,31},{8,104},... | collective-permute-start | bytes 2777096 | tf_op jit(solution)/shard_map/ppermute | solution.py:101
  57.1 24.3 %collective-permute-start.6 = (bf16[1808,256]{1,0:T(8,128)(2,1)S(1)}, bf16[1808,256]{1,0:T(8,128)(2,1)S(1)}, u32[]{:S(2)}, u32[]{:S(2)}) collective-permute-start(bf16[1808,256]{1,0:T(8,128)(2,1)S(1)} %shard_map.123.refs_0_.refs_5_), channel_id=1, source_target_pairs={{0,32},{1,9},{2,34},{3,11},{4,36},{5,13},{6,38},{7,15},{8,40},{9,1... | collective-permute-start | bytes 2777096 | tf_op jit(solution)/shard_map/ppermute | solution.py:101
  78.2 18.3 %collective-permute-start.13 = (bf16[1024,256]{1,0:T(8,128)(2,1)S(1)}, bf16[1024,256]{1,0:T(8,128)(2,1)S(1)}, u32[]{:S(2)}, u32[]{:S(2)}) collective-permute-start(bf16[1024,256]{1,0:T(8,128)(2,1)S(1)} %slice.28), channel_id=1, source_target_pairs={{0,2},{1,3},{2,4},{3,5},{4,6},{5,7},{6,0},{7,1},{8,10},{9,11},{10,... | collective-permute-start | bytes 1572872 | tf_op jit(solution)/shard_map/ppermute | solution.py:101
  78.4 18.2 %collective-permute-start.14 = (bf16[1024,256]{1,0:T(8,128)(2,1)S(1)}, bf16[1024,256]{1,0:T(8,128)(2,1)S(1)}, u32[]{:S(2)}, u32[]{:S(2)}) collective-permute-start(bf16[1024,256]{1,0:T(8,128)(2,1)S(1)} %slice.29), channel_id=1, source_target_pairs={{0,6},{1,7},{2,0},{3,1},{4,2},{5,3},{6,4},{7,5},{8,14},{9,15},{10,... | collective-permute-start | bytes 1572872 | tf_op jit(solution)/shard_map/ppermute | solution.py:101
  81.3 14.6 %collective-permute-start.8 = (bf16[912,256]{1,0:T(8,128)(2,1)S(1)}, bf16[912,256]{1,0:T(8,128)(2,1)S(1)}, u32[]{:S(2)}, u32[]{:S(2)}) collective-permute-start(bf16[912,256]{1,0:T(8,128)(2,1)S(1)} %slice.25), channel_id=1, source_target_pairs={{0,96},{1,25},{2,98},{3,27},{4,100},{5,29},{6,102},{7,31},{8,104},... | collective-permute-start | bytes 1400840 | tf_op jit(solution)/shard_map/ppermute | solution.py:101
  81.4 14.4 %collective-permute-start.7 = (bf16[896,256]{1,0:T(8,128)(2,1)S(1)}, bf16[896,256]{1,0:T(8,128)(2,1)S(1)}, u32[]{:S(2)}, u32[]{:S(2)}) collective-permute-start(bf16[896,256]{1,0:T(8,128)(2,1)S(1)} %slice.24), channel_id=1, source_target_pairs={{0,32},{1,9},{2,34},{3,11},{4,36},{5,13},{6,38},{7,15},{8,40},{9,1... | collective-permute-start | bytes 1376264 | tf_op jit(solution)/shard_map/ppermute | solution.py:101
  113.1 22.2 %collective-permute-start.10 = (bf16[1024,256]{1,0:T(8,128)(2,1)S(1)}, bf16[1024,256]{1,0:T(8,128)(2,1)S(1)}, u32[]{:S(2)}, u32[]{:S(2)}) collective-permute-start(bf16[1024,256]{1,0:T(8,128)(2,1)S(1)} %fusion.7), channel_id=1, source_target_pairs={{0,6},{1,7},{2,0},{3,1},{4,2},{5,3},{6,4},{7,5},{8,14},{9,15},{10,... | collective-permute-start | bytes 1572872 | tf_op jit(solution)/shard_map/ppermute | solution.py:101
  116.4 18.9 %collective-permute-start.9 = (bf16[1024,256]{1,0:T(8,128)(2,1)S(1)}, bf16[1024,256]{1,0:T(8,128)(2,1)S(1)}, u32[]{:S(2)}, u32[]{:S(2)}) collective-permute-start(bf16[1024,256]{1,0:T(8,128)(2,1)S(1)} %fusion.4), channel_id=1, source_target_pairs={{0,2},{1,3},{2,4},{3,5},{4,6},{5,7},{6,0},{7,1},{8,10},{9,11},{10,... | collective-permute-start | bytes 1572872 | tf_op jit(solution)/shard_map/ppermute | solution.py:101
  135.6 35.9 %collective-permute-start.15 = (bf16[2048,256]{1,0:T(8,128)(2,1)S(1)}, bf16[2048,256]{1,0:T(8,128)(2,1)S(1)}, u32[]{:S(2)}, u32[]{:S(2)}) collective-permute-start(bf16[2048,256]{1,0:T(8,128)(2,1)S(1)} %get-tuple-element.48), channel_id=1, source_target_pairs={{0,2},{1,3},{2,4},{3,5},{4,6},{5,7},{6,0},{7,1},{8,10},{9,11},{10,... | collective-permute-start | bytes 3145736 | tf_op jit(solution)/shard_map/ppermute | solution.py:101
  135.8 35.7 %collective-permute-start.16 = (bf16[2048,256]{1,0:T(8,128)(2,1)S(1)}, bf16[2048,256]{1,0:T(8,128)(2,1)S(1)}, u32[]{:S(2)}, u32[]{:S(2)}) collective-permute-start(bf16[2048,256]{1,0:T(8,128)(2,1)S(1)} %get-tuple-element.49), channel_id=1, source_target_pairs={{0,6},{1,7},{2,0},{3,1},{4,2},{5,3},{6,4},{7,5},{8,14},{9,15},{10,... | collective-permute-start | bytes 3145736 | tf_op jit(solution)/shard_map/ppermute | solution.py:101
  140.1 19.5 %collective-permute-start.22 = (bf16[1792,256]{1,0:T(8,128)(2,1)S(1)}, bf16[1792,256]{1,0:T(8,128)(2,1)S(1)}, u32[]{:S(2)}, u32[]{:S(2)}) collective-permute-start(bf16[1792,256]{1,0:T(8,128)(2,1)S(1)} %convolution_convert_fusion.1.refs_7_), channel_id=1, source_target_pairs={{0,96},{1,25},{2,98},{3,27},{4,100},{5,29},{6,102},{7,31},{8,104},... | collective-permute-start | bytes 2752520 | tf_op jit(solution)/shard_map/ppermute | solution.py:101
  141.1 28.7 %collective-permute-start.21 = (bf16[1792,256]{1,0:T(8,128)(2,1)S(1)}, bf16[1792,256]{1,0:T(8,128)(2,1)S(1)}, u32[]{:S(2)}, u32[]{:S(2)}) collective-permute-start(bf16[1792,256]{1,0:T(8,128)(2,1)S(1)} %convolution_convert_fusion.2.refs_6_), channel_id=1, source_target_pairs={{0,64},{1,17},{2,66},{3,19},{4,68},{5,21},{6,70},{7,23},{8,72},{9,... | collective-permute-start | bytes 2752520 | tf_op jit(solution)/shard_map/ppermute | solution.py:101
  143.2 26.6 %collective-permute-start.20 = (bf16[1792,256]{1,0:T(8,128)(2,1)S(1)}, bf16[1792,256]{1,0:T(8,128)(2,1)S(1)}, u32[]{:S(2)}, u32[]{:S(2)}) collective-permute-start(bf16[1792,256]{1,0:T(8,128)(2,1)S(1)} %convolution_convert_fusion.3.refs_5_), channel_id=1, source_target_pairs={{0,32},{1,9},{2,34},{3,11},{4,36},{5,13},{6,38},{7,15},{8,40},{9,1... | collective-permute-start | bytes 2752520 | tf_op jit(solution)/shard_map/ppermute | solution.py:101
  172.8 21.3 %collective-permute-start.18 = (bf16[528,256]{1,0:T(8,128)(2,1)S(1)}, bf16[528,256]{1,0:T(8,128)(2,1)S(1)}, u32[]{:S(2)}, u32[]{:S(2)}) collective-permute-start(bf16[528,256]{1,0:T(8,128)(2,1)S(1)} %get-tuple-element.51), channel_id=1, source_target_pairs={{8,0},{24,1},{10,2},{26,3},{12,4},{28,5},{14,6},{30,7},{11,8},{15,... | collective-permute-start | bytes 811016 | tf_op jit(solution)/shard_map/ppermute | solution.py:101
  176.3 17.8 %collective-permute-start.19 = (bf16[528,256]{1,0:T(8,128)(2,1)S(1)}, bf16[528,256]{1,0:T(8,128)(2,1)S(1)}, u32[]{:S(2)}, u32[]{:S(2)}) collective-permute-start(bf16[528,256]{1,0:T(8,128)(2,1)S(1)} %get-tuple-element.52), channel_id=1, source_target_pairs={{3,0},{7,1},{35,2},{39,3},{67,4},{71,5},{99,6},{103,7},{9,8},{13,9... | collective-permute-start | bytes 811016 | tf_op jit(solution)/shard_map/ppermute | solution.py:101
  186.0 13.4 %collective-permute-start.23 = (bf16[528,256]{1,0:T(8,128)(2,1)S(1)}, bf16[528,256]{1,0:T(8,128)(2,1)S(1)}, u32[]{:S(2)}, u32[]{:S(2)}) collective-permute-start(bf16[528,256]{1,0:T(8,128)(2,1)S(1)} %get-tuple-element.59), channel_id=1, source_target_pairs={{0,0},{16,1},{2,2},{18,3},{4,4},{20,5},{6,6},{22,7},{8,8},{24,9},{... | collective-permute-start | bytes 811016 | tf_op jit(solution)/shard_map/ppermute | solution.py:101
  (28 other events, 213.9 us)
Sparse Core Ops, SparseCore 0:
  53.1 51.9 all-gather.1
  109.5 52.0 reduce-scatter.1

commit v4 on v3

--- a/solution.py
+++ b/solution.py
@@ -521,7 +521,7 @@
     token[...] = jnp.zeros(token.shape, F32)
 
 
-def add(parts):
+def add(parts, after):
     steps = 4
     rows = row_blocks(parts[0], steps)
     return call(
@@ -530,6 +530,7 @@
         (0, 0),
         [rows] * 4,
         parts,
+        after,
         grid=(steps,),
         out_specs=[rows, fixed(8, 128)],
     )
@@ -642,10 +643,10 @@
     weight_grad = [
         dot(act, block_of(tile, feature_place + step), ((0,), (0,))) for step in range(N)
     ]
-    after, before = add_halves(mixed[1], mixed[2], top, bottom, weight_grad)
+    after, before = add_halves(mixed[1], mixed[2], top, bottom, weight_grad[2:])
     mixed = (mixed[0], send(after, hidden_ring(1)), send(before, hidden_ring(-1)))
     blocks = list(return_blocks(mixed, peaks))
-    weight_grad, added = add(ring_exchange(weight_grad, feature_ring))
+    weight_grad, added = add(ring_exchange(weight_grad, feature_ring), blocks[:1])
     grad_gate, grad_up, finished = finish(slope, silu, grad_act)
     blocks[2:] = gate(blocks[2:], (added, finished))
     blocks = [

time: 213 us -> 213 us (level)
  waiting for transfers between devices: 74.9 us -> 63.2 us
  matrix products: 31.6 us -> 37.5 us
  Pallas kernels: 14.9 us -> 19.9 us
    ppermute x26, waiting for transfers between devices: 74.9 us -> 63.1 us  [send(): return lax.ppermute(value, AXES, pairs)]
    dot_general x10, matrix products: 31.6 us -> 37.5 us  [dot(): lax.dot_general(left, right, (dims, ((), ())), preferred_element_type=F32)]
    pallas_call x18, Pallas kernels: 14.9 us -> 19.9 us  [call(): pl.pallas_call(body, out_shape=out_shape, in_specs=list(in_specs) + [ANYW...]
    unnamed x48 -> x50, local copies, waits for them, and re-layouts: 19.6 us -> 19.8 us
  transfers between devices with their start and end apart: 28 -> 28, of which waited for: 8 -> 7; matrix products, arithmetic and copies ran while one was open for 15% -> 18% of each run, Pallas kernels for 5% -> 7%
where the time goes in v4:
time: 213 us; the launch traced here: 211 us
  waiting for transfers between devices  63.2 us (30%)
  starting transfers between devices  55.7 us (26%)
  matrix products  37.5 us (18%)
  local copies, waits for them, and re-layouts  19.9 us (9%)
  Pallas kernels  19.9 us (9%)
  between operations  14.6 us (7%)
    ppermute x26, waiting for transfers between devices, send(): return lax.ppermute(value, AXES, pairs)  63.1 us
    ppermute x26, starting transfers between devices, send(): return lax.ppermute(value, AXES, pairs)  55.6 us
    dot_general x10, matrix products, dot(): lax.dot_general(left, right, (dims, ((), ())), preferred_element_type=F32)  37.5 us
    pallas_call x18, Pallas kernels, call(): pl.pallas_call(body, out_shape=out_shape, in_specs=list(in_specs) + [ANYW...  19.9 us
    unnamed x50, local copies, waits for them, and re-layouts  19.8 us
  transfers between devices with their start and end apart: 28, of which 7 were waited for; matrix products, arithmetic and copies ran while one was open for 18% of the time, Pallas kernels for 7%

profile of v4, /device:TPU:15, one launch (start us, length us, event | category | flops | bytes accessed | tf_op | source)
XLA Modules:
  0.0 210.7 jit_solution(1148780452681207646)
XLA Ops:
  18.3 4.1 %collective-permute-start.1 = (bf16[528,256]{1,0:T(8,128)(2,1)S(1)}, bf16[528,256]{1,0:T(8,128)(2,1)S(1)}, u32[]{:S(2)}, u32[]{:S(2)}) collective-permute-start(bf16[528,256]{1,0:T(8,128)(2,1)S(1)} %get-tuple-element.39), channel_id=1, source_target_pairs={{0,8},{1,24},{2,10},{3,26},{4,12},{5,28},{6,14},{7,30},{8,11},{9,1... | collective-permute-start | bytes 811016 | tf_op jit(solution)/shard_map/ppermute | solution.py:101
  24.4 7.0 %collective-permute-start.3 = (bf16[528,256]{1,0:T(8,128)(2,1)S(1)}, bf16[528,256]{1,0:T(8,128)(2,1)S(1)}, u32[]{:S(2)}, u32[]{:S(2)}) collective-permute-start(bf16[528,256]{1,0:T(8,128)(2,1)S(1)} %get-tuple-element.41), channel_id=1, source_target_pairs={{0,0},{1,16},{2,2},{3,18},{4,4},{5,20},{6,6},{7,22},{8,8},{9,24},{... | collective-permute-start | bytes 811016 | tf_op jit(solution)/shard_map/ppermute | solution.py:101
  31.4 2.8 %collective-permute-start.4 = (bf16[528,256]{1,0:T(8,128)(2,1)S(1)}, bf16[528,256]{1,0:T(8,128)(2,1)S(1)}, u32[]{:S(2)}, u32[]{:S(2)}) collective-permute-start(bf16[528,256]{1,0:T(8,128)(2,1)S(1)} %get-tuple-element.42), channel_id=1, source_target_pairs={{0,1},{1,5},{2,33},{3,37},{4,65},{5,69},{6,97},{7,101},{8,0},{9,16... | collective-permute-start | bytes 811016 | tf_op jit(solution)/shard_map/ppermute | solution.py:101
  34.2 16.7 %collective-permute-done.2.refs_2_ = bf16[528,256]{1,0:T(8,128)(2,1)S(1)} collective-permute-done((bf16[528,256]{1,0:T(8,128)(2,1)S(1)}, bf16[528,256]{1,0:T(8,128)(2,1)S(1)}, u32[]{:S(2)}, u32[]{:S(2)}) %collective-permute-start.2) | collective-permute-done | bytes 270368 | tf_op jit(solution)/shard_map/ppermute | solution.py:101
  53.1 2.7 %collective-permute-start.11 = (bf16[2048,256]{1,0:T(8,128)(2,1)S(1)}, bf16[2048,256]{1,0:T(8,128)(2,1)S(1)}, u32[]{:S(2)}, u32[]{:S(2)}) collective-permute-start(bf16[2048,256]{1,0:T(8,128)(2,1)S(1)} %get-tuple-element.43.refs_1_.refs_2_.refs_0_), channel_id=1, source_target_pairs={{0,6},{1,7},{2,0},{3,1},{4,2},{5,3},{6,4},{7,5},{8,14},{9,15},{10,... | collective-permute-start | bytes 3145736 | tf_op jit(solution)/shard_map/ppermute | solution.py:101
  57.1 4.7 %collective-permute-start.6 = (bf16[1808,256]{1,0:T(8,128)(2,1)S(1)}, bf16[1808,256]{1,0:T(8,128)(2,1)S(1)}, u32[]{:S(2)}, u32[]{:S(2)}) collective-permute-start(bf16[1808,256]{1,0:T(8,128)(2,1)S(1)} %shard_map.123.refs_0_.refs_5_), channel_id=1, source_target_pairs={{0,32},{1,9},{2,34},{3,11},{4,36},{5,13},{6,38},{7,15},{8,40},{9,1... | collective-permute-start | bytes 2777096 | tf_op jit(solution)/shard_map/ppermute | solution.py:101
  61.8 16.4 %collective-permute-done.12.refs_4_ = bf16[2048,256]{1,0:T(8,128)(2,1)S(1)} collective-permute-done((bf16[2048,256]{1,0:T(8,128)(2,1)S(1)}, bf16[2048,256]{1,0:T(8,128)(2,1)S(1)}, u32[]{:S(2)}, u32[]{:S(2)}) %collective-permute-start.12) | collective-permute-done | bytes 1048608 | tf_op jit(solution)/shard_map/ppermute | solution.py:101
  78.4 2.9 %collective-permute-start.14 = (bf16[1024,256]{1,0:T(8,128)(2,1)S(1)}, bf16[1024,256]{1,0:T(8,128)(2,1)S(1)}, u32[]{:S(2)}, u32[]{:S(2)}) collective-permute-start(bf16[1024,256]{1,0:T(8,128)(2,1)S(1)} %slice.29), channel_id=1, source_target_pairs={{0,6},{1,7},{2,0},{3,1},{4,2},{5,3},{6,4},{7,5},{8,14},{9,15},{10,... | collective-permute-start | bytes 1572872 | tf_op jit(solution)/shard_map/ppermute | solution.py:101
  87.1 8.8 %collective-permute-done.7.refs_2_ = bf16[896,256]{1,0:T(8,128)(2,1)S(1)} collective-permute-done((bf16[896,256]{1,0:T(8,128)(2,1)S(1)}, bf16[896,256]{1,0:T(8,128)(2,1)S(1)}, u32[]{:S(2)}, u32[]{:S(2)}) %collective-permute-start.7) | collective-permute-done | bytes 458784 | tf_op jit(solution)/shard_map/ppermute | solution.py:101
  99.6 9.7 %convolution_convert_fusion = bf16[2048,1792]{1,0:T(8,128)(2,1)} fusion(bf16[2048,1024]{1,0:T(8,128)(2,1)S(1)} %shard_map.127, bf16[1792,1024]{1,0:T(8,128)(2,1)S(1)} %get-tuple-element.46), kind=kOutput, calls=%fused_computation | convolution fusion | flops 7519862784 | bytes 15204352 | tf_op jit(solution)/shard_map/dot_general | solution.py:589
  110.2 3.5 %fusion.7 = bf16[1024,256]{1,0:T(8,128)(2,1)S(1)} fusion(bf16[2048,1792]{1,0:T(8,128)(2,1)} %all-gather.2.cloned.1.call-done.refs_0_, bf16[1792,1024]{1,0:T(8,128)(2,1)} %copy-done.23, s32[]{:T(128)S(6)} %select_n.69), kind=kOutput, calls=%fused_computation.13 | convolution fusion | flops 939786240 | bytes 5111812 | tf_op jit(solution)/shard_map/dot_general | solution.py:589
  114.7 2.4 %fusion.4 = bf16[1024,256]{1,0:T(8,128)(2,1)S(1)} fusion(bf16[2048,1792]{1,0:T(8,128)(2,1)S(1)} %copy-done.5, bf16[1792,1024]{1,0:T(8,128)(2,1)} %copy-done.23, s32[]{:T(128)S(6)} %select_n.69), kind=kOutput, calls=%fused_computation.12 | convolution fusion | flops 939786240 | bytes 5111812 | tf_op jit(solution)/shard_map/dot_general | solution.py:589
  126.9 3.2 %convolution_convert_fusion.3.refs_5_ = bf16[1792,256]{1,0:T(8,128)(2,1)} fusion(bf16[2048,1792]{1,0:T(8,128)(2,1)S(1)} %shard_map.125, bf16[2048,1024]{1,0:T(8,128)(2,1)S(1)} %copy-done.8, s32[]{:T(128)S(6)} %select_n.74), kind=kOutput, calls=%fused_computation.7 | convolution fusion | flops 1879506944 | bytes 9306116 | tf_op jit(solution)/shard_map/dot_general | solution.py:589
  132.1 3.2 %convolution_convert_fusion.4.refs_4_ = bf16[1792,256]{1,0:T(8,128)(2,1)} fusion(bf16[2048,1792]{1,0:T(8,128)(2,1)S(1)} %shard_map.125, bf16[2048,1024]{1,0:T(8,128)(2,1)S(1)} %copy-done.8, s32[]{:T(128)S(6)} %select_n.72), kind=kOutput, calls=%fused_computation.8 | convolution fusion | flops 1879506944 | bytes 9306116 | tf_op jit(solution)/shard_map/dot_general | solution.py:589
  136.8 2.6 %collective-permute-start.16 = (bf16[2048,256]{1,0:T(8,128)(2,1)}, bf16[2048,256]{1,0:T(8,128)(2,1)}, u32[]{:S(2)}, u32[]{:S(2)}) collective-permute-start(bf16[2048,256]{1,0:T(8,128)(2,1)} %get-tuple-element.49), channel_id=1, source_target_pairs={{0,6},{1,7},{2,0},{3,1},{4,2},{5,3},{6,4},{7,5},{8,14},{9,15},{10,... | collective-permute-start | bytes 3145736 | tf_op jit(solution)/shard_map/ppermute | solution.py:101
  139.5 3.2 %convolution_convert_fusion.1 = bf16[1792,256]{1,0:T(8,128)(2,1)} fusion(bf16[2048,1792]{1,0:T(8,128)(2,1)S(1)} %shard_map.125, bf16[2048,1024]{1,0:T(8,128)(2,1)S(1)} %copy-done.8, s32[]{:T(128)S(6)} %select_n.78), kind=kOutput, calls=%fused_computation.5 | convolution fusion | flops 1879506944 | bytes 9306116 | tf_op jit(solution)/shard_map/dot_general | solution.py:589
  142.7 3.6 %collective-permute-start.21 = (bf16[1792,256]{1,0:T(8,128)(2,1)}, bf16[1792,256]{1,0:T(8,128)(2,1)}, u32[]{:S(2)}, u32[]{:S(2)}) collective-permute-start(bf16[1792,256]{1,0:T(8,128)(2,1)} %convolution_convert_fusion.4.refs_4_), channel_id=1, source_target_pairs={{0,64},{1,17},{2,66},{3,19},{4,68},{5,21},{6,70},{7,23},{8,72},{9,... | collective-permute-start | bytes 2752520 | tf_op jit(solution)/shard_map/ppermute | solution.py:101
  146.3 5.5 %convolution_convert_fusion.2.refs_0_ = bf16[1792,256]{1,0:T(8,128)(2,1)S(1)} fusion(bf16[2048,1792]{1,0:T(8,128)(2,1)} %copy-done.6, bf16[2048,1024]{1,0:T(8,128)(2,1)} %copy-done.7, s32[]{:T(128)S(6)} %select_n.76), kind=kOutput, calls=%fused_computation.6 | convolution fusion | flops 1879506944 | bytes 9306116 | tf_op jit(solution)/shard_map/dot_general | solution.py:589
  151.8 10.7 %collective-permute-done.15.refs_2_ = bf16[2048,256]{1,0:T(8,128)(2,1)} collective-permute-done((bf16[2048,256]{1,0:T(8,128)(2,1)}, bf16[2048,256]{1,0:T(8,128)(2,1)}, u32[]{:S(2)}, u32[]{:S(2)}) %collective-permute-start.15) | collective-permute-done | bytes 1048608 | tf_op jit(solution)/shard_map/ppermute | solution.py:101
  162.5 2.8 %shard_map.129 = (bf16[528,256]{1,0:T(8,128)(2,1)}, bf16[528,256]{1,0:T(8,128)(2,1)}, bf16[528,256]{1,0:T(8,128)(2,1)S(1)}, bf16[528,256]{1,0:T(8,128)(2,1)S(1)}) custom-call(s32[8,128]{1,0:T(8,128)S(1)} %copy-done.18, bf16[2048,256]{1,0:T(8,128)(2,1)S(1)} %convolution_convert_fusion.7.refs_1_, bf16[2048,256]{1,0:T(8,128)(2,1)} %collective-permute-done.15.refs_2_, ...), custom_call_target="tpu_custom_call" | custom-call | tf_op jit(solution)/shard_map/pallas_call | solution.py:117
  165.3 4.1 %collective-permute-start.18 = (bf16[528,256]{1,0:T(8,128)(2,1)}, bf16[528,256]{1,0:T(8,128)(2,1)S(1)}, u32[]{:S(2)}, u32[]{:S(2)}) collective-permute-start(bf16[528,256]{1,0:T(8,128)(2,1)} %get-tuple-element.51.refs_4_), channel_id=1, source_target_pairs={{8,0},{24,1},{10,2},{26,3},{12,4},{28,5},{14,6},{30,7},{11,8},{15,... | collective-permute-start | bytes 811016 | tf_op jit(solution)/shard_map/ppermute | solution.py:101
  169.4 7.8 %collective-permute-start.19 = (bf16[528,256]{1,0:T(8,128)(2,1)}, bf16[528,256]{1,0:T(8,128)(2,1)S(1)}, u32[]{:S(2)}, u32[]{:S(2)}) collective-permute-start(bf16[528,256]{1,0:T(8,128)(2,1)} %get-tuple-element.52), channel_id=1, source_target_pairs={{3,0},{7,1},{35,2},{39,3},{67,4},{71,5},{99,6},{103,7},{9,8},{13,9... | collective-permute-start | bytes 811016 | tf_op jit(solution)/shard_map/ppermute | solution.py:101
  177.3 3.9 %shard_map.130 = (bf16[1792,256]{1,0:T(8,128)(2,1)}, f32[8,128]{1,0:T(8,128)S(1)}) custom-call(bf16[1792,256]{1,0:T(8,128)(2,1)S(1)} %convolution_convert_fusion.2.refs_0_, bf16[1792,256]{1,0:T(8,128)(2,1)} %collective-permute-done.20.refs_1_, bf16[1792,256]{1,0:T(8,128)(2,1)} %collective-permute-done.21.refs_2_, ...), custom_call_target="tpu_custom_call" | custom-call | tf_op jit(solution)/shard_map/pallas_call | solution.py:117
  190.6 7.8 %collective-permute-done.23.refs_3_.refs_2_ = bf16[528,256]{1,0:T(8,128)(2,1)S(1)} collective-permute-done((bf16[528,256]{1,0:T(8,128)(2,1)S(1)}, bf16[528,256]{1,0:T(8,128)(2,1)S(1)}, u32[]{:S(2)}, u32[]{:S(2)}) %collective-permute-start.23) | collective-permute-done | bytes 270368 | tf_op jit(solution)/shard_map/ppermute | solution.py:101
  (117 shorter events, 55.8 us)
Async XLA Ops:
  7.2 103.0 %all-gather.2.cloned.1.call-start = ((), (), s32[]{:S(2)}) async-start(), calls=%async_computation.1 | async-start | bytes 9175040 | tf_op jit(solution)/shard_map/all_gather | solution.py:617
  18.3 15.9 %collective-permute-start.1 = (bf16[528,256]{1,0:T(8,128)(2,1)S(1)}, bf16[528,256]{1,0:T(8,128)(2,1)S(1)}, u32[]{:S(2)}, u32[]{:S(2)}) collective-permute-start(bf16[528,256]{1,0:T(8,128)(2,1)S(1)} %get-tuple-element.39), channel_id=1, source_target_pairs={{0,8},{1,24},{2,10},{3,26},{4,12},{5,28},{6,14},{7,30},{8,11},{9,1... | collective-permute-start | bytes 811016 | tf_op jit(solution)/shard_map/ppermute | solution.py:101
  22.4 28.5 %collective-permute-start.2 = (bf16[528,256]{1,0:T(8,128)(2,1)S(1)}, bf16[528,256]{1,0:T(8,128)(2,1)S(1)}, u32[]{:S(2)}, u32[]{:S(2)}) collective-permute-start(bf16[528,256]{1,0:T(8,128)(2,1)S(1)} %get-tuple-element.40), channel_id=1, source_target_pairs={{0,3},{1,7},{2,35},{3,39},{4,67},{5,71},{6,99},{7,103},{8,9},{9,13... | collective-permute-start | bytes 811016 | tf_op jit(solution)/shard_map/ppermute | solution.py:101
  24.4 26.6 %collective-permute-start.3 = (bf16[528,256]{1,0:T(8,128)(2,1)S(1)}, bf16[528,256]{1,0:T(8,128)(2,1)S(1)}, u32[]{:S(2)}, u32[]{:S(2)}) collective-permute-start(bf16[528,256]{1,0:T(8,128)(2,1)S(1)} %get-tuple-element.41), channel_id=1, source_target_pairs={{0,0},{1,16},{2,2},{3,18},{4,4},{5,20},{6,6},{7,22},{8,8},{9,24},{... | collective-permute-start | bytes 811016 | tf_op jit(solution)/shard_map/ppermute | solution.py:101
  31.4 19.6 %collective-permute-start.4 = (bf16[528,256]{1,0:T(8,128)(2,1)S(1)}, bf16[528,256]{1,0:T(8,128)(2,1)S(1)}, u32[]{:S(2)}, u32[]{:S(2)}) collective-permute-start(bf16[528,256]{1,0:T(8,128)(2,1)S(1)} %get-tuple-element.42), channel_id=1, source_target_pairs={{0,1},{1,5},{2,33},{3,37},{4,65},{5,69},{6,97},{7,101},{8,0},{9,16... | collective-permute-start | bytes 811016 | tf_op jit(solution)/shard_map/ppermute | solution.py:101
  52.9 128.3 %reduce-scatter.2.cloned.1.call-start = ((), (), s32[]{:S(2)}) async-start(), calls=%async_computation.2 | async-start | bytes 9175040 | tf_op jit(solution)/shard_map/reduce_scatter | solution.py:635
  53.0 25.2 %collective-permute-start.12 = (bf16[2048,256]{1,0:T(8,128)(2,1)S(1)}, bf16[2048,256]{1,0:T(8,128)(2,1)S(1)}, u32[]{:S(2)}, u32[]{:S(2)}) collective-permute-start(bf16[2048,256]{1,0:T(8,128)(2,1)S(1)} %get-tuple-element.43.refs_1_.refs_2_.refs_0_), channel_id=1, source_target_pairs={{0,2},{1,3},{2,4},{3,5},{4,6},{5,7},{6,0},{7,1},{8,10},{9,11},{10,... | collective-permute-start | bytes 3145736 | tf_op jit(solution)/shard_map/ppermute | solution.py:101
  53.1 25.2 %collective-permute-start.11 = (bf16[2048,256]{1,0:T(8,128)(2,1)S(1)}, bf16[2048,256]{1,0:T(8,128)(2,1)S(1)}, u32[]{:S(2)}, u32[]{:S(2)}) collective-permute-start(bf16[2048,256]{1,0:T(8,128)(2,1)S(1)} %get-tuple-element.43.refs_1_.refs_2_.refs_0_), channel_id=1, source_target_pairs={{0,6},{1,7},{2,0},{3,1},{4,2},{5,3},{6,4},{7,5},{8,14},{9,15},{10,... | collective-permute-start | bytes 3145736 | tf_op jit(solution)/shard_map/ppermute | solution.py:101
  57.0 24.2 %collective-permute-start.5 = (bf16[1808,256]{1,0:T(8,128)(2,1)S(1)}, bf16[1808,256]{1,0:T(8,128)(2,1)S(1)}, u32[]{:S(2)}, u32[]{:S(2)}) collective-permute-start(bf16[1808,256]{1,0:T(8,128)(2,1)S(1)} %shard_map.123.refs_0_.refs_5_), channel_id=1, source_target_pairs={{0,96},{1,25},{2,98},{3,27},{4,100},{5,29},{6,102},{7,31},{8,104},... | collective-permute-start | bytes 2777096 | tf_op jit(solution)/shard_map/ppermute | solution.py:101
  57.1 24.3 %collective-permute-start.6 = (bf16[1808,256]{1,0:T(8,128)(2,1)S(1)}, bf16[1808,256]{1,0:T(8,128)(2,1)S(1)}, u32[]{:S(2)}, u32[]{:S(2)}) collective-permute-start(bf16[1808,256]{1,0:T(8,128)(2,1)S(1)} %shard_map.123.refs_0_.refs_5_), channel_id=1, source_target_pairs={{0,32},{1,9},{2,34},{3,11},{4,36},{5,13},{6,38},{7,15},{8,40},{9,1... | collective-permute-start | bytes 2777096 | tf_op jit(solution)/shard_map/ppermute | solution.py:101
  78.2 18.3 %collective-permute-start.13 = (bf16[1024,256]{1,0:T(8,128)(2,1)S(1)}, bf16[1024,256]{1,0:T(8,128)(2,1)S(1)}, u32[]{:S(2)}, u32[]{:S(2)}) collective-permute-start(bf16[1024,256]{1,0:T(8,128)(2,1)S(1)} %slice.28), channel_id=1, source_target_pairs={{0,2},{1,3},{2,4},{3,5},{4,6},{5,7},{6,0},{7,1},{8,10},{9,11},{10,... | collective-permute-start | bytes 1572872 | tf_op jit(solution)/shard_map/ppermute | solution.py:101
  78.4 18.2 %collective-permute-start.14 = (bf16[1024,256]{1,0:T(8,128)(2,1)S(1)}, bf16[1024,256]{1,0:T(8,128)(2,1)S(1)}, u32[]{:S(2)}, u32[]{:S(2)}) collective-permute-start(bf16[1024,256]{1,0:T(8,128)(2,1)S(1)} %slice.29), channel_id=1, source_target_pairs={{0,6},{1,7},{2,0},{3,1},{4,2},{5,3},{6,4},{7,5},{8,14},{9,15},{10,... | collective-permute-start | bytes 1572872 | tf_op jit(solution)/shard_map/ppermute | solution.py:101
  81.3 14.6 %collective-permute-start.8 = (bf16[912,256]{1,0:T(8,128)(2,1)S(1)}, bf16[912,256]{1,0:T(8,128)(2,1)S(1)}, u32[]{:S(2)}, u32[]{:S(2)}) collective-permute-start(bf16[912,256]{1,0:T(8,128)(2,1)S(1)} %slice.25), channel_id=1, source_target_pairs={{0,96},{1,25},{2,98},{3,27},{4,100},{5,29},{6,102},{7,31},{8,104},... | collective-permute-start | bytes 1400840 | tf_op jit(solution)/shard_map/ppermute | solution.py:101
  81.4 14.4 %collective-permute-start.7 = (bf16[896,256]{1,0:T(8,128)(2,1)S(1)}, bf16[896,256]{1,0:T(8,128)(2,1)S(1)}, u32[]{:S(2)}, u32[]{:S(2)}) collective-permute-start(bf16[896,256]{1,0:T(8,128)(2,1)S(1)} %slice.24), channel_id=1, source_target_pairs={{0,32},{1,9},{2,34},{3,11},{4,36},{5,13},{6,38},{7,15},{8,40},{9,1... | collective-permute-start | bytes 1376264 | tf_op jit(solution)/shard_map/ppermute | solution.py:101
  109.5 33.3 %collective-permute-start.17 = (f32[8,128]{1,0:T(8,128)S(1)}, f32[8,128]{1,0:T(8,128)S(1)}, u32[]{:S(2)}, u32[]{:S(2)}) collective-permute-start(f32[8,128]{1,0:T(8,128)S(1)} %get-tuple-element.50), channel_id=1, source_target_pairs={{0,1},{1,0},{2,3},{3,2},{4,5},{5,4},{6,7},{7,6},{8,9},{9,8},{10,11... | collective-permute-start | bytes 12296 | tf_op jit(solution)/shard_map/ppermute | solution.py:101
  113.8 21.5 %collective-permute-start.10 = (bf16[1024,256]{1,0:T(8,128)(2,1)S(1)}, bf16[1024,256]{1,0:T(8,128)(2,1)S(1)}, u32[]{:S(2)}, u32[]{:S(2)}) collective-permute-start(bf16[1024,256]{1,0:T(8,128)(2,1)S(1)} %fusion.7), channel_id=1, source_target_pairs={{0,6},{1,7},{2,0},{3,1},{4,2},{5,3},{6,4},{7,5},{8,14},{9,15},{10,... | collective-permute-start | bytes 1572872 | tf_op jit(solution)/shard_map/ppermute | solution.py:101
  117.1 18.2 %collective-permute-start.9 = (bf16[1024,256]{1,0:T(8,128)(2,1)S(1)}, bf16[1024,256]{1,0:T(8,128)(2,1)S(1)}, u32[]{:S(2)}, u32[]{:S(2)}) collective-permute-start(bf16[1024,256]{1,0:T(8,128)(2,1)S(1)} %fusion.4), channel_id=1, source_target_pairs={{0,2},{1,3},{2,4},{3,5},{4,6},{5,7},{6,0},{7,1},{8,10},{9,11},{10,... | collective-permute-start | bytes 1572872 | tf_op jit(solution)/shard_map/ppermute | solution.py:101
  130.1 47.2 %collective-permute-start.22 = (bf16[1792,256]{1,0:T(8,128)(2,1)}, bf16[1792,256]{1,0:T(8,128)(2,1)}, u32[]{:S(2)}, u32[]{:S(2)}) collective-permute-start(bf16[1792,256]{1,0:T(8,128)(2,1)} %convolution_convert_fusion.3.refs_5_), channel_id=1, source_target_pairs={{0,96},{1,25},{2,98},{3,27},{4,100},{5,29},{6,102},{7,31},{8,104},... | collective-permute-start | bytes 2752520 | tf_op jit(solution)/shard_map/ppermute | solution.py:101
  136.8 25.7 %collective-permute-start.15 = (bf16[2048,256]{1,0:T(8,128)(2,1)}, bf16[2048,256]{1,0:T(8,128)(2,1)}, u32[]{:S(2)}, u32[]{:S(2)}) collective-permute-start(bf16[2048,256]{1,0:T(8,128)(2,1)} %get-tuple-element.48), channel_id=1, source_target_pairs={{0,2},{1,3},{2,4},{3,5},{4,6},{5,7},{6,0},{7,1},{8,10},{9,11},{10,... | collective-permute-start | bytes 3145736 | tf_op jit(solution)/shard_map/ppermute | solution.py:101
  136.8 25.6 %collective-permute-start.16 = (bf16[2048,256]{1,0:T(8,128)(2,1)}, bf16[2048,256]{1,0:T(8,128)(2,1)}, u32[]{:S(2)}, u32[]{:S(2)}) collective-permute-start(bf16[2048,256]{1,0:T(8,128)(2,1)} %get-tuple-element.49), channel_id=1, source_target_pairs={{0,6},{1,7},{2,0},{3,1},{4,2},{5,3},{6,4},{7,5},{8,14},{9,15},{10,... | collective-permute-start | bytes 3145736 | tf_op jit(solution)/shard_map/ppermute | solution.py:101
  142.7 34.5 %collective-permute-start.20 = (bf16[1792,256]{1,0:T(8,128)(2,1)}, bf16[1792,256]{1,0:T(8,128)(2,1)}, u32[]{:S(2)}, u32[]{:S(2)}) collective-permute-start(bf16[1792,256]{1,0:T(8,128)(2,1)} %convolution_convert_fusion.1), channel_id=1, source_target_pairs={{0,32},{1,9},{2,34},{3,11},{4,36},{5,13},{6,38},{7,15},{8,40},{9,1... | collective-permute-start | bytes 2752520 | tf_op jit(solution)/shard_map/ppermute | solution.py:101
  142.7 34.5 %collective-permute-start.21 = (bf16[1792,256]{1,0:T(8,128)(2,1)}, bf16[1792,256]{1,0:T(8,128)(2,1)}, u32[]{:S(2)}, u32[]{:S(2)}) collective-permute-start(bf16[1792,256]{1,0:T(8,128)(2,1)} %convolution_convert_fusion.4.refs_4_), channel_id=1, source_target_pairs={{0,64},{1,17},{2,66},{3,19},{4,68},{5,21},{6,70},{7,23},{8,72},{9,... | collective-permute-start | bytes 2752520 | tf_op jit(solution)/shard_map/ppermute | solution.py:101
  165.3 25.3 %collective-permute-start.18 = (bf16[528,256]{1,0:T(8,128)(2,1)}, bf16[528,256]{1,0:T(8,128)(2,1)S(1)}, u32[]{:S(2)}, u32[]{:S(2)}) collective-permute-start(bf16[528,256]{1,0:T(8,128)(2,1)} %get-tuple-element.51.refs_4_), channel_id=1, source_target_pairs={{8,0},{24,1},{10,2},{26,3},{12,4},{28,5},{14,6},{30,7},{11,8},{15,... | collective-permute-start | bytes 811016 | tf_op jit(solution)/shard_map/ppermute | solution.py:101
  169.4 21.1 %collective-permute-start.19 = (bf16[528,256]{1,0:T(8,128)(2,1)}, bf16[528,256]{1,0:T(8,128)(2,1)S(1)}, u32[]{:S(2)}, u32[]{:S(2)}) collective-permute-start(bf16[528,256]{1,0:T(8,128)(2,1)} %get-tuple-element.52), channel_id=1, source_target_pairs={{3,0},{7,1},{35,2},{39,3},{67,4},{71,5},{99,6},{103,7},{9,8},{13,9... | collective-permute-start | bytes 811016 | tf_op jit(solution)/shard_map/ppermute | solution.py:101
  (29 other events, 216.4 us)
Sparse Core Ops, SparseCore 0:
  53.1 51.9 all-gather.1
  109.5 55.6 reduce-scatter.1

commit v5 on v4

--- a/solution.py
+++ b/solution.py
@@ -648,11 +648,12 @@
     blocks = list(return_blocks(mixed, peaks))
     weight_grad, added = add(ring_exchange(weight_grad, feature_ring), blocks[:1])
     grad_gate, grad_up, finished = finish(slope, silu, grad_act)
-    blocks[2:] = gate(blocks[2:], (added, finished))
+    blocks[2:] = gate(blocks[2:], (added,))
     blocks = [
         send(block, [(edge[1], edge[0]) for edge in ROUNDS[number]])
         for number, block in enumerate(blocks)
     ]
+    blocks = gate(blocks, (finished,))
     mixed = merge(blocks, ())
     peaks = read_notes(blocks)
     new_weight, new_act = histories(

time: 213 us -> 207 us (0.972)
  the two profiles are of different devices: /device:TPU:15 before, /device:TPU:23 now
where the time goes in v5:
time: 207 us
  waiting for transfers between devices  63.8 us (31%)
  starting transfers between devices  52 us (25%)
  matrix products  36.7 us (18%)
  Pallas kernels  19.9 us (10%)
  local copies, waits for them, and re-layouts  19.8 us (10%)
  between operations  14.6 us (7%)
    ppermute x26, waiting for transfers between devices, send(): return lax.ppermute(value, AXES, pairs)  63.7 us
    ppermute x26, starting transfers between devices, send(): return lax.ppermute(value, AXES, pairs)  51.9 us
    dot_general x10, matrix products, dot(): lax.dot_general(left, right, (dims, ((), ())), preferred_element_type=F32)  36.7 us
    pallas_call x19, Pallas kernels, call(): pl.pallas_call(body, out_shape=out_shape, in_specs=list(in_specs) + [ANYW...  19.9 us
    unnamed x50, local copies, waits for them, and re-layouts  19.6 us
  transfers between devices with their start and end apart: 28, of which 8 were waited for; matrix products, arithmetic and copies ran while one was open for 18% of the time, Pallas kernels for 7%

profile of v5, /device:TPU:23, one launch (start us, length us, event | category | flops | bytes accessed | tf_op | source)
XLA Modules:
  0.0 206.7 jit_solution(10996816032999878329)
XLA Ops:
  18.3 5.4 %collective-permute-start.1 = (bf16[528,256]{1,0:T(8,128)(2,1)S(1)}, bf16[528,256]{1,0:T(8,128)(2,1)S(1)}, u32[]{:S(2)}, u32[]{:S(2)}) collective-permute-start(bf16[528,256]{1,0:T(8,128)(2,1)S(1)} %get-tuple-element.43), channel_id=1, source_target_pairs={{0,8},{1,24},{2,10},{3,26},{4,12},{5,28},{6,14},{7,30},{8,11},{9,1... | collective-permute-start | bytes 811016 | tf_op jit(solution)/shard_map/ppermute | solution.py:101
  23.7 2.4 %collective-permute-start.2 = (bf16[528,256]{1,0:T(8,128)(2,1)S(1)}, bf16[528,256]{1,0:T(8,128)(2,1)S(1)}, u32[]{:S(2)}, u32[]{:S(2)}) collective-permute-start(bf16[528,256]{1,0:T(8,128)(2,1)S(1)} %get-tuple-element.44), channel_id=1, source_target_pairs={{0,3},{1,7},{2,35},{3,39},{4,67},{5,71},{6,99},{7,103},{8,9},{9,13... | collective-permute-start | bytes 811016 | tf_op jit(solution)/shard_map/ppermute | solution.py:101
  28.1 3.0 %collective-permute-start.4 = (bf16[528,256]{1,0:T(8,128)(2,1)S(1)}, bf16[528,256]{1,0:T(8,128)(2,1)S(1)}, u32[]{:S(2)}, u32[]{:S(2)}) collective-permute-start(bf16[528,256]{1,0:T(8,128)(2,1)S(1)} %get-tuple-element.46), channel_id=1, source_target_pairs={{0,1},{1,5},{2,33},{3,37},{4,65},{5,69},{6,97},{7,101},{8,0},{9,16... | collective-permute-start | bytes 811016 | tf_op jit(solution)/shard_map/ppermute | solution.py:101
  31.0 11.7 %collective-permute-done.1.refs_1_ = bf16[528,256]{1,0:T(8,128)(2,1)S(1)} collective-permute-done((bf16[528,256]{1,0:T(8,128)(2,1)S(1)}, bf16[528,256]{1,0:T(8,128)(2,1)S(1)}, u32[]{:S(2)}, u32[]{:S(2)}) %collective-permute-start.1) | collective-permute-done | bytes 270368 | tf_op jit(solution)/shard_map/ppermute | solution.py:101
  42.7 4.0 %collective-permute-done.2.refs_2_ = bf16[528,256]{1,0:T(8,128)(2,1)S(1)} collective-permute-done((bf16[528,256]{1,0:T(8,128)(2,1)S(1)}, bf16[528,256]{1,0:T(8,128)(2,1)S(1)}, u32[]{:S(2)}, u32[]{:S(2)}) %collective-permute-start.2) | collective-permute-done | bytes 270368 | tf_op jit(solution)/shard_map/ppermute | solution.py:101
  46.7 7.6 %collective-permute-done.4.refs_4_ = bf16[528,256]{1,0:T(8,128)(2,1)S(1)} collective-permute-done((bf16[528,256]{1,0:T(8,128)(2,1)S(1)}, bf16[528,256]{1,0:T(8,128)(2,1)S(1)}, u32[]{:S(2)}, u32[]{:S(2)}) %collective-permute-start.4) | collective-permute-done | bytes 270368 | tf_op jit(solution)/shard_map/ppermute | solution.py:101
  56.4 2.7 %collective-permute-start.11 = (bf16[2048,256]{1,0:T(8,128)(2,1)S(1)}, bf16[2048,256]{1,0:T(8,128)(2,1)S(1)}, u32[]{:S(2)}, u32[]{:S(2)}) collective-permute-start(bf16[2048,256]{1,0:T(8,128)(2,1)S(1)} %get-tuple-element.47.refs_1_.refs_2_.refs_0_), channel_id=1, source_target_pairs={{0,6},{1,7},{2,0},{3,1},{4,2},{5,3},{6,4},{7,5},{8,14},{9,15},{10,... | collective-permute-start | bytes 3145736 | tf_op jit(solution)/shard_map/ppermute | solution.py:101
  61.9 16.0 %collective-permute-done.12.refs_4_ = bf16[2048,256]{1,0:T(8,128)(2,1)S(1)} collective-permute-done((bf16[2048,256]{1,0:T(8,128)(2,1)S(1)}, bf16[2048,256]{1,0:T(8,128)(2,1)S(1)}, u32[]{:S(2)}, u32[]{:S(2)}) %collective-permute-start.12) | collective-permute-done | bytes 1048608 | tf_op jit(solution)/shard_map/ppermute | solution.py:101
  78.1 2.7 %collective-permute-start.14 = (bf16[1024,256]{1,0:T(8,128)(2,1)S(1)}, bf16[1024,256]{1,0:T(8,128)(2,1)S(1)}, u32[]{:S(2)}, u32[]{:S(2)}) collective-permute-start(bf16[1024,256]{1,0:T(8,128)(2,1)S(1)} %slice.29), channel_id=1, source_target_pairs={{0,6},{1,7},{2,0},{3,1},{4,2},{5,3},{6,4},{7,5},{8,14},{9,15},{10,... | collective-permute-start | bytes 1572872 | tf_op jit(solution)/shard_map/ppermute | solution.py:101
  86.9 7.3 %collective-permute-done.7.refs_2_ = bf16[896,256]{1,0:T(8,128)(2,1)S(1)} collective-permute-done((bf16[896,256]{1,0:T(8,128)(2,1)S(1)}, bf16[896,256]{1,0:T(8,128)(2,1)S(1)}, u32[]{:S(2)}, u32[]{:S(2)}) %collective-permute-start.7) | collective-permute-done | bytes 458784 | tf_op jit(solution)/shard_map/ppermute | solution.py:101
  98.0 9.7 %convolution_convert_fusion = bf16[2048,1792]{1,0:T(8,128)(2,1)} fusion(bf16[2048,1024]{1,0:T(8,128)(2,1)S(1)} %shard_map.127, bf16[1792,1024]{1,0:T(8,128)(2,1)S(1)} %get-tuple-element.50), kind=kOutput, calls=%fused_computation | convolution fusion | flops 7519862784 | bytes 15204352 | tf_op jit(solution)/shard_map/dot_general | solution.py:589
  109.8 3.5 %fusion.7 = bf16[1024,256]{1,0:T(8,128)(2,1)S(1)} fusion(bf16[2048,1792]{1,0:T(8,128)(2,1)} %all-gather.2.cloned.1.call-done.refs_0_, bf16[1792,1024]{1,0:T(8,128)(2,1)} %copy-done.23, s32[]{:T(128)S(6)} %select_n.69), kind=kOutput, calls=%fused_computation.13 | convolution fusion | flops 939786240 | bytes 5111812 | tf_op jit(solution)/shard_map/dot_general | solution.py:589
  114.3 2.4 %fusion.4 = bf16[1024,256]{1,0:T(8,128)(2,1)S(1)} fusion(bf16[2048,1792]{1,0:T(8,128)(2,1)S(1)} %copy-done.5, bf16[1792,1024]{1,0:T(8,128)(2,1)} %copy-done.23, s32[]{:T(128)S(6)} %select_n.69), kind=kOutput, calls=%fused_computation.12 | convolution fusion | flops 939786240 | bytes 5111812 | tf_op jit(solution)/shard_map/dot_general | solution.py:589
  126.0 3.2 %convolution_convert_fusion.3.refs_5_ = bf16[1792,256]{1,0:T(8,128)(2,1)} fusion(bf16[2048,1792]{1,0:T(8,128)(2,1)S(1)} %shard_map.125, bf16[2048,1024]{1,0:T(8,128)(2,1)S(1)} %copy-done.8, s32[]{:T(128)S(6)} %select_n.74), kind=kOutput, calls=%fused_computation.7 | convolution fusion | flops 1879506944 | bytes 9306116 | tf_op jit(solution)/shard_map/dot_general | solution.py:589
  129.7 3.0 %convolution_convert_fusion.4.refs_4_ = bf16[1792,256]{1,0:T(8,128)(2,1)} fusion(bf16[2048,1792]{1,0:T(8,128)(2,1)S(1)} %shard_map.125, bf16[2048,1024]{1,0:T(8,128)(2,1)S(1)} %copy-done.8, s32[]{:T(128)S(6)} %select_n.72), kind=kOutput, calls=%fused_computation.8 | convolution fusion | flops 1879506944 | bytes 9306116 | tf_op jit(solution)/shard_map/dot_general | solution.py:589
  134.4 2.6 %collective-permute-start.16 = (bf16[2048,256]{1,0:T(8,128)(2,1)}, bf16[2048,256]{1,0:T(8,128)(2,1)}, u32[]{:S(2)}, u32[]{:S(2)}) collective-permute-start(bf16[2048,256]{1,0:T(8,128)(2,1)} %get-tuple-element.53), channel_id=1, source_target_pairs={{0,6},{1,7},{2,0},{3,1},{4,2},{5,3},{6,4},{7,5},{8,14},{9,15},{10,... | collective-permute-start | bytes 3145736 | tf_op jit(solution)/shard_map/ppermute | solution.py:101
  137.0 3.1 %convolution_convert_fusion.1 = bf16[1792,256]{1,0:T(8,128)(2,1)} fusion(bf16[2048,1792]{1,0:T(8,128)(2,1)S(1)} %shard_map.125, bf16[2048,1024]{1,0:T(8,128)(2,1)S(1)} %copy-done.8, s32[]{:T(128)S(6)} %select_n.78), kind=kOutput, calls=%fused_computation.5 | convolution fusion | flops 1879506944 | bytes 9306116 | tf_op jit(solution)/shard_map/dot_general | solution.py:589
  143.7 5.5 %convolution_convert_fusion.2.refs_0_ = bf16[1792,256]{1,0:T(8,128)(2,1)S(1)} fusion(bf16[2048,1792]{1,0:T(8,128)(2,1)} %copy-done.6, bf16[2048,1024]{1,0:T(8,128)(2,1)} %copy-done.7, s32[]{:T(128)S(6)} %select_n.76), kind=kOutput, calls=%fused_computation.6 | convolution fusion | flops 1879506944 | bytes 9306116 | tf_op jit(solution)/shard_map/dot_general | solution.py:589
  149.2 9.9 %collective-permute-done.15.refs_2_ = bf16[2048,256]{1,0:T(8,128)(2,1)} collective-permute-done((bf16[2048,256]{1,0:T(8,128)(2,1)}, bf16[2048,256]{1,0:T(8,128)(2,1)}, u32[]{:S(2)}, u32[]{:S(2)}) %collective-permute-start.15) | collective-permute-done | bytes 1048608 | tf_op jit(solution)/shard_map/ppermute | solution.py:101
  159.1 2.8 %shard_map.129 = (bf16[528,256]{1,0:T(8,128)(2,1)}, bf16[528,256]{1,0:T(8,128)(2,1)}, bf16[528,256]{1,0:T(8,128)(2,1)S(1)}, bf16[528,256]{1,0:T(8,128)(2,1)S(1)}) custom-call(s32[8,128]{1,0:T(8,128)S(1)} %copy-done.18, bf16[2048,256]{1,0:T(8,128)(2,1)S(1)} %convolution_convert_fusion.7.refs_1_, bf16[2048,256]{1,0:T(8,128)(2,1)} %collective-permute-done.15.refs_2_, ...), custom_call_target="tpu_custom_call" | custom-call | tf_op jit(solution)/shard_map/pallas_call | solution.py:117
  162.0 6.7 %collective-permute-start.18 = (bf16[528,256]{1,0:T(8,128)(2,1)}, bf16[528,256]{1,0:T(8,128)(2,1)S(1)}, u32[]{:S(2)}, u32[]{:S(2)}) collective-permute-start(bf16[528,256]{1,0:T(8,128)(2,1)} %get-tuple-element.55.refs_4_), channel_id=1, source_target_pairs={{8,0},{24,1},{10,2},{26,3},{12,4},{28,5},{14,6},{30,7},{11,8},{15,... | collective-permute-start | bytes 811016 | tf_op jit(solution)/shard_map/ppermute | solution.py:101
  168.7 3.9 %shard_map.130 = (bf16[1792,256]{1,0:T(8,128)(2,1)}, f32[8,128]{1,0:T(8,128)S(1)}) custom-call(bf16[1792,256]{1,0:T(8,128)(2,1)S(1)} %convolution_convert_fusion.2.refs_0_, bf16[1792,256]{1,0:T(8,128)(2,1)} %collective-permute-done.20.refs_1_, bf16[1792,256]{1,0:T(8,128)(2,1)} %collective-permute-done.21.refs_2_, ...), custom_call_target="tpu_custom_call" | custom-call | tf_op jit(solution)/shard_map/pallas_call | solution.py:117
  172.6 9.2 %collective-permute-start.23 = (bf16[528,256]{1,0:T(8,128)(2,1)S(1)}, bf16[528,256]{1,0:T(8,128)(2,1)S(1)}, u32[]{:S(2)}, u32[]{:S(2)}) collective-permute-start(bf16[528,256]{1,0:T(8,128)(2,1)S(1)} %get-tuple-element.60), channel_id=1, source_target_pairs={{0,0},{16,1},{2,2},{18,3},{4,4},{20,5},{6,6},{22,7},{8,8},{24,9},{... | collective-permute-start | bytes 811016 | tf_op jit(solution)/shard_map/ppermute | solution.py:101
  191.1 6.3 %collective-permute-done.19.refs_1_ = bf16[528,256]{1,0:T(8,128)(2,1)S(1)} collective-permute-done((bf16[528,256]{1,0:T(8,128)(2,1)}, bf16[528,256]{1,0:T(8,128)(2,1)S(1)}, u32[]{:S(2)}, u32[]{:S(2)}) %collective-permute-start.19) | collective-permute-done | bytes 270368 | tf_op jit(solution)/shard_map/ppermute | solution.py:101
  (118 shorter events, 57.5 us)
Async XLA Ops:
  7.2 102.6 %all-gather.2.cloned.1.call-start = ((), (), s32[]{:S(2)}) async-start(), calls=%async_computation.1 | async-start | bytes 9175040 | tf_op jit(solution)/shard_map/all_gather | solution.py:617
  18.3 24.4 %collective-permute-start.1 = (bf16[528,256]{1,0:T(8,128)(2,1)S(1)}, bf16[528,256]{1,0:T(8,128)(2,1)S(1)}, u32[]{:S(2)}, u32[]{:S(2)}) collective-permute-start(bf16[528,256]{1,0:T(8,128)(2,1)S(1)} %get-tuple-element.43), channel_id=1, source_target_pairs={{0,8},{1,24},{2,10},{3,26},{4,12},{5,28},{6,14},{7,30},{8,11},{9,1... | collective-permute-start | bytes 811016 | tf_op jit(solution)/shard_map/ppermute | solution.py:101
  23.7 23.0 %collective-permute-start.2 = (bf16[528,256]{1,0:T(8,128)(2,1)S(1)}, bf16[528,256]{1,0:T(8,128)(2,1)S(1)}, u32[]{:S(2)}, u32[]{:S(2)}) collective-permute-start(bf16[528,256]{1,0:T(8,128)(2,1)S(1)} %get-tuple-element.44), channel_id=1, source_target_pairs={{0,3},{1,7},{2,35},{3,39},{4,67},{5,71},{6,99},{7,103},{8,9},{9,13... | collective-permute-start | bytes 811016 | tf_op jit(solution)/shard_map/ppermute | solution.py:101
  26.1 20.6 %collective-permute-start.3 = (bf16[528,256]{1,0:T(8,128)(2,1)S(1)}, bf16[528,256]{1,0:T(8,128)(2,1)S(1)}, u32[]{:S(2)}, u32[]{:S(2)}) collective-permute-start(bf16[528,256]{1,0:T(8,128)(2,1)S(1)} %get-tuple-element.45), channel_id=1, source_target_pairs={{0,0},{1,16},{2,2},{3,18},{4,4},{5,20},{6,6},{7,22},{8,8},{9,24},{... | collective-permute-start | bytes 811016 | tf_op jit(solution)/shard_map/ppermute | solution.py:101
  28.1 26.3 %collective-permute-start.4 = (bf16[528,256]{1,0:T(8,128)(2,1)S(1)}, bf16[528,256]{1,0:T(8,128)(2,1)S(1)}, u32[]{:S(2)}, u32[]{:S(2)}) collective-permute-start(bf16[528,256]{1,0:T(8,128)(2,1)S(1)} %get-tuple-element.46), channel_id=1, source_target_pairs={{0,1},{1,5},{2,33},{3,37},{4,65},{5,69},{6,97},{7,101},{8,0},{9,16... | collective-permute-start | bytes 811016 | tf_op jit(solution)/shard_map/ppermute | solution.py:101
  56.3 129.4 %reduce-scatter.2.cloned.1.call-start = ((), (), s32[]{:S(2)}) async-start(), calls=%async_computation.2 | async-start | bytes 9175040 | tf_op jit(solution)/shard_map/reduce_scatter | solution.py:635
  56.4 21.6 %collective-permute-start.12 = (bf16[2048,256]{1,0:T(8,128)(2,1)S(1)}, bf16[2048,256]{1,0:T(8,128)(2,1)S(1)}, u32[]{:S(2)}, u32[]{:S(2)}) collective-permute-start(bf16[2048,256]{1,0:T(8,128)(2,1)S(1)} %get-tuple-element.47.refs_1_.refs_2_.refs_0_), channel_id=1, source_target_pairs={{0,2},{1,3},{2,4},{3,5},{4,6},{5,7},{6,0},{7,1},{8,10},{9,11},{10,... | collective-permute-start | bytes 3145736 | tf_op jit(solution)/shard_map/ppermute | solution.py:101
  56.4 21.6 %collective-permute-start.11 = (bf16[2048,256]{1,0:T(8,128)(2,1)S(1)}, bf16[2048,256]{1,0:T(8,128)(2,1)S(1)}, u32[]{:S(2)}, u32[]{:S(2)}) collective-permute-start(bf16[2048,256]{1,0:T(8,128)(2,1)S(1)} %get-tuple-element.47.refs_1_.refs_2_.refs_0_), channel_id=1, source_target_pairs={{0,6},{1,7},{2,0},{3,1},{4,2},{5,3},{6,4},{7,5},{8,14},{9,15},{10,... | collective-permute-start | bytes 3145736 | tf_op jit(solution)/shard_map/ppermute | solution.py:101
  60.4 20.4 %collective-permute-start.5 = (bf16[1808,256]{1,0:T(8,128)(2,1)S(1)}, bf16[1808,256]{1,0:T(8,128)(2,1)S(1)}, u32[]{:S(2)}, u32[]{:S(2)}) collective-permute-start(bf16[1808,256]{1,0:T(8,128)(2,1)S(1)} %shard_map.123.refs_0_.refs_5_), channel_id=1, source_target_pairs={{0,96},{1,25},{2,98},{3,27},{4,100},{5,29},{6,102},{7,31},{8,104},... | collective-permute-start | bytes 2777096 | tf_op jit(solution)/shard_map/ppermute | solution.py:101
  60.5 21.1 %collective-permute-start.6 = (bf16[1808,256]{1,0:T(8,128)(2,1)S(1)}, bf16[1808,256]{1,0:T(8,128)(2,1)S(1)}, u32[]{:S(2)}, u32[]{:S(2)}) collective-permute-start(bf16[1808,256]{1,0:T(8,128)(2,1)S(1)} %shard_map.123.refs_0_.refs_5_), channel_id=1, source_target_pairs={{0,32},{1,9},{2,34},{3,11},{4,36},{5,13},{6,38},{7,15},{8,40},{9,1... | collective-permute-start | bytes 2777096 | tf_op jit(solution)/shard_map/ppermute | solution.py:101
  78.0 17.0 %collective-permute-start.13 = (bf16[1024,256]{1,0:T(8,128)(2,1)S(1)}, bf16[1024,256]{1,0:T(8,128)(2,1)S(1)}, u32[]{:S(2)}, u32[]{:S(2)}) collective-permute-start(bf16[1024,256]{1,0:T(8,128)(2,1)S(1)} %slice.28), channel_id=1, source_target_pairs={{0,2},{1,3},{2,4},{3,5},{4,6},{5,7},{6,0},{7,1},{8,10},{9,11},{10,... | collective-permute-start | bytes 1572872 | tf_op jit(solution)/shard_map/ppermute | solution.py:101
  78.1 16.8 %collective-permute-start.14 = (bf16[1024,256]{1,0:T(8,128)(2,1)S(1)}, bf16[1024,256]{1,0:T(8,128)(2,1)S(1)}, u32[]{:S(2)}, u32[]{:S(2)}) collective-permute-start(bf16[1024,256]{1,0:T(8,128)(2,1)S(1)} %slice.29), channel_id=1, source_target_pairs={{0,6},{1,7},{2,0},{3,1},{4,2},{5,3},{6,4},{7,5},{8,14},{9,15},{10,... | collective-permute-start | bytes 1572872 | tf_op jit(solution)/shard_map/ppermute | solution.py:101
  80.9 13.4 %collective-permute-start.8 = (bf16[912,256]{1,0:T(8,128)(2,1)S(1)}, bf16[912,256]{1,0:T(8,128)(2,1)S(1)}, u32[]{:S(2)}, u32[]{:S(2)}) collective-permute-start(bf16[912,256]{1,0:T(8,128)(2,1)S(1)} %slice.25), channel_id=1, source_target_pairs={{0,96},{1,25},{2,98},{3,27},{4,100},{5,29},{6,102},{7,31},{8,104},... | collective-permute-start | bytes 1400840 | tf_op jit(solution)/shard_map/ppermute | solution.py:101
  107.8 34.1 %collective-permute-start.17 = (f32[8,128]{1,0:T(8,128)S(1)}, f32[8,128]{1,0:T(8,128)S(1)}, u32[]{:S(2)}, u32[]{:S(2)}) collective-permute-start(f32[8,128]{1,0:T(8,128)S(1)} %get-tuple-element.54), channel_id=1, source_target_pairs={{0,1},{1,0},{2,3},{3,2},{4,5},{5,4},{6,7},{7,6},{8,9},{9,8},{10,11... | collective-permute-start | bytes 12296 | tf_op jit(solution)/shard_map/ppermute | solution.py:101
  113.4 19.4 %collective-permute-start.10 = (bf16[1024,256]{1,0:T(8,128)(2,1)S(1)}, bf16[1024,256]{1,0:T(8,128)(2,1)S(1)}, u32[]{:S(2)}, u32[]{:S(2)}) collective-permute-start(bf16[1024,256]{1,0:T(8,128)(2,1)S(1)} %fusion.7), channel_id=1, source_target_pairs={{0,6},{1,7},{2,0},{3,1},{4,2},{5,3},{6,4},{7,5},{8,14},{9,15},{10,... | collective-permute-start | bytes 1572872 | tf_op jit(solution)/shard_map/ppermute | solution.py:101
  116.7 16.1 %collective-permute-start.9 = (bf16[1024,256]{1,0:T(8,128)(2,1)S(1)}, bf16[1024,256]{1,0:T(8,128)(2,1)S(1)}, u32[]{:S(2)}, u32[]{:S(2)}) collective-permute-start(bf16[1024,256]{1,0:T(8,128)(2,1)S(1)} %fusion.4), channel_id=1, source_target_pairs={{0,2},{1,3},{2,4},{3,5},{4,6},{5,7},{6,0},{7,1},{8,10},{9,11},{10,... | collective-permute-start | bytes 1572872 | tf_op jit(solution)/shard_map/ppermute | solution.py:101
  129.2 39.5 %collective-permute-start.22 = (bf16[1792,256]{1,0:T(8,128)(2,1)}, bf16[1792,256]{1,0:T(8,128)(2,1)}, u32[]{:S(2)}, u32[]{:S(2)}) collective-permute-start(bf16[1792,256]{1,0:T(8,128)(2,1)} %convolution_convert_fusion.3.refs_5_), channel_id=1, source_target_pairs={{0,96},{1,25},{2,98},{3,27},{4,100},{5,29},{6,102},{7,31},{8,104},... | collective-permute-start | bytes 2752520 | tf_op jit(solution)/shard_map/ppermute | solution.py:101
  134.3 24.8 %collective-permute-start.15 = (bf16[2048,256]{1,0:T(8,128)(2,1)}, bf16[2048,256]{1,0:T(8,128)(2,1)}, u32[]{:S(2)}, u32[]{:S(2)}) collective-permute-start(bf16[2048,256]{1,0:T(8,128)(2,1)} %get-tuple-element.52), channel_id=1, source_target_pairs={{0,2},{1,3},{2,4},{3,5},{4,6},{5,7},{6,0},{7,1},{8,10},{9,11},{10,... | collective-permute-start | bytes 3145736 | tf_op jit(solution)/shard_map/ppermute | solution.py:101
  134.4 24.7 %collective-permute-start.16 = (bf16[2048,256]{1,0:T(8,128)(2,1)}, bf16[2048,256]{1,0:T(8,128)(2,1)}, u32[]{:S(2)}, u32[]{:S(2)}) collective-permute-start(bf16[2048,256]{1,0:T(8,128)(2,1)} %get-tuple-element.53), channel_id=1, source_target_pairs={{0,6},{1,7},{2,0},{3,1},{4,2},{5,3},{6,4},{7,5},{8,14},{9,15},{10,... | collective-permute-start | bytes 3145736 | tf_op jit(solution)/shard_map/ppermute | solution.py:101
  140.1 28.6 %collective-permute-start.20 = (bf16[1792,256]{1,0:T(8,128)(2,1)}, bf16[1792,256]{1,0:T(8,128)(2,1)}, u32[]{:S(2)}, u32[]{:S(2)}) collective-permute-start(bf16[1792,256]{1,0:T(8,128)(2,1)} %convolution_convert_fusion.1), channel_id=1, source_target_pairs={{0,32},{1,9},{2,34},{3,11},{4,36},{5,13},{6,38},{7,15},{8,40},{9,1... | collective-permute-start | bytes 2752520 | tf_op jit(solution)/shard_map/ppermute | solution.py:101
  141.9 26.8 %collective-permute-start.21 = (bf16[1792,256]{1,0:T(8,128)(2,1)}, bf16[1792,256]{1,0:T(8,128)(2,1)}, u32[]{:S(2)}, u32[]{:S(2)}) collective-permute-start(bf16[1792,256]{1,0:T(8,128)(2,1)} %convolution_convert_fusion.4.refs_4_), channel_id=1, source_target_pairs={{0,64},{1,17},{2,66},{3,19},{4,68},{5,21},{6,70},{7,23},{8,72},{9,... | collective-permute-start | bytes 2752520 | tf_op jit(solution)/shard_map/ppermute | solution.py:101
  162.0 29.1 %collective-permute-start.18 = (bf16[528,256]{1,0:T(8,128)(2,1)}, bf16[528,256]{1,0:T(8,128)(2,1)S(1)}, u32[]{:S(2)}, u32[]{:S(2)}) collective-permute-start(bf16[528,256]{1,0:T(8,128)(2,1)} %get-tuple-element.55.refs_4_), channel_id=1, source_target_pairs={{8,0},{24,1},{10,2},{26,3},{12,4},{28,5},{14,6},{30,7},{11,8},{15,... | collective-permute-start | bytes 811016 | tf_op jit(solution)/shard_map/ppermute | solution.py:101
  172.6 18.4 %collective-permute-start.23 = (bf16[528,256]{1,0:T(8,128)(2,1)S(1)}, bf16[528,256]{1,0:T(8,128)(2,1)S(1)}, u32[]{:S(2)}, u32[]{:S(2)}) collective-permute-start(bf16[528,256]{1,0:T(8,128)(2,1)S(1)} %get-tuple-element.60), channel_id=1, source_target_pairs={{0,0},{16,1},{2,2},{18,3},{4,4},{20,5},{6,6},{22,7},{8,8},{24,9},{... | collective-permute-start | bytes 811016 | tf_op jit(solution)/shard_map/ppermute | solution.py:101
  183.7 13.6 %collective-permute-start.19 = (bf16[528,256]{1,0:T(8,128)(2,1)}, bf16[528,256]{1,0:T(8,128)(2,1)S(1)}, u32[]{:S(2)}, u32[]{:S(2)}) collective-permute-start(bf16[528,256]{1,0:T(8,128)(2,1)} %get-tuple-element.56), channel_id=1, source_target_pairs={{3,0},{7,1},{35,2},{39,3},{67,4},{71,5},{99,6},{103,7},{9,8},{13,9... | collective-permute-start | bytes 811016 | tf_op jit(solution)/shard_map/ppermute | solution.py:101
  (29 other events, 195.3 us)
Sparse Core Ops, SparseCore 0:
  56.4 47.6 all-gather.1
  107.8 56.5 reduce-scatter.1

commit v6 on v5

--- a/solution.py
+++ b/solution.py
@@ -638,13 +638,14 @@
     far = block_of(weight, z + 2)
     top = send(dot(act[:half], far, ((1,), (0,))), hidden_ring(1))
     bottom = send(dot(act[half:], far, ((1,), (0,))), hidden_ring(-1))
-    mixed = [dot(act, block_of(weight, z + step), ((1,), (0,))) for step in (0, 1, 3)]
+    mixed = [dot(act, block_of(weight, z + step), ((1,), (0,))) for step in (1, 3)]
     (act,) = gate((act,), mixed)
+    own = dot(act, block_of(weight, z), ((1,), (0,)))
     weight_grad = [
         dot(act, block_of(tile, feature_place + step), ((0,), (0,))) for step in range(N)
     ]
-    after, before = add_halves(mixed[1], mixed[2], top, bottom, weight_grad[2:])
-    mixed = (mixed[0], send(after, hidden_ring(1)), send(before, hidden_ring(-1)))
+    after, before = add_halves(*mixed, top, bottom, weight_grad[2:])
+    mixed = (own, send(after, hidden_ring(1)), send(before, hidden_ring(-1)))
     blocks = list(return_blocks(mixed, peaks))
     weight_grad, added = add(ring_exchange(weight_grad, feature_ring), blocks[:1])
     grad_gate, grad_up, finished = finish(slope, silu, grad_act)

time: 207 us -> 204 us (0.986)
  the two profiles are of different devices: /device:TPU:23 before, /device:TPU:15 now
where the time goes in v6:
time: 204 us
  waiting for transfers between devices  68.5 us (34%)
  starting transfers between devices  53.9 us (26%)
  matrix products  31.3 us (15%)
  local copies, waits for them, and re-layouts  19.9 us (10%)
  Pallas kernels  15.5 us (8%)
  between operations  14.5 us (7%)
    ppermute x26, waiting for transfers between devices, send(): return lax.ppermute(value, AXES, pairs)  68.4 us
    ppermute x26, starting transfers between devices, send(): return lax.ppermute(value, AXES, pairs)  53.9 us
    dot_general x10, matrix products, dot(): lax.dot_general(left, right, (dims, ((), ())), preferred_element_type=F32)  31.3 us
    unnamed x48, local copies, waits for them, and re-layouts  19.8 us
    pallas_call x19, Pallas kernels, call(): pl.pallas_call(body, out_shape=out_shape, in_specs=list(in_specs) + [ANYW...  15.5 us
  transfers between devices with their start and end apart: 28, of which 8 were waited for; matrix products, arithmetic and copies ran while one was open for 15% of the time, Pallas kernels for 5%

profile of v6, /device:TPU:15, one launch (start us, length us, event | category | flops | bytes accessed | tf_op | source)
XLA Modules:
  0.0 203.7 jit_solution(15474293381107708089)
XLA Ops:
  18.3 4.1 %collective-permute-start.1 = (bf16[528,256]{1,0:T(8,128)(2,1)S(1)}, bf16[528,256]{1,0:T(8,128)(2,1)S(1)}, u32[]{:S(2)}, u32[]{:S(2)}) collective-permute-start(bf16[528,256]{1,0:T(8,128)(2,1)S(1)} %get-tuple-element.43), channel_id=1, source_target_pairs={{0,8},{1,24},{2,10},{3,26},{4,12},{5,28},{6,14},{7,30},{8,11},{9,1... | collective-permute-start | bytes 811016 | tf_op jit(solution)/shard_map/ppermute | solution.py:101
  24.4 7.0 %collective-permute-start.3 = (bf16[528,256]{1,0:T(8,128)(2,1)S(1)}, bf16[528,256]{1,0:T(8,128)(2,1)S(1)}, u32[]{:S(2)}, u32[]{:S(2)}) collective-permute-start(bf16[528,256]{1,0:T(8,128)(2,1)S(1)} %get-tuple-element.45), channel_id=1, source_target_pairs={{0,0},{1,16},{2,2},{3,18},{4,4},{5,20},{6,6},{7,22},{8,8},{9,24},{... | collective-permute-start | bytes 811016 | tf_op jit(solution)/shard_map/ppermute | solution.py:101
  31.4 2.8 %collective-permute-start.4 = (bf16[528,256]{1,0:T(8,128)(2,1)S(1)}, bf16[528,256]{1,0:T(8,128)(2,1)S(1)}, u32[]{:S(2)}, u32[]{:S(2)}) collective-permute-start(bf16[528,256]{1,0:T(8,128)(2,1)S(1)} %get-tuple-element.46), channel_id=1, source_target_pairs={{0,1},{1,5},{2,33},{3,37},{4,65},{5,69},{6,97},{7,101},{8,0},{9,16... | collective-permute-start | bytes 811016 | tf_op jit(solution)/shard_map/ppermute | solution.py:101
  34.2 16.7 %collective-permute-done.2.refs_2_ = bf16[528,256]{1,0:T(8,128)(2,1)S(1)} collective-permute-done((bf16[528,256]{1,0:T(8,128)(2,1)S(1)}, bf16[528,256]{1,0:T(8,128)(2,1)S(1)}, u32[]{:S(2)}, u32[]{:S(2)}) %collective-permute-start.2) | collective-permute-done | bytes 270368 | tf_op jit(solution)/shard_map/ppermute | solution.py:101
  53.1 2.7 %collective-permute-start.11 = (bf16[2048,256]{1,0:T(8,128)(2,1)S(1)}, bf16[2048,256]{1,0:T(8,128)(2,1)S(1)}, u32[]{:S(2)}, u32[]{:S(2)}) collective-permute-start(bf16[2048,256]{1,0:T(8,128)(2,1)S(1)} %get-tuple-element.47.refs_1_.refs_2_.refs_0_), channel_id=1, source_target_pairs={{0,6},{1,7},{2,0},{3,1},{4,2},{5,3},{6,4},{7,5},{8,14},{9,15},{10,... | collective-permute-start | bytes 3145736 | tf_op jit(solution)/shard_map/ppermute | solution.py:101
  57.1 4.7 %collective-permute-start.6 = (bf16[1808,256]{1,0:T(8,128)(2,1)S(1)}, bf16[1808,256]{1,0:T(8,128)(2,1)S(1)}, u32[]{:S(2)}, u32[]{:S(2)}) collective-permute-start(bf16[1808,256]{1,0:T(8,128)(2,1)S(1)} %shard_map.123.refs_0_.refs_5_), channel_id=1, source_target_pairs={{0,32},{1,9},{2,34},{3,11},{4,36},{5,13},{6,38},{7,15},{8,40},{9,1... | collective-permute-start | bytes 2777096 | tf_op jit(solution)/shard_map/ppermute | solution.py:101
  61.8 16.4 %collective-permute-done.12.refs_4_ = bf16[2048,256]{1,0:T(8,128)(2,1)S(1)} collective-permute-done((bf16[2048,256]{1,0:T(8,128)(2,1)S(1)}, bf16[2048,256]{1,0:T(8,128)(2,1)S(1)}, u32[]{:S(2)}, u32[]{:S(2)}) %collective-permute-start.12) | collective-permute-done | bytes 1048608 | tf_op jit(solution)/shard_map/ppermute | solution.py:101
  78.4 2.9 %collective-permute-start.14 = (bf16[1024,256]{1,0:T(8,128)(2,1)S(1)}, bf16[1024,256]{1,0:T(8,128)(2,1)S(1)}, u32[]{:S(2)}, u32[]{:S(2)}) collective-permute-start(bf16[1024,256]{1,0:T(8,128)(2,1)S(1)} %slice.29), channel_id=1, source_target_pairs={{0,6},{1,7},{2,0},{3,1},{4,2},{5,3},{6,4},{7,5},{8,14},{9,15},{10,... | collective-permute-start | bytes 1572872 | tf_op jit(solution)/shard_map/ppermute | solution.py:101
  87.1 8.8 %collective-permute-done.7.refs_2_ = bf16[896,256]{1,0:T(8,128)(2,1)S(1)} collective-permute-done((bf16[896,256]{1,0:T(8,128)(2,1)S(1)}, bf16[896,256]{1,0:T(8,128)(2,1)S(1)}, u32[]{:S(2)}, u32[]{:S(2)}) %collective-permute-start.7) | collective-permute-done | bytes 458784 | tf_op jit(solution)/shard_map/ppermute | solution.py:101
  99.6 9.7 %convolution_convert_fusion = bf16[2048,1792]{1,0:T(8,128)(2,1)} fusion(bf16[2048,1024]{1,0:T(8,128)(2,1)S(1)} %shard_map.127, bf16[1792,1024]{1,0:T(8,128)(2,1)S(1)} %get-tuple-element.50), kind=kOutput, calls=%fused_computation | convolution fusion | flops 7519862784 | bytes 15204352 | tf_op jit(solution)/shard_map/dot_general | solution.py:589
  111.0 3.5 %fusion.4 = bf16[1024,256]{1,0:T(8,128)(2,1)S(1)} fusion(bf16[2048,1792]{1,0:T(8,128)(2,1)} %all-gather.2.cloned.1.call-done.refs_0_, bf16[1792,1024]{1,0:T(8,128)(2,1)} %copy-done.22, s32[]{:T(128)S(6)} %select_n.69), kind=kOutput, calls=%fused_computation.12 | convolution fusion | flops 939786240 | bytes 5111812 | tf_op jit(solution)/shard_map/dot_general | solution.py:589
  115.4 2.4 %fusion.7 = bf16[1024,256]{1,0:T(8,128)(2,1)S(1)} fusion(bf16[2048,1792]{1,0:T(8,128)(2,1)S(1)} %copy-done.5, bf16[1792,1024]{1,0:T(8,128)(2,1)} %copy-done.22, s32[]{:T(128)S(6)} %select_n.69), kind=kOutput, calls=%fused_computation.13 | convolution fusion | flops 939786240 | bytes 5111812 | tf_op jit(solution)/shard_map/dot_general | solution.py:589
  124.3 2.3 %copy-done.7 = bf16[2048,1024]{1,0:T(8,128)(2,1)S(1)} copy-done((bf16[2048,1024]{1,0:T(8,128)(2,1)S(1)}, bf16[2048,1024]{1,0:T(8,128)(2,1)}, u32[]{:S(2)}) %copy-start.7) | copy-done | bytes 4194328
  126.6 2.3 %convolution_convert_fusion.1 = bf16[1792,256]{1,0:T(8,128)(2,1)S(1)} fusion(bf16[2048,1792]{1,0:T(8,128)(2,1)S(1)} %shard_map.125, bf16[2048,1024]{1,0:T(8,128)(2,1)S(1)} %copy-done.7, s32[]{:T(128)S(6)} %select_n.78), kind=kOutput, calls=%fused_computation.5 | convolution fusion | flops 1879506944 | bytes 9306116 | tf_op jit(solution)/shard_map/dot_general | solution.py:589
  129.8 2.2 %convolution_convert_fusion.4.refs_4_ = bf16[1792,256]{1,0:T(8,128)(2,1)S(1)} fusion(bf16[2048,1792]{1,0:T(8,128)(2,1)S(1)} %shard_map.125, bf16[2048,1024]{1,0:T(8,128)(2,1)S(1)} %copy-done.7, s32[]{:T(128)S(6)} %select_n.72), kind=kOutput, calls=%fused_computation.8 | convolution fusion | flops 1879506944 | bytes 9306116 | tf_op jit(solution)/shard_map/dot_general | solution.py:589
  132.1 3.2 %collective-permute-start.21 = (bf16[1792,256]{1,0:T(8,128)(2,1)S(1)}, bf16[1792,256]{1,0:T(8,128)(2,1)S(1)}, u32[]{:S(2)}, u32[]{:S(2)}) collective-permute-start(bf16[1792,256]{1,0:T(8,128)(2,1)S(1)} %convolution_convert_fusion.4.refs_4_), channel_id=1, source_target_pairs={{0,64},{1,17},{2,66},{3,19},{4,68},{5,21},{6,70},{7,23},{8,72},{9,... | collective-permute-start | bytes 2752520 | tf_op jit(solution)/shard_map/ppermute | solution.py:101
  138.9 2.7 %collective-permute-start.16 = (bf16[2048,256]{1,0:T(8,128)(2,1)S(1)}, bf16[2048,256]{1,0:T(8,128)(2,1)S(1)}, u32[]{:S(2)}, u32[]{:S(2)}) collective-permute-start(bf16[2048,256]{1,0:T(8,128)(2,1)S(1)} %get-tuple-element.53), channel_id=1, source_target_pairs={{0,6},{1,7},{2,0},{3,1},{4,2},{5,3},{6,4},{7,5},{8,14},{9,15},{10,... | collective-permute-start | bytes 3145736 | tf_op jit(solution)/shard_map/ppermute | solution.py:101
  143.8 2.3 %convolution_convert_fusion.2.refs_0_ = bf16[1792,256]{1,0:T(8,128)(2,1)S(1)} fusion(bf16[2048,1792]{1,0:T(8,128)(2,1)S(1)} %shard_map.125, bf16[2048,1024]{1,0:T(8,128)(2,1)S(1)} %copy-done.7, s32[]{:T(128)S(6)} %select_n.76), kind=kOutput, calls=%fused_computation.6 | convolution fusion | flops 1879506944 | bytes 9306116 | tf_op jit(solution)/shard_map/dot_general | solution.py:589
  146.1 18.6 %collective-permute-done.15.refs_2_ = bf16[2048,256]{1,0:T(8,128)(2,1)S(1)} collective-permute-done((bf16[2048,256]{1,0:T(8,128)(2,1)S(1)}, bf16[2048,256]{1,0:T(8,128)(2,1)S(1)}, u32[]{:S(2)}, u32[]{:S(2)}) %collective-permute-start.15) | collective-permute-done | bytes 1048608 | tf_op jit(solution)/shard_map/ppermute | solution.py:101
  166.5 3.9 %collective-permute-start.18 = (bf16[528,256]{1,0:T(8,128)(2,1)}, bf16[528,256]{1,0:T(8,128)(2,1)S(1)}, u32[]{:S(2)}, u32[]{:S(2)}) collective-permute-start(bf16[528,256]{1,0:T(8,128)(2,1)} %get-tuple-element.55.refs_4_), channel_id=1, source_target_pairs={{8,0},{24,1},{10,2},{26,3},{12,4},{28,5},{14,6},{30,7},{11,8},{15,... | collective-permute-start | bytes 811016 | tf_op jit(solution)/shard_map/ppermute | solution.py:101
  170.4 6.5 %collective-permute-start.19 = (bf16[528,256]{1,0:T(8,128)(2,1)}, bf16[528,256]{1,0:T(8,128)(2,1)S(1)}, u32[]{:S(2)}, u32[]{:S(2)}) collective-permute-start(bf16[528,256]{1,0:T(8,128)(2,1)} %get-tuple-element.56), channel_id=1, source_target_pairs={{3,0},{7,1},{35,2},{39,3},{67,4},{71,5},{99,6},{103,7},{9,8},{13,9... | collective-permute-start | bytes 811016 | tf_op jit(solution)/shard_map/ppermute | solution.py:101
  185.8 2.4 %shard_map.132 = (bf16[512,1792]{1,0:T(8,128)(2,1)}, bf16[512,1792]{1,0:T(8,128)(2,1)}, f32[8,128]{1,0:T(8,128)S(1)}) custom-call(bf16[512,1792]{1,0:T(8,128)(2,1)S(1)} %copy-done.9, bf16[512,1792]{1,0:T(8,128)(2,1)S(1)} %copy-done.11, bf16[512,1792]{1,0:T(8,128)(2,1)S(1)} %copy-done.12), custom_call_target="tpu_custom_call" | custom-call | tf_op jit(solution)/shard_map/pallas_call | solution.py:117
  188.1 4.0 %collective-permute-done.23.refs_2_ = bf16[528,256]{1,0:T(8,128)(2,1)S(1)} collective-permute-done((bf16[528,256]{1,0:T(8,128)(2,1)S(1)}, bf16[528,256]{1,0:T(8,128)(2,1)S(1)}, u32[]{:S(2)}, u32[]{:S(2)}) %collective-permute-start.23) | collective-permute-done | bytes 270368 | tf_op jit(solution)/shard_map/ppermute | solution.py:101
  192.1 2.2 %collective-permute-done.24.refs_3_ = bf16[528,256]{1,0:T(8,128)(2,1)S(1)} collective-permute-done((bf16[528,256]{1,0:T(8,128)(2,1)S(1)}, bf16[528,256]{1,0:T(8,128)(2,1)S(1)}, u32[]{:S(2)}, u32[]{:S(2)}) %collective-permute-start.24) | collective-permute-done | bytes 270368 | tf_op jit(solution)/shard_map/ppermute | solution.py:101
  (116 shorter events, 54.8 us)
Async XLA Ops:
  7.2 103.8 %all-gather.2.cloned.1.call-start = ((), (), s32[]{:S(2)}) async-start(), calls=%async_computation.1 | async-start | bytes 9175040 | tf_op jit(solution)/shard_map/all_gather | solution.py:617
  18.3 15.9 %collective-permute-start.1 = (bf16[528,256]{1,0:T(8,128)(2,1)S(1)}, bf16[528,256]{1,0:T(8,128)(2,1)S(1)}, u32[]{:S(2)}, u32[]{:S(2)}) collective-permute-start(bf16[528,256]{1,0:T(8,128)(2,1)S(1)} %get-tuple-element.43), channel_id=1, source_target_pairs={{0,8},{1,24},{2,10},{3,26},{4,12},{5,28},{6,14},{7,30},{8,11},{9,1... | collective-permute-start | bytes 811016 | tf_op jit(solution)/shard_map/ppermute | solution.py:101
  22.4 28.5 %collective-permute-start.2 = (bf16[528,256]{1,0:T(8,128)(2,1)S(1)}, bf16[528,256]{1,0:T(8,128)(2,1)S(1)}, u32[]{:S(2)}, u32[]{:S(2)}) collective-permute-start(bf16[528,256]{1,0:T(8,128)(2,1)S(1)} %get-tuple-element.44), channel_id=1, source_target_pairs={{0,3},{1,7},{2,35},{3,39},{4,67},{5,71},{6,99},{7,103},{8,9},{9,13... | collective-permute-start | bytes 811016 | tf_op jit(solution)/shard_map/ppermute | solution.py:101
  24.4 26.6 %collective-permute-start.3 = (bf16[528,256]{1,0:T(8,128)(2,1)S(1)}, bf16[528,256]{1,0:T(8,128)(2,1)S(1)}, u32[]{:S(2)}, u32[]{:S(2)}) collective-permute-start(bf16[528,256]{1,0:T(8,128)(2,1)S(1)} %get-tuple-element.45), channel_id=1, source_target_pairs={{0,0},{1,16},{2,2},{3,18},{4,4},{5,20},{6,6},{7,22},{8,8},{9,24},{... | collective-permute-start | bytes 811016 | tf_op jit(solution)/shard_map/ppermute | solution.py:101
  31.4 19.6 %collective-permute-start.4 = (bf16[528,256]{1,0:T(8,128)(2,1)S(1)}, bf16[528,256]{1,0:T(8,128)(2,1)S(1)}, u32[]{:S(2)}, u32[]{:S(2)}) collective-permute-start(bf16[528,256]{1,0:T(8,128)(2,1)S(1)} %get-tuple-element.46), channel_id=1, source_target_pairs={{0,1},{1,5},{2,33},{3,37},{4,65},{5,69},{6,97},{7,101},{8,0},{9,16... | collective-permute-start | bytes 811016 | tf_op jit(solution)/shard_map/ppermute | solution.py:101
  52.9 129.8 %reduce-scatter.2.cloned.1.call-start = ((), (), s32[]{:S(2)}) async-start(), calls=%async_computation.2 | async-start | bytes 9175040 | tf_op jit(solution)/shard_map/reduce_scatter | solution.py:635
  53.0 25.2 %collective-permute-start.12 = (bf16[2048,256]{1,0:T(8,128)(2,1)S(1)}, bf16[2048,256]{1,0:T(8,128)(2,1)S(1)}, u32[]{:S(2)}, u32[]{:S(2)}) collective-permute-start(bf16[2048,256]{1,0:T(8,128)(2,1)S(1)} %get-tuple-element.47.refs_1_.refs_2_.refs_0_), channel_id=1, source_target_pairs={{0,2},{1,3},{2,4},{3,5},{4,6},{5,7},{6,0},{7,1},{8,10},{9,11},{10,... | collective-permute-start | bytes 3145736 | tf_op jit(solution)/shard_map/ppermute | solution.py:101
  53.1 25.2 %collective-permute-start.11 = (bf16[2048,256]{1,0:T(8,128)(2,1)S(1)}, bf16[2048,256]{1,0:T(8,128)(2,1)S(1)}, u32[]{:S(2)}, u32[]{:S(2)}) collective-permute-start(bf16[2048,256]{1,0:T(8,128)(2,1)S(1)} %get-tuple-element.47.refs_1_.refs_2_.refs_0_), channel_id=1, source_target_pairs={{0,6},{1,7},{2,0},{3,1},{4,2},{5,3},{6,4},{7,5},{8,14},{9,15},{10,... | collective-permute-start | bytes 3145736 | tf_op jit(solution)/shard_map/ppermute | solution.py:101
  57.0 24.2 %collective-permute-start.5 = (bf16[1808,256]{1,0:T(8,128)(2,1)S(1)}, bf16[1808,256]{1,0:T(8,128)(2,1)S(1)}, u32[]{:S(2)}, u32[]{:S(2)}) collective-permute-start(bf16[1808,256]{1,0:T(8,128)(2,1)S(1)} %shard_map.123.refs_0_.refs_5_), channel_id=1, source_target_pairs={{0,96},{1,25},{2,98},{3,27},{4,100},{5,29},{6,102},{7,31},{8,104},... | collective-permute-start | bytes 2777096 | tf_op jit(solution)/shard_map/ppermute | solution.py:101
  57.1 24.3 %collective-permute-start.6 = (bf16[1808,256]{1,0:T(8,128)(2,1)S(1)}, bf16[1808,256]{1,0:T(8,128)(2,1)S(1)}, u32[]{:S(2)}, u32[]{:S(2)}) collective-permute-start(bf16[1808,256]{1,0:T(8,128)(2,1)S(1)} %shard_map.123.refs_0_.refs_5_), channel_id=1, source_target_pairs={{0,32},{1,9},{2,34},{3,11},{4,36},{5,13},{6,38},{7,15},{8,40},{9,1... | collective-permute-start | bytes 2777096 | tf_op jit(solution)/shard_map/ppermute | solution.py:101
  78.2 18.3 %collective-permute-start.13 = (bf16[1024,256]{1,0:T(8,128)(2,1)S(1)}, bf16[1024,256]{1,0:T(8,128)(2,1)S(1)}, u32[]{:S(2)}, u32[]{:S(2)}) collective-permute-start(bf16[1024,256]{1,0:T(8,128)(2,1)S(1)} %slice.28), channel_id=1, source_target_pairs={{0,2},{1,3},{2,4},{3,5},{4,6},{5,7},{6,0},{7,1},{8,10},{9,11},{10,... | collective-permute-start | bytes 1572872 | tf_op jit(solution)/shard_map/ppermute | solution.py:101
  78.4 18.2 %collective-permute-start.14 = (bf16[1024,256]{1,0:T(8,128)(2,1)S(1)}, bf16[1024,256]{1,0:T(8,128)(2,1)S(1)}, u32[]{:S(2)}, u32[]{:S(2)}) collective-permute-start(bf16[1024,256]{1,0:T(8,128)(2,1)S(1)} %slice.29), channel_id=1, source_target_pairs={{0,6},{1,7},{2,0},{3,1},{4,2},{5,3},{6,4},{7,5},{8,14},{9,15},{10,... | collective-permute-start | bytes 1572872 | tf_op jit(solution)/shard_map/ppermute | solution.py:101
  81.3 14.6 %collective-permute-start.8 = (bf16[912,256]{1,0:T(8,128)(2,1)S(1)}, bf16[912,256]{1,0:T(8,128)(2,1)S(1)}, u32[]{:S(2)}, u32[]{:S(2)}) collective-permute-start(bf16[912,256]{1,0:T(8,128)(2,1)S(1)} %slice.25), channel_id=1, source_target_pairs={{0,96},{1,25},{2,98},{3,27},{4,100},{5,29},{6,102},{7,31},{8,104},... | collective-permute-start | bytes 1400840 | tf_op jit(solution)/shard_map/ppermute | solution.py:101
  81.4 14.4 %collective-permute-start.7 = (bf16[896,256]{1,0:T(8,128)(2,1)S(1)}, bf16[896,256]{1,0:T(8,128)(2,1)S(1)}, u32[]{:S(2)}, u32[]{:S(2)}) collective-permute-start(bf16[896,256]{1,0:T(8,128)(2,1)S(1)} %slice.24), channel_id=1, source_target_pairs={{0,32},{1,9},{2,34},{3,11},{4,36},{5,13},{6,38},{7,15},{8,40},{9,1... | collective-permute-start | bytes 1376264 | tf_op jit(solution)/shard_map/ppermute | solution.py:101
  114.5 24.0 %collective-permute-start.9 = (bf16[1024,256]{1,0:T(8,128)(2,1)S(1)}, bf16[1024,256]{1,0:T(8,128)(2,1)S(1)}, u32[]{:S(2)}, u32[]{:S(2)}) collective-permute-start(bf16[1024,256]{1,0:T(8,128)(2,1)S(1)} %fusion.4), channel_id=1, source_target_pairs={{0,2},{1,3},{2,4},{3,5},{4,6},{5,7},{6,0},{7,1},{8,10},{9,11},{10,... | collective-permute-start | bytes 1572872 | tf_op jit(solution)/shard_map/ppermute | solution.py:101
  117.9 20.7 %collective-permute-start.10 = (bf16[1024,256]{1,0:T(8,128)(2,1)S(1)}, bf16[1024,256]{1,0:T(8,128)(2,1)S(1)}, u32[]{:S(2)}, u32[]{:S(2)}) collective-permute-start(bf16[1024,256]{1,0:T(8,128)(2,1)S(1)} %fusion.7), channel_id=1, source_target_pairs={{0,6},{1,7},{2,0},{3,1},{4,2},{5,3},{6,4},{7,5},{8,14},{9,15},{10,... | collective-permute-start | bytes 1572872 | tf_op jit(solution)/shard_map/ppermute | solution.py:101
  128.9 48.1 %collective-permute-start.20 = (bf16[1792,256]{1,0:T(8,128)(2,1)S(1)}, bf16[1792,256]{1,0:T(8,128)(2,1)S(1)}, u32[]{:S(2)}, u32[]{:S(2)}) collective-permute-start(bf16[1792,256]{1,0:T(8,128)(2,1)S(1)} %convolution_convert_fusion.1), channel_id=1, source_target_pairs={{0,32},{1,9},{2,34},{3,11},{4,36},{5,13},{6,38},{7,15},{8,40},{9,1... | collective-permute-start | bytes 2752520 | tf_op jit(solution)/shard_map/ppermute | solution.py:101
  132.1 44.9 %collective-permute-start.21 = (bf16[1792,256]{1,0:T(8,128)(2,1)S(1)}, bf16[1792,256]{1,0:T(8,128)(2,1)S(1)}, u32[]{:S(2)}, u32[]{:S(2)}) collective-permute-start(bf16[1792,256]{1,0:T(8,128)(2,1)S(1)} %convolution_convert_fusion.4.refs_4_), channel_id=1, source_target_pairs={{0,64},{1,17},{2,66},{3,19},{4,68},{5,21},{6,70},{7,23},{8,72},{9,... | collective-permute-start | bytes 2752520 | tf_op jit(solution)/shard_map/ppermute | solution.py:101
  137.6 39.4 %collective-permute-start.22 = (bf16[1792,256]{1,0:T(8,128)(2,1)S(1)}, bf16[1792,256]{1,0:T(8,128)(2,1)S(1)}, u32[]{:S(2)}, u32[]{:S(2)}) collective-permute-start(bf16[1792,256]{1,0:T(8,128)(2,1)S(1)} %convolution_convert_fusion.3.refs_5_), channel_id=1, source_target_pairs={{0,96},{1,25},{2,98},{3,27},{4,100},{5,29},{6,102},{7,31},{8,104},... | collective-permute-start | bytes 2752520 | tf_op jit(solution)/shard_map/ppermute | solution.py:101
  138.8 25.8 %collective-permute-start.15 = (bf16[2048,256]{1,0:T(8,128)(2,1)S(1)}, bf16[2048,256]{1,0:T(8,128)(2,1)S(1)}, u32[]{:S(2)}, u32[]{:S(2)}) collective-permute-start(bf16[2048,256]{1,0:T(8,128)(2,1)S(1)} %get-tuple-element.52), channel_id=1, source_target_pairs={{0,2},{1,3},{2,4},{3,5},{4,6},{5,7},{6,0},{7,1},{8,10},{9,11},{10,... | collective-permute-start | bytes 3145736 | tf_op jit(solution)/shard_map/ppermute | solution.py:101
  138.9 25.8 %collective-permute-start.16 = (bf16[2048,256]{1,0:T(8,128)(2,1)S(1)}, bf16[2048,256]{1,0:T(8,128)(2,1)S(1)}, u32[]{:S(2)}, u32[]{:S(2)}) collective-permute-start(bf16[2048,256]{1,0:T(8,128)(2,1)S(1)} %get-tuple-element.53), channel_id=1, source_target_pairs={{0,6},{1,7},{2,0},{3,1},{4,2},{5,3},{6,4},{7,5},{8,14},{9,15},{10,... | collective-permute-start | bytes 3145736 | tf_op jit(solution)/shard_map/ppermute | solution.py:101
  166.5 21.6 %collective-permute-start.18 = (bf16[528,256]{1,0:T(8,128)(2,1)}, bf16[528,256]{1,0:T(8,128)(2,1)S(1)}, u32[]{:S(2)}, u32[]{:S(2)}) collective-permute-start(bf16[528,256]{1,0:T(8,128)(2,1)} %get-tuple-element.55.refs_4_), channel_id=1, source_target_pairs={{8,0},{24,1},{10,2},{26,3},{12,4},{28,5},{14,6},{30,7},{11,8},{15,... | collective-permute-start | bytes 811016 | tf_op jit(solution)/shard_map/ppermute | solution.py:101
  170.4 17.7 %collective-permute-start.19 = (bf16[528,256]{1,0:T(8,128)(2,1)}, bf16[528,256]{1,0:T(8,128)(2,1)S(1)}, u32[]{:S(2)}, u32[]{:S(2)}) collective-permute-start(bf16[528,256]{1,0:T(8,128)(2,1)} %get-tuple-element.56), channel_id=1, source_target_pairs={{3,0},{7,1},{35,2},{39,3},{67,4},{71,5},{99,6},{103,7},{9,8},{13,9... | collective-permute-start | bytes 811016 | tf_op jit(solution)/shard_map/ppermute | solution.py:101
  180.7 13.7 %collective-permute-start.24 = (bf16[528,256]{1,0:T(8,128)(2,1)S(1)}, bf16[528,256]{1,0:T(8,128)(2,1)S(1)}, u32[]{:S(2)}, u32[]{:S(2)}) collective-permute-start(bf16[528,256]{1,0:T(8,128)(2,1)S(1)} %get-tuple-element.61), channel_id=1, source_target_pairs={{1,0},{5,1},{33,2},{37,3},{65,4},{69,5},{97,6},{101,7},{0,8},{16,9... | collective-permute-start | bytes 811016 | tf_op jit(solution)/shard_map/ppermute | solution.py:101
  (28 other events, 185.6 us)
Sparse Core Ops, SparseCore 0:
  53.1 51.9 all-gather.1
  109.5 57.5 reduce-scatter.1

commit v7 on v6

--- a/solution.py
+++ b/solution.py
@@ -487,7 +487,7 @@
         out[tokens:, :] = note
 
 
-def return_blocks(parts, peaks):
+def return_blocks(parts, peaks, after):
     rows, features = parts[0].shape
     return call(
         return_kernel,
@@ -495,6 +495,7 @@
         (0, 0),
         [SCALARS] + [IN_VMEM] * 4,
         (jnp.asarray(TABLE), *parts, peaks),
+        after,
         out_specs=[IN_VMEM] * 4,
     )
 
@@ -646,15 +647,16 @@
     ]
     after, before = add_halves(*mixed, top, bottom, weight_grad[2:])
     mixed = (own, send(after, hidden_ring(1)), send(before, hidden_ring(-1)))
-    blocks = list(return_blocks(mixed, peaks))
-    weight_grad, added = add(ring_exchange(weight_grad, feature_ring), blocks[:1])
+    blocks = list(return_blocks(mixed, peaks, weight_grad[:1]))
+    parts = ring_exchange(weight_grad, feature_ring)
+    blocks[2:] = gate(blocks[2:], (*parts[1:], blocks[0]))
     grad_gate, grad_up, finished = finish(slope, silu, grad_act)
-    blocks[2:] = gate(blocks[2:], (added,))
+    weight_grad, added = add(parts, blocks[2:])
     blocks = [
         send(block, [(edge[1], edge[0]) for edge in ROUNDS[number]])
         for number, block in enumerate(blocks)
     ]
-    blocks = gate(blocks, (finished,))
+    blocks = gate(blocks, (added, finished))
     mixed = merge(blocks, ())
     peaks = read_notes(blocks)
     new_weight, new_act = histories(

time: 204 us -> 203 us (level)
  transfers between devices with their start and end apart: 28 -> 28, of which waited for: 8 -> 8; matrix products, arithmetic and copies ran while one was open for 15% -> 16% of each run, Pallas kernels for 5% -> 5%
where the time goes in v7:
time: 203 us; the launch traced here: 202 us
  waiting for transfers between devices  66.7 us (33%)
  starting transfers between devices  54.1 us (27%)
  matrix products  31.3 us (15%)
  local copies, waits for them, and re-layouts  19.9 us (10%)
  Pallas kernels  15.5 us (8%)
  between operations  14.5 us (7%)
    ppermute x26, waiting for transfers between devices, send(): return lax.ppermute(value, AXES, pairs)  66.7 us
    ppermute x26, starting transfers between devices, send(): return lax.ppermute(value, AXES, pairs)  54 us
    dot_general x10, matrix products, dot(): lax.dot_general(left, right, (dims, ((), ())), preferred_element_type=F32)  31.3 us
    unnamed x48, local copies, waits for them, and re-layouts  19.8 us
    pallas_call x19, Pallas kernels, call(): pl.pallas_call(body, out_shape=out_shape, in_specs=list(in_specs) + [ANYW...  15.5 us
  transfers between devices with their start and end apart: 28, of which 8 were waited for; matrix products, arithmetic and copies ran while one was open for 16% of the time, Pallas kernels for 5%

profile of v7, /device:TPU:15, one launch (start us, length us, event | category | flops | bytes accessed | tf_op | source)
XLA Modules:
  0.0 202.1 jit_solution(17408035669253487980)
XLA Ops:
  18.3 4.1 %collective-permute-start.1 = (bf16[528,256]{1,0:T(8,128)(2,1)S(1)}, bf16[528,256]{1,0:T(8,128)(2,1)S(1)}, u32[]{:S(2)}, u32[]{:S(2)}) collective-permute-start(bf16[528,256]{1,0:T(8,128)(2,1)S(1)} %get-tuple-element.43), channel_id=1, source_target_pairs={{0,8},{1,24},{2,10},{3,26},{4,12},{5,28},{6,14},{7,30},{8,11},{9,1... | collective-permute-start | bytes 811016 | tf_op jit(solution)/shard_map/ppermute | solution.py:101
  24.4 7.0 %collective-permute-start.3 = (bf16[528,256]{1,0:T(8,128)(2,1)S(1)}, bf16[528,256]{1,0:T(8,128)(2,1)S(1)}, u32[]{:S(2)}, u32[]{:S(2)}) collective-permute-start(bf16[528,256]{1,0:T(8,128)(2,1)S(1)} %get-tuple-element.45), channel_id=1, source_target_pairs={{0,0},{1,16},{2,2},{3,18},{4,4},{5,20},{6,6},{7,22},{8,8},{9,24},{... | collective-permute-start | bytes 811016 | tf_op jit(solution)/shard_map/ppermute | solution.py:101
  31.4 2.8 %collective-permute-start.4 = (bf16[528,256]{1,0:T(8,128)(2,1)S(1)}, bf16[528,256]{1,0:T(8,128)(2,1)S(1)}, u32[]{:S(2)}, u32[]{:S(2)}) collective-permute-start(bf16[528,256]{1,0:T(8,128)(2,1)S(1)} %get-tuple-element.46), channel_id=1, source_target_pairs={{0,1},{1,5},{2,33},{3,37},{4,65},{5,69},{6,97},{7,101},{8,0},{9,16... | collective-permute-start | bytes 811016 | tf_op jit(solution)/shard_map/ppermute | solution.py:101
  34.2 16.7 %collective-permute-done.2.refs_2_ = bf16[528,256]{1,0:T(8,128)(2,1)S(1)} collective-permute-done((bf16[528,256]{1,0:T(8,128)(2,1)S(1)}, bf16[528,256]{1,0:T(8,128)(2,1)S(1)}, u32[]{:S(2)}, u32[]{:S(2)}) %collective-permute-start.2) | collective-permute-done | bytes 270368 | tf_op jit(solution)/shard_map/ppermute | solution.py:101
  53.1 2.7 %collective-permute-start.11 = (bf16[2048,256]{1,0:T(8,128)(2,1)S(1)}, bf16[2048,256]{1,0:T(8,128)(2,1)S(1)}, u32[]{:S(2)}, u32[]{:S(2)}) collective-permute-start(bf16[2048,256]{1,0:T(8,128)(2,1)S(1)} %get-tuple-element.47.refs_1_.refs_2_.refs_0_), channel_id=1, source_target_pairs={{0,6},{1,7},{2,0},{3,1},{4,2},{5,3},{6,4},{7,5},{8,14},{9,15},{10,... | collective-permute-start | bytes 3145736 | tf_op jit(solution)/shard_map/ppermute | solution.py:101
  57.1 4.7 %collective-permute-start.6 = (bf16[1808,256]{1,0:T(8,128)(2,1)S(1)}, bf16[1808,256]{1,0:T(8,128)(2,1)S(1)}, u32[]{:S(2)}, u32[]{:S(2)}) collective-permute-start(bf16[1808,256]{1,0:T(8,128)(2,1)S(1)} %shard_map.123.refs_0_.refs_5_), channel_id=1, source_target_pairs={{0,32},{1,9},{2,34},{3,11},{4,36},{5,13},{6,38},{7,15},{8,40},{9,1... | collective-permute-start | bytes 2777096 | tf_op jit(solution)/shard_map/ppermute | solution.py:101
  61.8 16.4 %collective-permute-done.12.refs_4_ = bf16[2048,256]{1,0:T(8,128)(2,1)S(1)} collective-permute-done((bf16[2048,256]{1,0:T(8,128)(2,1)S(1)}, bf16[2048,256]{1,0:T(8,128)(2,1)S(1)}, u32[]{:S(2)}, u32[]{:S(2)}) %collective-permute-start.12) | collective-permute-done | bytes 1048608 | tf_op jit(solution)/shard_map/ppermute | solution.py:101
  78.4 2.9 %collective-permute-start.14 = (bf16[1024,256]{1,0:T(8,128)(2,1)S(1)}, bf16[1024,256]{1,0:T(8,128)(2,1)S(1)}, u32[]{:S(2)}, u32[]{:S(2)}) collective-permute-start(bf16[1024,256]{1,0:T(8,128)(2,1)S(1)} %slice.29), channel_id=1, source_target_pairs={{0,6},{1,7},{2,0},{3,1},{4,2},{5,3},{6,4},{7,5},{8,14},{9,15},{10,... | collective-permute-start | bytes 1572872 | tf_op jit(solution)/shard_map/ppermute | solution.py:101
  87.1 8.8 %collective-permute-done.7.refs_2_ = bf16[896,256]{1,0:T(8,128)(2,1)S(1)} collective-permute-done((bf16[896,256]{1,0:T(8,128)(2,1)S(1)}, bf16[896,256]{1,0:T(8,128)(2,1)S(1)}, u32[]{:S(2)}, u32[]{:S(2)}) %collective-permute-start.7) | collective-permute-done | bytes 458784 | tf_op jit(solution)/shard_map/ppermute | solution.py:101
  99.6 9.7 %convolution_convert_fusion = bf16[2048,1792]{1,0:T(8,128)(2,1)} fusion(bf16[2048,1024]{1,0:T(8,128)(2,1)S(1)} %shard_map.127, bf16[1792,1024]{1,0:T(8,128)(2,1)S(1)} %get-tuple-element.50), kind=kOutput, calls=%fused_computation | convolution fusion | flops 7519862784 | bytes 15204352 | tf_op jit(solution)/shard_map/dot_general | solution.py:590
  111.0 3.5 %fusion.4 = bf16[1024,256]{1,0:T(8,128)(2,1)S(1)} fusion(bf16[2048,1792]{1,0:T(8,128)(2,1)} %all-gather.2.cloned.1.call-done.refs_0_, bf16[1792,1024]{1,0:T(8,128)(2,1)} %copy-done.22, s32[]{:T(128)S(6)} %select_n.69), kind=kOutput, calls=%fused_computation.12 | convolution fusion | flops 939786240 | bytes 5111812 | tf_op jit(solution)/shard_map/dot_general | solution.py:590
  115.4 2.4 %fusion.7 = bf16[1024,256]{1,0:T(8,128)(2,1)S(1)} fusion(bf16[2048,1792]{1,0:T(8,128)(2,1)S(1)} %copy-done.5, bf16[1792,1024]{1,0:T(8,128)(2,1)} %copy-done.22, s32[]{:T(128)S(6)} %select_n.69), kind=kOutput, calls=%fused_computation.13 | convolution fusion | flops 939786240 | bytes 5111812 | tf_op jit(solution)/shard_map/dot_general | solution.py:590
  124.3 2.3 %copy-done.7 = bf16[2048,1024]{1,0:T(8,128)(2,1)S(1)} copy-done((bf16[2048,1024]{1,0:T(8,128)(2,1)S(1)}, bf16[2048,1024]{1,0:T(8,128)(2,1)}, u32[]{:S(2)}) %copy-start.7) | copy-done | bytes 4194328
  126.6 2.3 %convolution_convert_fusion.1 = bf16[1792,256]{1,0:T(8,128)(2,1)S(1)} fusion(bf16[2048,1792]{1,0:T(8,128)(2,1)S(1)} %shard_map.125, bf16[2048,1024]{1,0:T(8,128)(2,1)S(1)} %copy-done.7, s32[]{:T(128)S(6)} %select_n.78), kind=kOutput, calls=%fused_computation.5 | convolution fusion | flops 1879506944 | bytes 9306116 | tf_op jit(solution)/shard_map/dot_general | solution.py:590
  129.8 2.2 %convolution_convert_fusion.4.refs_4_ = bf16[1792,256]{1,0:T(8,128)(2,1)S(1)} fusion(bf16[2048,1792]{1,0:T(8,128)(2,1)S(1)} %shard_map.125, bf16[2048,1024]{1,0:T(8,128)(2,1)S(1)} %copy-done.7, s32[]{:T(128)S(6)} %select_n.72), kind=kOutput, calls=%fused_computation.8 | convolution fusion | flops 1879506944 | bytes 9306116 | tf_op jit(solution)/shard_map/dot_general | solution.py:590
  132.1 3.2 %collective-permute-start.21 = (bf16[1792,256]{1,0:T(8,128)(2,1)S(1)}, bf16[1792,256]{1,0:T(8,128)(2,1)S(1)}, u32[]{:S(2)}, u32[]{:S(2)}) collective-permute-start(bf16[1792,256]{1,0:T(8,128)(2,1)S(1)} %convolution_convert_fusion.4.refs_4_), channel_id=1, source_target_pairs={{0,64},{1,17},{2,66},{3,19},{4,68},{5,21},{6,70},{7,23},{8,72},{9,... | collective-permute-start | bytes 2752520 | tf_op jit(solution)/shard_map/ppermute | solution.py:101
  138.9 2.7 %collective-permute-start.16 = (bf16[2048,256]{1,0:T(8,128)(2,1)S(1)}, bf16[2048,256]{1,0:T(8,128)(2,1)S(1)}, u32[]{:S(2)}, u32[]{:S(2)}) collective-permute-start(bf16[2048,256]{1,0:T(8,128)(2,1)S(1)} %get-tuple-element.53), channel_id=1, source_target_pairs={{0,6},{1,7},{2,0},{3,1},{4,2},{5,3},{6,4},{7,5},{8,14},{9,15},{10,... | collective-permute-start | bytes 3145736 | tf_op jit(solution)/shard_map/ppermute | solution.py:101
  143.8 2.3 %convolution_convert_fusion.2.refs_5_.refs_0_ = bf16[1792,256]{1,0:T(8,128)(2,1)S(1)} fusion(bf16[2048,1792]{1,0:T(8,128)(2,1)S(1)} %shard_map.125, bf16[2048,1024]{1,0:T(8,128)(2,1)S(1)} %copy-done.7, s32[]{:T(128)S(6)} %select_n.76), kind=kOutput, calls=%fused_computation.6 | convolution fusion | flops 1879506944 | bytes 9306116 | tf_op jit(solution)/shard_map/dot_general | solution.py:590
  146.0 18.6 %collective-permute-done.15.refs_2_ = bf16[2048,256]{1,0:T(8,128)(2,1)S(1)} collective-permute-done((bf16[2048,256]{1,0:T(8,128)(2,1)S(1)}, bf16[2048,256]{1,0:T(8,128)(2,1)S(1)}, u32[]{:S(2)}, u32[]{:S(2)}) %collective-permute-start.15) | collective-permute-done | bytes 1048608 | tf_op jit(solution)/shard_map/ppermute | solution.py:101
  166.5 4.0 %collective-permute-start.18 = (bf16[528,256]{1,0:T(8,128)(2,1)}, bf16[528,256]{1,0:T(8,128)(2,1)S(1)}, u32[]{:S(2)}, u32[]{:S(2)}) collective-permute-start(bf16[528,256]{1,0:T(8,128)(2,1)} %get-tuple-element.55.refs_5_), channel_id=1, source_target_pairs={{8,0},{24,1},{10,2},{26,3},{12,4},{28,5},{14,6},{30,7},{11,8},{15,... | collective-permute-start | bytes 811016 | tf_op jit(solution)/shard_map/ppermute | solution.py:101
  170.6 6.5 %collective-permute-start.19 = (bf16[528,256]{1,0:T(8,128)(2,1)}, bf16[528,256]{1,0:T(8,128)(2,1)S(1)}, u32[]{:S(2)}, u32[]{:S(2)}) collective-permute-start(bf16[528,256]{1,0:T(8,128)(2,1)} %get-tuple-element.56), channel_id=1, source_target_pairs={{3,0},{7,1},{35,2},{39,3},{67,4},{71,5},{99,6},{103,7},{9,8},{13,9... | collective-permute-start | bytes 811016 | tf_op jit(solution)/shard_map/ppermute | solution.py:101
  185.9 2.4 %shard_map.132 = (bf16[512,1792]{1,0:T(8,128)(2,1)}, bf16[512,1792]{1,0:T(8,128)(2,1)}, f32[8,128]{1,0:T(8,128)S(1)}) custom-call(bf16[512,1792]{1,0:T(8,128)(2,1)S(1)} %copy-done.9, bf16[512,1792]{1,0:T(8,128)(2,1)S(1)} %copy-done.11, bf16[512,1792]{1,0:T(8,128)(2,1)S(1)} %copy-done.12), custom_call_target="tpu_custom_call" | custom-call | tf_op jit(solution)/shard_map/pallas_call | solution.py:117
  188.3 2.3 %collective-permute-done.23.refs_2_ = bf16[528,256]{1,0:T(8,128)(2,1)S(1)} collective-permute-done((bf16[528,256]{1,0:T(8,128)(2,1)S(1)}, bf16[528,256]{1,0:T(8,128)(2,1)S(1)}, u32[]{:S(2)}, u32[]{:S(2)}) %collective-permute-start.23) | collective-permute-done | bytes 270368 | tf_op jit(solution)/shard_map/ppermute | solution.py:101
  190.5 2.2 %collective-permute-done.24.refs_3_ = bf16[528,256]{1,0:T(8,128)(2,1)S(1)} collective-permute-done((bf16[528,256]{1,0:T(8,128)(2,1)S(1)}, bf16[528,256]{1,0:T(8,128)(2,1)S(1)}, u32[]{:S(2)}, u32[]{:S(2)}) %collective-permute-start.24) | collective-permute-done | bytes 270368 | tf_op jit(solution)/shard_map/ppermute | solution.py:101
  (116 shorter events, 54.8 us)
Async XLA Ops:
  7.2 103.8 %all-gather.2.cloned.1.call-start = ((), (), s32[]{:S(2)}) async-start(), calls=%async_computation.1 | async-start | bytes 9175040 | tf_op jit(solution)/shard_map/all_gather | solution.py:618
  18.3 15.9 %collective-permute-start.1 = (bf16[528,256]{1,0:T(8,128)(2,1)S(1)}, bf16[528,256]{1,0:T(8,128)(2,1)S(1)}, u32[]{:S(2)}, u32[]{:S(2)}) collective-permute-start(bf16[528,256]{1,0:T(8,128)(2,1)S(1)} %get-tuple-element.43), channel_id=1, source_target_pairs={{0,8},{1,24},{2,10},{3,26},{4,12},{5,28},{6,14},{7,30},{8,11},{9,1... | collective-permute-start | bytes 811016 | tf_op jit(solution)/shard_map/ppermute | solution.py:101
  22.4 28.5 %collective-permute-start.2 = (bf16[528,256]{1,0:T(8,128)(2,1)S(1)}, bf16[528,256]{1,0:T(8,128)(2,1)S(1)}, u32[]{:S(2)}, u32[]{:S(2)}) collective-permute-start(bf16[528,256]{1,0:T(8,128)(2,1)S(1)} %get-tuple-element.44), channel_id=1, source_target_pairs={{0,3},{1,7},{2,35},{3,39},{4,67},{5,71},{6,99},{7,103},{8,9},{9,13... | collective-permute-start | bytes 811016 | tf_op jit(solution)/shard_map/ppermute | solution.py:101
  24.4 26.6 %collective-permute-start.3 = (bf16[528,256]{1,0:T(8,128)(2,1)S(1)}, bf16[528,256]{1,0:T(8,128)(2,1)S(1)}, u32[]{:S(2)}, u32[]{:S(2)}) collective-permute-start(bf16[528,256]{1,0:T(8,128)(2,1)S(1)} %get-tuple-element.45), channel_id=1, source_target_pairs={{0,0},{1,16},{2,2},{3,18},{4,4},{5,20},{6,6},{7,22},{8,8},{9,24},{... | collective-permute-start | bytes 811016 | tf_op jit(solution)/shard_map/ppermute | solution.py:101
  31.4 19.6 %collective-permute-start.4 = (bf16[528,256]{1,0:T(8,128)(2,1)S(1)}, bf16[528,256]{1,0:T(8,128)(2,1)S(1)}, u32[]{:S(2)}, u32[]{:S(2)}) collective-permute-start(bf16[528,256]{1,0:T(8,128)(2,1)S(1)} %get-tuple-element.46), channel_id=1, source_target_pairs={{0,1},{1,5},{2,33},{3,37},{4,65},{5,69},{6,97},{7,101},{8,0},{9,16... | collective-permute-start | bytes 811016 | tf_op jit(solution)/shard_map/ppermute | solution.py:101
  52.9 129.9 %reduce-scatter.2.cloned.1.call-start = ((), (), s32[]{:S(2)}) async-start(), calls=%async_computation.2 | async-start | bytes 9175040 | tf_op jit(solution)/shard_map/reduce_scatter | solution.py:636
  53.0 25.2 %collective-permute-start.12 = (bf16[2048,256]{1,0:T(8,128)(2,1)S(1)}, bf16[2048,256]{1,0:T(8,128)(2,1)S(1)}, u32[]{:S(2)}, u32[]{:S(2)}) collective-permute-start(bf16[2048,256]{1,0:T(8,128)(2,1)S(1)} %get-tuple-element.47.refs_1_.refs_2_.refs_0_), channel_id=1, source_target_pairs={{0,2},{1,3},{2,4},{3,5},{4,6},{5,7},{6,0},{7,1},{8,10},{9,11},{10,... | collective-permute-start | bytes 3145736 | tf_op jit(solution)/shard_map/ppermute | solution.py:101
  53.1 25.2 %collective-permute-start.11 = (bf16[2048,256]{1,0:T(8,128)(2,1)S(1)}, bf16[2048,256]{1,0:T(8,128)(2,1)S(1)}, u32[]{:S(2)}, u32[]{:S(2)}) collective-permute-start(bf16[2048,256]{1,0:T(8,128)(2,1)S(1)} %get-tuple-element.47.refs_1_.refs_2_.refs_0_), channel_id=1, source_target_pairs={{0,6},{1,7},{2,0},{3,1},{4,2},{5,3},{6,4},{7,5},{8,14},{9,15},{10,... | collective-permute-start | bytes 3145736 | tf_op jit(solution)/shard_map/ppermute | solution.py:101
  57.0 24.2 %collective-permute-start.5 = (bf16[1808,256]{1,0:T(8,128)(2,1)S(1)}, bf16[1808,256]{1,0:T(8,128)(2,1)S(1)}, u32[]{:S(2)}, u32[]{:S(2)}) collective-permute-start(bf16[1808,256]{1,0:T(8,128)(2,1)S(1)} %shard_map.123.refs_0_.refs_5_), channel_id=1, source_target_pairs={{0,96},{1,25},{2,98},{3,27},{4,100},{5,29},{6,102},{7,31},{8,104},... | collective-permute-start | bytes 2777096 | tf_op jit(solution)/shard_map/ppermute | solution.py:101
  57.1 24.3 %collective-permute-start.6 = (bf16[1808,256]{1,0:T(8,128)(2,1)S(1)}, bf16[1808,256]{1,0:T(8,128)(2,1)S(1)}, u32[]{:S(2)}, u32[]{:S(2)}) collective-permute-start(bf16[1808,256]{1,0:T(8,128)(2,1)S(1)} %shard_map.123.refs_0_.refs_5_), channel_id=1, source_target_pairs={{0,32},{1,9},{2,34},{3,11},{4,36},{5,13},{6,38},{7,15},{8,40},{9,1... | collective-permute-start | bytes 2777096 | tf_op jit(solution)/shard_map/ppermute | solution.py:101
  78.2 18.3 %collective-permute-start.13 = (bf16[1024,256]{1,0:T(8,128)(2,1)S(1)}, bf16[1024,256]{1,0:T(8,128)(2,1)S(1)}, u32[]{:S(2)}, u32[]{:S(2)}) collective-permute-start(bf16[1024,256]{1,0:T(8,128)(2,1)S(1)} %slice.28), channel_id=1, source_target_pairs={{0,2},{1,3},{2,4},{3,5},{4,6},{5,7},{6,0},{7,1},{8,10},{9,11},{10,... | collective-permute-start | bytes 1572872 | tf_op jit(solution)/shard_map/ppermute | solution.py:101
  78.4 18.2 %collective-permute-start.14 = (bf16[1024,256]{1,0:T(8,128)(2,1)S(1)}, bf16[1024,256]{1,0:T(8,128)(2,1)S(1)}, u32[]{:S(2)}, u32[]{:S(2)}) collective-permute-start(bf16[1024,256]{1,0:T(8,128)(2,1)S(1)} %slice.29), channel_id=1, source_target_pairs={{0,6},{1,7},{2,0},{3,1},{4,2},{5,3},{6,4},{7,5},{8,14},{9,15},{10,... | collective-permute-start | bytes 1572872 | tf_op jit(solution)/shard_map/ppermute | solution.py:101
  81.3 14.6 %collective-permute-start.8 = (bf16[912,256]{1,0:T(8,128)(2,1)S(1)}, bf16[912,256]{1,0:T(8,128)(2,1)S(1)}, u32[]{:S(2)}, u32[]{:S(2)}) collective-permute-start(bf16[912,256]{1,0:T(8,128)(2,1)S(1)} %slice.25), channel_id=1, source_target_pairs={{0,96},{1,25},{2,98},{3,27},{4,100},{5,29},{6,102},{7,31},{8,104},... | collective-permute-start | bytes 1400840 | tf_op jit(solution)/shard_map/ppermute | solution.py:101
  81.4 14.4 %collective-permute-start.7 = (bf16[896,256]{1,0:T(8,128)(2,1)S(1)}, bf16[896,256]{1,0:T(8,128)(2,1)S(1)}, u32[]{:S(2)}, u32[]{:S(2)}) collective-permute-start(bf16[896,256]{1,0:T(8,128)(2,1)S(1)} %slice.24), channel_id=1, source_target_pairs={{0,32},{1,9},{2,34},{3,11},{4,36},{5,13},{6,38},{7,15},{8,40},{9,1... | collective-permute-start | bytes 1376264 | tf_op jit(solution)/shard_map/ppermute | solution.py:101
  114.5 24.0 %collective-permute-start.9 = (bf16[1024,256]{1,0:T(8,128)(2,1)S(1)}, bf16[1024,256]{1,0:T(8,128)(2,1)S(1)}, u32[]{:S(2)}, u32[]{:S(2)}) collective-permute-start(bf16[1024,256]{1,0:T(8,128)(2,1)S(1)} %fusion.4), channel_id=1, source_target_pairs={{0,2},{1,3},{2,4},{3,5},{4,6},{5,7},{6,0},{7,1},{8,10},{9,11},{10,... | collective-permute-start | bytes 1572872 | tf_op jit(solution)/shard_map/ppermute | solution.py:101
  117.9 20.7 %collective-permute-start.10 = (bf16[1024,256]{1,0:T(8,128)(2,1)S(1)}, bf16[1024,256]{1,0:T(8,128)(2,1)S(1)}, u32[]{:S(2)}, u32[]{:S(2)}) collective-permute-start(bf16[1024,256]{1,0:T(8,128)(2,1)S(1)} %fusion.7), channel_id=1, source_target_pairs={{0,6},{1,7},{2,0},{3,1},{4,2},{5,3},{6,4},{7,5},{8,14},{9,15},{10,... | collective-permute-start | bytes 1572872 | tf_op jit(solution)/shard_map/ppermute | solution.py:101
  128.9 48.3 %collective-permute-start.20 = (bf16[1792,256]{1,0:T(8,128)(2,1)S(1)}, bf16[1792,256]{1,0:T(8,128)(2,1)S(1)}, u32[]{:S(2)}, u32[]{:S(2)}) collective-permute-start(bf16[1792,256]{1,0:T(8,128)(2,1)S(1)} %convolution_convert_fusion.1), channel_id=1, source_target_pairs={{0,32},{1,9},{2,34},{3,11},{4,36},{5,13},{6,38},{7,15},{8,40},{9,1... | collective-permute-start | bytes 2752520 | tf_op jit(solution)/shard_map/ppermute | solution.py:101
  132.1 45.1 %collective-permute-start.21 = (bf16[1792,256]{1,0:T(8,128)(2,1)S(1)}, bf16[1792,256]{1,0:T(8,128)(2,1)S(1)}, u32[]{:S(2)}, u32[]{:S(2)}) collective-permute-start(bf16[1792,256]{1,0:T(8,128)(2,1)S(1)} %convolution_convert_fusion.4.refs_4_), channel_id=1, source_target_pairs={{0,64},{1,17},{2,66},{3,19},{4,68},{5,21},{6,70},{7,23},{8,72},{9,... | collective-permute-start | bytes 2752520 | tf_op jit(solution)/shard_map/ppermute | solution.py:101
  137.6 39.6 %collective-permute-start.22 = (bf16[1792,256]{1,0:T(8,128)(2,1)S(1)}, bf16[1792,256]{1,0:T(8,128)(2,1)S(1)}, u32[]{:S(2)}, u32[]{:S(2)}) collective-permute-start(bf16[1792,256]{1,0:T(8,128)(2,1)S(1)} %convolution_convert_fusion.3.refs_5_), channel_id=1, source_target_pairs={{0,96},{1,25},{2,98},{3,27},{4,100},{5,29},{6,102},{7,31},{8,104},... | collective-permute-start | bytes 2752520 | tf_op jit(solution)/shard_map/ppermute | solution.py:101
  138.8 25.8 %collective-permute-start.15 = (bf16[2048,256]{1,0:T(8,128)(2,1)S(1)}, bf16[2048,256]{1,0:T(8,128)(2,1)S(1)}, u32[]{:S(2)}, u32[]{:S(2)}) collective-permute-start(bf16[2048,256]{1,0:T(8,128)(2,1)S(1)} %get-tuple-element.52), channel_id=1, source_target_pairs={{0,2},{1,3},{2,4},{3,5},{4,6},{5,7},{6,0},{7,1},{8,10},{9,11},{10,... | collective-permute-start | bytes 3145736 | tf_op jit(solution)/shard_map/ppermute | solution.py:101
  138.9 25.8 %collective-permute-start.16 = (bf16[2048,256]{1,0:T(8,128)(2,1)S(1)}, bf16[2048,256]{1,0:T(8,128)(2,1)S(1)}, u32[]{:S(2)}, u32[]{:S(2)}) collective-permute-start(bf16[2048,256]{1,0:T(8,128)(2,1)S(1)} %get-tuple-element.53), channel_id=1, source_target_pairs={{0,6},{1,7},{2,0},{3,1},{4,2},{5,3},{6,4},{7,5},{8,14},{9,15},{10,... | collective-permute-start | bytes 3145736 | tf_op jit(solution)/shard_map/ppermute | solution.py:101
  166.5 21.7 %collective-permute-start.18 = (bf16[528,256]{1,0:T(8,128)(2,1)}, bf16[528,256]{1,0:T(8,128)(2,1)S(1)}, u32[]{:S(2)}, u32[]{:S(2)}) collective-permute-start(bf16[528,256]{1,0:T(8,128)(2,1)} %get-tuple-element.55.refs_5_), channel_id=1, source_target_pairs={{8,0},{24,1},{10,2},{26,3},{12,4},{28,5},{14,6},{30,7},{11,8},{15,... | collective-permute-start | bytes 811016 | tf_op jit(solution)/shard_map/ppermute | solution.py:101
  170.6 17.7 %collective-permute-start.19 = (bf16[528,256]{1,0:T(8,128)(2,1)}, bf16[528,256]{1,0:T(8,128)(2,1)S(1)}, u32[]{:S(2)}, u32[]{:S(2)}) collective-permute-start(bf16[528,256]{1,0:T(8,128)(2,1)} %get-tuple-element.56), channel_id=1, source_target_pairs={{3,0},{7,1},{35,2},{39,3},{67,4},{71,5},{99,6},{103,7},{9,8},{13,9... | collective-permute-start | bytes 811016 | tf_op jit(solution)/shard_map/ppermute | solution.py:101
  179.1 13.7 %collective-permute-start.24 = (bf16[528,256]{1,0:T(8,128)(2,1)S(1)}, bf16[528,256]{1,0:T(8,128)(2,1)S(1)}, u32[]{:S(2)}, u32[]{:S(2)}) collective-permute-start(bf16[528,256]{1,0:T(8,128)(2,1)S(1)} %get-tuple-element.60.refs_5_), channel_id=1, source_target_pairs={{1,0},{5,1},{33,2},{37,3},{65,4},{69,5},{97,6},{101,7},{0,8},{16,9... | collective-permute-start | bytes 811016 | tf_op jit(solution)/shard_map/ppermute | solution.py:101
  (28 other events, 161.8 us)
Sparse Core Ops, SparseCore 0:
  53.1 51.9 all-gather.1
  109.5 57.5 reduce-scatter.1
